TPU v7x, 32 devices: a whole 2x2x4 slice. The times are simulated.
32 devices in a mesh: ctx: 8 (over z, y), hg: 4 (over x, core).
Axes of the slice: x: 2, y: 2, z: 4, core: 2. Of those that a mesh axis runs over, the one named last changes fastest.
Arguments:
- doc_ids: int32 [4096], P('ctx'), may hold values from 0 to 7, never falling along the last dimension, each value on 1 to 1024 neighbouring positions
- rotated_queries: bfloat16 [4096, 2048], P('ctx', 'hg'), may hold values from -6 to 6
- rotated_keys: bfloat16 [4096, 512], P('ctx', 'hg'), may hold values from -6 to 6
- value_matrix: bfloat16 [4096, 512], P('ctx', 'hg'), may hold values from -6 to 6
- out_proj: bfloat16 [4096, 2048], P('ctx', 'hg'), may hold values from -0.125 to 0.125
- cotangent: bfloat16 [4096, 4096], P('ctx'), may hold values from -6 to 6
Outputs:
- layer_output: bfloat16 [4096, 4096], P('ctx', 'hg')
- query_grad: bfloat16 [4096, 2048], P('ctx', 'hg')
- key_gradient: bfloat16 [4096, 512], P('ctx', 'hg')
- value_gradient: bfloat16 [4096, 512], P('ctx', 'hg')
- proj_grad: bfloat16 [4096, 2048], P('ctx', 'hg')
Inputs may be any that keep to these rules, and one draw needn't show every extreme that they name: `doc_ids`: document ids in token order, never falling; every document has 1 to 1024 tokens and one has exactly 1024.
All inputs are finite; a program needn't handle non-finite values.
Results may differ from a plain program's by a relative error of at most 0.013.
Values may be sent and summed in bfloat16 or wider, within the bound.
No kernel may reach another device: no remote copies, remote signals or barrier semaphores. Data moves between devices by JAX's collectives and lax.ppermute only.
A program may use at most 128 MiB of HBM per device.

v0:
```python
import jax
import jax.numpy as jnp
from jax import lax
from jax.sharding import PartitionSpec as P

HEAD_SIZE = 128
TOK_DEV = 512
DOC_MOST = 1024


def from_behind(value, axis, by):
    devices = lax.axis_size(axis)
    pairs = [(i, i + by) for i in range(devices) if 0 <= i + by < devices]
    return lax.ppermute(value, axis, pairs)


def contract_last(left_side, right_side):
    return lax.dot_general(
        left_side, right_side, (((1,), (1,)), ((), ())), preferred_element_type=jnp.float32
    )


def contract_first(left_side, right_side):
    return lax.dot_general(
        left_side, right_side, (((0,), (0,)), ((), ())), preferred_element_type=jnp.float32
    )


def body(doc_ids, rotated_queries, rotated_keys, value_matrix, out_proj, cotangent):
    row_count = rotated_queries.shape[0]
    head_count = rotated_queries.shape[1] // HEAD_SIZE
    kv_count = rotated_keys.shape[1] // HEAD_SIZE
    group_length = head_count // kv_count
    steps_back = DOC_MOST // TOK_DEV
    score_scale = HEAD_SIZE ** (-0.5)
    device_index = lax.axis_index("ctx")
    earlier = [(rotated_keys, value_matrix, doc_ids)]
    for offset in range(1, steps_back + 1):
        earlier.append(from_behind((rotated_keys, value_matrix, doc_ids), "ctx", offset))
    ordered = earlier[::-1]
    key_cat = jnp.concatenate([member[0] for member in ordered], 0)
    value_cat = jnp.concatenate([member[1] for member in ordered], 0)
    doc_cat = jnp.concatenate([member[2] for member in ordered], 0)
    key_width = key_cat.shape[0]
    query_pos = jnp.arange(row_count, dtype=jnp.int32)
    column_pos = jnp.arange(key_width, dtype=jnp.int32)
    key_pos = column_pos - steps_back * row_count
    first_valid = (steps_back - device_index) * row_count
    allowed = (
        (doc_ids[:, None] == doc_cat[None, :])
        & (key_pos[None, :] <= query_pos[:, None])
        & (column_pos[None, :] >= first_valid)
    )
    outputs = []
    probs_list = []
    for head_index in range(head_count):
        kv_index = head_index // group_length
        query_head = rotated_queries[:, head_index * HEAD_SIZE : (head_index + 1) * HEAD_SIZE]
        key_head = key_cat
        value_head = value_cat
        scores = contract_last(query_head, key_head) * score_scale
        masked = jnp.where(allowed, scores, -jnp.inf)
        row_max = jnp.max(masked, axis=1, keepdims=True)
        row_sum = jnp.sum(jnp.where(allowed, jnp.exp(masked - row_max), 0.0), axis=1, keepdims=True)
        log_total = row_max + jnp.log(row_sum)
        weights = jnp.where(allowed, jnp.exp(masked - log_total), 0.0).astype(jnp.bfloat16)
        probs_list.append(weights)
        outputs.append(
            jnp.dot(weights, value_head, preferred_element_type=jnp.float32).astype(jnp.bfloat16)
        )
    attended = jnp.concatenate(outputs, 1)
    all_rows = lax.all_gather(out_proj, "ctx", axis=0, tiled=True)
    wide_rows = lax.all_to_all(all_rows, "hg", split_axis=0, concat_axis=1, tiled=True)
    all_heads = lax.all_gather(attended, "hg", axis=1, tiled=True)
    layer_output = contract_last(all_heads, wide_rows).astype(jnp.bfloat16)
    columns = cotangent
    attention_gradient = jnp.dot(
        columns,
        lax.all_gather(out_proj, "ctx", axis=0, tiled=True),
        preferred_element_type=jnp.float32,
    ).astype(jnp.bfloat16)
    columns = cotangent
    proj_grad = lax.psum_scatter(
        contract_first(columns, attended), "ctx", scatter_dimension=0, tiled=True
    ).astype(jnp.bfloat16)
    key_parts = [jnp.zeros((key_width, HEAD_SIZE), jnp.float32)]
    value_parts = [jnp.zeros((key_width, HEAD_SIZE), jnp.float32)]
    query_grads = []
    for head_index in range(head_count):
        kv_index = head_index // group_length
        query_head = rotated_queries[:, head_index * HEAD_SIZE : (head_index + 1) * HEAD_SIZE]
        key_head = key_cat
        value_head = value_cat
        grad_head = attention_gradient[:, head_index * HEAD_SIZE : (head_index + 1) * HEAD_SIZE]
        weights = probs_list[head_index]
        row_delta = jnp.sum(
            grad_head.astype(jnp.float32) * outputs[head_index].astype(jnp.float32),
            axis=1,
            keepdims=True,
        )
        grad_dots = contract_last(grad_head, value_head)
        shifted = (weights.astype(jnp.float32) * (grad_dots - row_delta) * score_scale).astype(
            jnp.bfloat16
        )
        query_grads.append(
            jnp.dot(shifted, key_head, preferred_element_type=jnp.float32).astype(jnp.bfloat16)
        )
        key_parts[kv_index] = key_parts[kv_index] + contract_first(shifted, query_head)
        value_parts[kv_index] = value_parts[kv_index] + contract_first(weights, grad_head)
    query_grad = jnp.concatenate(query_grads, 1)
    key_all = key_parts[0]
    value_all = value_parts[0]
    pieces = []
    for offset in range(steps_back + 1):
        lower = (steps_back - offset) * row_count
        pieces.append((key_all[lower : lower + row_count], value_all[lower : lower + row_count]))
    key_sum, value_sum = pieces[0]
    for offset in range(1, steps_back + 1):
        arrived = (
            from_behind(pieces[offset][0].astype(jnp.bfloat16), "ctx", -offset).astype(jnp.float32),
            from_behind(pieces[offset][1].astype(jnp.bfloat16), "ctx", -offset).astype(jnp.float32),
        )
        key_sum = key_sum + arrived[0]
        value_sum = value_sum + arrived[1]
    key_gradient = key_sum.astype(jnp.bfloat16)
    value_gradient = value_sum.astype(jnp.bfloat16)
    return (layer_output, query_grad, key_gradient, value_gradient, proj_grad)


def solution(mesh):
    in_specs = (
        P("ctx"),
        P("ctx", "hg"),
        P("ctx", "hg"),
        P("ctx", "hg"),
        P("ctx", "hg"),
        P("ctx", None),
    )
    out_specs = (P("ctx", "hg"), P("ctx", "hg"), P("ctx", "hg"), P("ctx", "hg"), P("ctx", "hg"))
    return jax.shard_map(body, mesh=mesh, in_specs=in_specs, out_specs=out_specs, check_vma=False)
```

profile of v0, /device:TPU:0, one launch (start us, length us, event | category | flops | bytes accessed | tf_op | source)
XLA Modules:
  0.0 295.2 jit_solution(16118047019012819852)
XLA Ops:
  7.2 0.7 all-gather.5.cloned.1.call-update
  7.9 4.9 %collective-permute-start.2 = (bf16[512,128]{1,0:T(8,128)(2,1)}, bf16[512,128]{1,0:T(8,128)(2,1)S(1)}, u32[]{:S(2)}, u32[]{:S(2)}) collective-permute-start(bf16[512,128]{1,0:T(8,128)(2,1)} %param.8), channel_id=1, source_target_pairs={{0,8},{4,12},{8,16},{12,20},{16,24},{20,28},{1,9},{5,13},{9,17},{1... | collective-permute-start | bytes 393224 | tf_op jit(solution)/shard_map/ppermute | solution.py:14
  12.9 3.4 %collective-permute-start.3 = (bf16[512,128]{1,0:T(8,128)(2,1)}, bf16[512,128]{1,0:T(8,128)(2,1)S(1)}, u32[]{:S(2)}, u32[]{:S(2)}) collective-permute-start(bf16[512,128]{1,0:T(8,128)(2,1)} %param.8), channel_id=1, source_target_pairs={{0,4},{4,8},{8,12},{12,16},{16,20},{20,24},{24,28},{1,5},{5,9},{9,... | collective-permute-start | bytes 393224 | tf_op jit(solution)/shard_map/ppermute | solution.py:14
  16.3 3.4 %collective-permute-start.1 = (s32[512]{0:T(512)}, s32[512]{0:T(512)S(1)}, u32[]{:S(2)}, u32[]{:S(2)}) collective-permute-start(s32[512]{0:T(512)} %param.6), channel_id=1, source_target_pairs={{0,4},{4,8},{8,12},{12,16},{16,20},{20,24},{24,28},{1,5},{5,9},{9,... | collective-permute-start | bytes 6152 | tf_op jit(solution)/shard_map/ppermute | solution.py:14
  19.8 3.5 %collective-permute-start = (s32[512]{0:T(512)}, s32[512]{0:T(512)S(1)}, u32[]{:S(2)}, u32[]{:S(2)}) collective-permute-start(s32[512]{0:T(512)} %param.6), channel_id=1, source_target_pairs={{0,8},{4,12},{8,16},{12,20},{16,24},{20,28},{1,9},{5,13},{9,17},{1... | collective-permute-start | bytes 6152 | tf_op jit(solution)/shard_map/ppermute | solution.py:14
  23.3 2.0 collective-permute-start.4
  25.3 3.4 %collective-permute-start.5 = (bf16[512,128]{1,0:T(8,128)(2,1)}, bf16[512,128]{1,0:T(8,128)(2,1)S(1)}, u32[]{:S(2)}, u32[]{:S(2)}) collective-permute-start(bf16[512,128]{1,0:T(8,128)(2,1)} %param.9), channel_id=1, source_target_pairs={{0,4},{4,8},{8,12},{12,16},{16,20},{20,24},{24,28},{1,5},{5,9},{9,... | collective-permute-start | bytes 393224 | tf_op jit(solution)/shard_map/ppermute | solution.py:14
  28.7 0.7 pad_add_fusion
  29.4 0.9 constant_dynamic-update-slice_fusion
  30.4 1.2 collective-permute-done.4
  31.6 0.9 constant_dynamic-update-slice_fusion.3
  32.6 2.2 fusion.46
  34.8 1.2 fusion.47
  36.0 1.2 fusion.48
  37.2 1.2 fusion.49
  38.4 3.4 %select_reduce_fusion.3 = (f32[512]{0:T(512)S(1)}, f32[512]{0:T(512)S(1)}, f32[512]{0:T(512)S(1)}, f32[512]{0:T(512)S(1)}) fusion(f32[512,1536]{0,1:T(8,128)S(1)} %get-tuple-element.37, f32[512]{0:T(512)S(1)} %get-tuple-element.36, pred[1536]{0:T(1024)(128)(4,1)S(1)} %iota_compare_fusion.1, s32[1536]{0:T(1024)S(1)} %iota_add_fusion, ...), kind=kLoop, calls=%fused_computation.32 | loop fusion | flops 12580864 | bytes 12615168 | tf_op jit(solution)/shard_map/reduce_sum | solution.py:64
  41.8 4.0 %select_convert_fusion.3 = (bf16[512,1536]{0,1:T(8,128)(2,1)}, bf16[512,1536]{0,1:T(8,128)(2,1)S(1)}, bf16[512,1536]{0,1:T(8,128)(2,1)S(1)}, bf16[512,1536]{0,1:T(8,128)(2,1)S(1)}) fusion(f32[512,1536]{0,1:T(8,128)S(1)} %get-tuple-element.37, f32[512]{0:T(512)S(1)} %get-tuple-element.52, pred[1536]{0:T(1024)(128)(4,1)S(1)} %iota_compare_fusion.1, ...), kind=kLoop, calls=%fused_computation.31 | loop fusion | flops 12582912 | bytes 18898432 | tf_op jit(solution)/shard_map/convert_element_type | solution.py:66
  45.8 0.4 convolution_convert_fusion.6
  46.2 0.4 convolution_convert_fusion.7
  46.6 0.3 copy-done
  46.9 0.4 convolution_convert_fusion.8
  47.3 44.6 %all-gather.5.cloned.1.call-done = bf16[4096,512]{1,0:T(8,128)(2,1)} async-done(((bf16[512,512]{1,0:T(8,128)(2,1)}), bf16[4096,512]{1,0:T(8,128)(2,1)}) %all-gather.5.cloned.1.call-update) | async-done | bytes 4194320 | tf_op jit(solution)/shard_map/all_gather | solution.py:72
  92.0 6.0 %convolution_convert_fusion.1 = bf16[512,512]{0,1:T(8,128)(2,1)S(1)} fusion(bf16[512,4096]{1,0:T(8,128)(2,1)} %param.11, bf16[4096,512]{1,0:T(8,128)(2,1)} %all-gather.5.cloned.1.call-done), kind=kOutput, calls=%fused_computation.47 | convolution fusion | flops 2147745792 | bytes 8912896 | tf_op jit(solution)/shard_map/dot_general | solution.py:77
  98.0 0.5 multiply_reduce_fusion.3
  98.7 0.7 copy-done.11
  99.4 0.8 pad_maximum_fusion
  100.5 7.8 %convolution_bitcast_fusion = f32[4096,512]{0,1:T(8,128)} fusion(bf16[512,4096]{1,0:T(8,128)(2,1)} %param.11, bf16[512,128]{0,1:T(8,128)(2,1)S(1)} %convolution_convert_fusion.6, bf16[512,128]{0,1:T(8,128)(2,1)S(1)} %convolution_convert_fusion.7, bf16[512,128]{0,1:T(8,128)(2,1)S(1)} %convolution_convert_fusion.8, bf16[512,128]{0,1:T(8,128)(2,1)} %copy-done.11), kind=kOutput, calls=%fused_computation | convolution fusion | flops 2149580800 | bytes 13107200 | tf_op jit(solution)/shard_map/dot_general | solution.py:24
  108.4 5.1 %all-to-all-start = ((bf16[4,1024,512]{2,1,0:T(8,128)(2,1)}), bf16[4,1024,512]{2,1,0:T(8,128)(2,1)}, u32[]{:S(2)}, u32[]{:S(2)}) async-start(bf16[4,1024,512]{2,1,0:T(8,128)(2,1)} %bitcast.58), calls=%async_computation | async-start | bytes 8388608 | tf_op jit(solution)/shard_map/all_to_all | solution.py:73
  113.5 1.6 fusion.18
  115.1 1.2 copy-done.6
  116.2 0.4 convolution_convert_fusion.2
  116.7 0.6 fusion.19
  117.3 1.2 copy-done.8
  118.5 0.4 convolution_convert_fusion.3
  118.9 0.6 fusion.20
  119.5 0.4 convolution_convert_fusion.4
  120.0 0.3 copy-done.4
  120.3 0.6 fusion.21
  120.9 0.4 convolution_convert_fusion.5
  121.4 2.4 fusion.32
  123.7 0.8 pad_maximum_fusion.1
  124.6 2.0 copy.28
  126.6 2.4 convolution_add_fusion.5
  129.0 1.6 convolution_add_fusion.4
  130.7 1.6 fusion.50
  132.3 1.3 collective-permute-start.7
  133.6 1.3 collective-permute-start.6
  134.9 0.6 fusion.41
  135.5 0.6 convolution_add_fusion.2
  136.1 0.6 convolution_add_fusion.1
  136.7 0.6 fusion.51
  137.3 1.3 collective-permute-start.9
  138.6 1.5 collective-permute-start.8
  140.1 0.7 collective-permute-done.7
  140.8 2.3 collective-permute-done.6
  143.1 0.7 fusion.25
  143.8 14.6 %collective-permute-done.9 = bf16[512,128]{1,0:T(8,128)(2,1)S(1)} collective-permute-done((bf16[512,128]{1,0:T(8,128)(2,1)S(1)}, bf16[512,128]{1,0:T(8,128)(2,1)S(1)}, u32[]{:S(2)}, u32[]{:S(2)}) %collective-permute-start.9) | collective-permute-done | bytes 131104 | tf_op jit(solution)/shard_map/ppermute | solution.py:14
  158.4 0.7 fusion.23
  159.1 5.5 %all-to-all-done = bf16[4,1024,512]{2,1,0:T(8,128)(2,1)} async-done(((bf16[4,1024,512]{2,1,0:T(8,128)(2,1)}), bf16[4,1024,512]{2,1,0:T(8,128)(2,1)}, u32[]{:S(2)}, u32[]{:S(2)}) %all-to-all-start) | async-done | bytes 4194336 | tf_op jit(solution)/shard_map/all_to_all | solution.py:73
  164.6 6.3 %copy.23 = bf16[1024,4,512]{0,2,1:T(8,128)(2,1)} copy(bf16[1024,4,512]{2,0,1:T(8,128)(2,1)} %bitcast.5) | data formatting | bytes 8388608 | tf_op jit(solution)/shard_map/all_to_all | solution.py:73
  170.9 6.2 %convolution_convert_fusion = bf16[512,1024]{1,0:T(8,128)(2,1)} fusion(bf16[512,2048]{0,1:T(8,128)(2,1)} %all-gather.3.cloned.1.call-done, bf16[1024,2048]{0,1:T(8,128)(2,1)} %bitcast.59), kind=kOutput, calls=%fused_computation.46 | convolution fusion | flops 2148007936 | bytes 7340032 | tf_op jit(solution)/shard_map/dot_general | solution.py:18
  177.1 109.2 %reduce-scatter.2.cloned.1.call-done = f32[512,512]{0,1:T(8,128)} async-done(((f32[4096,512]{0,1:T(8,128)}), f32[512,512]{0,1:T(8,128)}) %reduce-scatter.2.cloned.1.call-update) | async-done | bytes 1048592 | tf_op jit(solution)/shard_map/reduce_scatter | solution.py:83
  286.3 1.3 convert_element_type.151
  287.6 1.0 copy.29
  (61 shorter events, 0.8 us)
Async XLA Ops:
  7.2 84.8 %all-gather.5.cloned.1.call-start = ((), (), s32[]{:S(2)}) async-start(), calls=%async_computation.3 | async-start | bytes 4718592 | tf_op jit(solution)/shard_map/all_gather | solution.py:72
  7.9 163.0 %all-gather.3.cloned.1.call-start = ((), (), s32[]{:S(2)}) async-start(), calls=%async_computation.2 | async-start | bytes 2621440 | tf_op jit(solution)/shard_map/all_gather | solution.py:74
  7.9 21.4 %collective-permute-start.2 = (bf16[512,128]{1,0:T(8,128)(2,1)}, bf16[512,128]{1,0:T(8,128)(2,1)S(1)}, u32[]{:S(2)}, u32[]{:S(2)}) collective-permute-start(bf16[512,128]{1,0:T(8,128)(2,1)} %param.8), channel_id=1, source_target_pairs={{0,8},{4,12},{8,16},{12,20},{16,24},{20,28},{1,9},{5,13},{9,17},{1... | collective-permute-start | bytes 393224 | tf_op jit(solution)/shard_map/ppermute | solution.py:14
  12.9 16.5 %collective-permute-start.3 = (bf16[512,128]{1,0:T(8,128)(2,1)}, bf16[512,128]{1,0:T(8,128)(2,1)S(1)}, u32[]{:S(2)}, u32[]{:S(2)}) collective-permute-start(bf16[512,128]{1,0:T(8,128)(2,1)} %param.8), channel_id=1, source_target_pairs={{0,4},{4,8},{8,12},{12,16},{16,20},{20,24},{24,28},{1,5},{5,9},{9,... | collective-permute-start | bytes 393224 | tf_op jit(solution)/shard_map/ppermute | solution.py:14
  16.3 9.0 %collective-permute-start.1 = (s32[512]{0:T(512)}, s32[512]{0:T(512)S(1)}, u32[]{:S(2)}, u32[]{:S(2)}) collective-permute-start(s32[512]{0:T(512)} %param.6), channel_id=1, source_target_pairs={{0,4},{4,8},{8,12},{12,16},{16,20},{20,24},{24,28},{1,5},{5,9},{9,... | collective-permute-start | bytes 6152 | tf_op jit(solution)/shard_map/ppermute | solution.py:14
  19.8 8.9 %collective-permute-start = (s32[512]{0:T(512)}, s32[512]{0:T(512)S(1)}, u32[]{:S(2)}, u32[]{:S(2)}) collective-permute-start(s32[512]{0:T(512)} %param.6), channel_id=1, source_target_pairs={{0,8},{4,12},{8,16},{12,20},{16,24},{20,28},{1,9},{5,13},{9,17},{1... | collective-permute-start | bytes 6152 | tf_op jit(solution)/shard_map/ppermute | solution.py:14
  23.3 8.3 %collective-permute-start.4 = (bf16[512,128]{1,0:T(8,128)(2,1)}, bf16[512,128]{1,0:T(8,128)(2,1)S(1)}, u32[]{:S(2)}, u32[]{:S(2)}) collective-permute-start(bf16[512,128]{1,0:T(8,128)(2,1)} %param.9), channel_id=1, source_target_pairs={{0,8},{4,12},{8,16},{12,20},{16,24},{20,28},{1,9},{5,13},{9,17},{1... | collective-permute-start | bytes 393224 | tf_op jit(solution)/shard_map/ppermute | solution.py:14
  25.3 6.3 %collective-permute-start.5 = (bf16[512,128]{1,0:T(8,128)(2,1)}, bf16[512,128]{1,0:T(8,128)(2,1)S(1)}, u32[]{:S(2)}, u32[]{:S(2)}) collective-permute-start(bf16[512,128]{1,0:T(8,128)(2,1)} %param.9), channel_id=1, source_target_pairs={{0,4},{4,8},{8,12},{12,16},{16,20},{20,24},{24,28},{1,5},{5,9},{9,... | collective-permute-start | bytes 393224 | tf_op jit(solution)/shard_map/ppermute | solution.py:14
  30.4 6.8 %copy-start.16 = (bf16[1536,128]{1,0:T(8,128)(2,1)}, bf16[1536,128]{1,0:T(8,128)(2,1)S(1)}, u32[]{:S(2)}) copy-start(bf16[1536,128]{1,0:T(8,128)(2,1)S(1)} %constant_dynamic-update-slice_fusion) | copy-start | bytes 1179652
  32.5 14.1 %copy-start.18 = (bf16[1536,128]{1,0:T(8,128)(2,1)}, bf16[1536,128]{1,0:T(8,128)(2,1)S(1)}, u32[]{:S(2)}) copy-start(bf16[1536,128]{1,0:T(8,128)(2,1)S(1)} %constant_dynamic-update-slice_fusion.3) | copy-start | bytes 1179652
  32.5 2.3 copy-start.12
  32.5 2.3 copy-start.21
  45.7 1.2 copy-start
  92.0 6.0 %copy-start.3 = (bf16[512,1536]{0,1:T(8,128)(2,1)S(1)}, bf16[512,1536]{0,1:T(8,128)(2,1)}, u32[]{:S(2)}) copy-start(bf16[512,1536]{0,1:T(8,128)(2,1)} %get-tuple-element.32) | copy-start | bytes 4718596
  92.0 6.0 %copy-start.19 = (bf16[1536,128]{1,0:T(8,128)(2,1)S(1)}, bf16[1536,128]{1,0:T(8,128)(2,1)}, u32[]{:S(2)}) copy-start(bf16[1536,128]{1,0:T(8,128)(2,1)} %copy-done.18) | copy-start | bytes 1179652
  97.9 0.8 copy-start.13
  98.7 0.7 copy-start.11
  100.2 186.1 %reduce-scatter.2.cloned.1.call-start = ((), (), s32[]{:S(2)}) async-start(), calls=%async_computation.4 | async-start | bytes 9437184 | tf_op jit(solution)/shard_map/reduce_scatter | solution.py:83
  108.3 5.1 %copy-start.20 = (bf16[1536,128]{1,0:T(8,128)(2,1)S(1)}, bf16[1536,128]{1,0:T(8,128)(2,1)}, u32[]{:S(2)}) copy-start(bf16[1536,128]{1,0:T(8,128)(2,1)} %copy-done.18) | copy-start | bytes 1179652
  108.4 56.3 %all-to-all-start = ((bf16[4,1024,512]{2,1,0:T(8,128)(2,1)}), bf16[4,1024,512]{2,1,0:T(8,128)(2,1)}, u32[]{:S(2)}, u32[]{:S(2)}) async-start(bf16[4,1024,512]{2,1,0:T(8,128)(2,1)} %bitcast.58), calls=%async_computation | async-start | bytes 8388608 | tf_op jit(solution)/shard_map/all_to_all | solution.py:73
  113.4 2.8 copy-start.17
  113.4 3.2 %copy-start.14 = (bf16[512,512]{0,1:T(8,128)(2,1)S(1)}, bf16[512,512]{0,1:T(8,128)(2,1)}, u32[]{:S(2)}) copy-start(bf16[512,512]{0,1:T(8,128)(2,1)} %copy-done.13) | copy-start | bytes 1572868
  115.1 1.2 copy-start.6
  116.6 2.3 copy-start.1
  117.3 1.2 copy-start.8
  118.9 1.4 copy-start.4
  119.5 1.8 copy-start.10
  126.6 2.4 copy-start.9
  126.6 4.1 %copy-start.7 = (bf16[512,1536]{0,1:T(8,128)(2,1)S(1)}, bf16[512,1536]{0,1:T(8,128)(2,1)}, u32[]{:S(2)}) copy-start(bf16[512,1536]{0,1:T(8,128)(2,1)} %copy-done.6) | copy-start | bytes 4718596
  129.0 5.9 %copy-start.5 = (bf16[512,1536]{0,1:T(8,128)(2,1)S(1)}, bf16[512,1536]{0,1:T(8,128)(2,1)}, u32[]{:S(2)}) copy-start(bf16[512,1536]{0,1:T(8,128)(2,1)} %get-tuple-element.32) | copy-start | bytes 4718596
  129.0 5.9 %copy-start.15 = (bf16[512,512]{0,1:T(8,128)(2,1)S(1)}, bf16[512,512]{0,1:T(8,128)(2,1)}, u32[]{:S(2)}) copy-start(bf16[512,512]{0,1:T(8,128)(2,1)} %copy-done.13) | copy-start | bytes 1572868
  130.7 4.8 %copy-start.2 = (bf16[512,1536]{0,1:T(8,128)(2,1)S(1)}, bf16[512,1536]{0,1:T(8,128)(2,1)}, u32[]{:S(2)}) copy-start(bf16[512,1536]{0,1:T(8,128)(2,1)} %copy-done) | copy-start | bytes 4718596
  132.3 8.4 %collective-permute-start.7 = (bf16[512,128]{1,0:T(8,128)(2,1)S(1)}, bf16[512,128]{1,0:T(8,128)(2,1)S(1)}, u32[]{:S(2)}, u32[]{:S(2)}) collective-permute-start(bf16[512,128]{1,0:T(8,128)(2,1)S(1)} %get-tuple-element.31), channel_id=1, source_target_pairs={{8,0},{12,4},{16,8},{20,12},{24,16},{28,20},{9,1},{13,5},{17,9},{2... | collective-permute-start | bytes 393224 | tf_op jit(solution)/shard_map/ppermute | solution.py:14
  133.6 9.5 %collective-permute-start.6 = (bf16[512,128]{1,0:T(8,128)(2,1)S(1)}, bf16[512,128]{1,0:T(8,128)(2,1)S(1)}, u32[]{:S(2)}, u32[]{:S(2)}) collective-permute-start(bf16[512,128]{1,0:T(8,128)(2,1)S(1)} %get-tuple-element.30), channel_id=1, source_target_pairs={{4,0},{8,4},{12,8},{16,12},{20,16},{24,20},{28,24},{5,1},{9,5},{13... | collective-permute-start | bytes 393224 | tf_op jit(solution)/shard_map/ppermute | solution.py:14
  137.3 21.2 %collective-permute-start.9 = (bf16[512,128]{1,0:T(8,128)(2,1)S(1)}, bf16[512,128]{1,0:T(8,128)(2,1)S(1)}, u32[]{:S(2)}, u32[]{:S(2)}) collective-permute-start(bf16[512,128]{1,0:T(8,128)(2,1)S(1)} %get-tuple-element.29), channel_id=1, source_target_pairs={{8,0},{12,4},{16,8},{20,12},{24,16},{28,20},{9,1},{13,5},{17,9},{2... | collective-permute-start | bytes 393224 | tf_op jit(solution)/shard_map/ppermute | solution.py:14
  138.6 19.9 %collective-permute-start.8 = (bf16[512,128]{1,0:T(8,128)(2,1)S(1)}, bf16[512,128]{1,0:T(8,128)(2,1)S(1)}, u32[]{:S(2)}, u32[]{:S(2)}) collective-permute-start(bf16[512,128]{1,0:T(8,128)(2,1)S(1)} %get-tuple-element.28), channel_id=1, source_target_pairs={{4,0},{8,4},{12,8},{16,12},{20,16},{24,20},{28,24},{5,1},{9,5},{13... | collective-permute-start | bytes 393224 | tf_op jit(solution)/shard_map/ppermute | solution.py:14
Sparse Core Ops, SparseCore 0:
  10.1 81.7 all-gather.4
  100.4 23.7 all-gather.2
  127.8 158.4 reduce-scatter.1
where the time goes:
time: 296 us; the launch traced here: 295 us
  waiting for transfers between devices  179 us (60%)
  matrix products  42.9 us (14%)
  starting transfers between devices  31.4 us (11%)
  local copies, waits for them, and re-layouts  15.3 us (5%)
  between operations  14.3 us (5%)
  other arithmetic  12.4 us (4%)
    reduce_scatter x1, waiting for transfers between devices, body(): lax.psum_scatter(contract_first(columns, attended), 'ctx', scatter_dimens...  109 us
    all_gather x1, waiting for transfers between devices, body(): all_rows = lax.all_gather(out_proj, 'ctx', axis=0, tiled=True)  44.6 us
    ppermute x10, starting transfers between devices, from_behind(): return lax.ppermute(value, axis, pairs)  26 us
    ppermute x10, waiting for transfers between devices, from_behind(): return lax.ppermute(value, axis, pairs)  18.8 us
    dot_general x9, matrix products, contract_first(): lax.dot_general(left_side, right_side, (((0,), (0,)), ((), ())), preferre...  18.1 us
    dot_general x9, matrix products, contract_last(): lax.dot_general(left_side, right_side, (((1,), (1,)), ((), ())), preferre...  15.4 us
    unnamed x50, local copies, waits for them, and re-layouts  7.08 us
    all_to_all x1, local copies, waits for them, and re-layouts, body(): lax.all_to_all(all_rows, 'hg', split_axis=0, concat_axis=1, tiled=True)  6.3 us
  transfers between devices with their start and end apart: 14, of which 7 were waited for; matrix products, arithmetic and copies ran while one was open for 19% of the time, Pallas kernels for 0%

commit v1 on v0

v1 whole, which is shorter than its diff:
```python
import functools

import jax
import jax.numpy as jnp
from jax import lax
from jax.experimental import pallas as pl
from jax.experimental.pallas import tpu as pltpu
from jax.sharding import PartitionSpec as P

HEAD_SIZE = 128
DOC_MOST = 1024
QUERY_TILE = 256
SCALE = HEAD_SIZE**-0.5
LOG2E = 1.4426950408889634
DOC_ROWS = 16


def dot_nn(a, b):
    return lax.dot_general(a, b, (((1,), (0,)), ((), ())), preferred_element_type=jnp.float32)


def dot_nt(a, b):
    return lax.dot_general(a, b, (((1,), (1,)), ((), ())), preferred_element_type=jnp.float32)


def dot_tn(a, b):
    return lax.dot_general(a, b, (((0,), (0,)), ((), ())), preferred_element_type=jnp.float32)


def windows(rows, key_rows):
    tile = min(QUERY_TILE, rows)
    for first in range(0, rows, tile):
        yield first, tile, first, DOC_MOST + tile


def mask_of(start_row, first, tile, low, width):
    key_pos = lax.broadcasted_iota(jnp.int32, (width, tile), 0) + low
    query_pos = lax.broadcasted_iota(jnp.int32, (width, tile), 1) + (first + DOC_MOST)
    return (key_pos <= query_pos) & (key_pos >= start_row)


def fill_keys(kv2, kv1, key_ref, value_ref, keys, values, rows):
    keys[0:rows] = kv2[0:rows, 0:HEAD_SIZE]
    keys[rows : 2 * rows] = kv1[0:rows, 0:HEAD_SIZE]
    keys[2 * rows : 3 * rows] = key_ref[...]
    values[0:rows] = kv2[0:rows, HEAD_SIZE:]
    values[rows : 2 * rows] = kv1[0:rows, HEAD_SIZE:]
    values[2 * rows : 3 * rows] = value_ref[...]


def forward_kernel(start, query, kv2, kv1, key_ref, value_ref, attended, log_total, keys, values):
    rows = query.shape[0]
    heads = query.shape[1] // HEAD_SIZE
    fill_keys(kv2, kv1, key_ref, value_ref, keys, values, rows)
    values_t = values[...].T
    for first, tile, low, width in windows(rows, keys.shape[0]):
        allowed = mask_of(start[:, first : first + tile], first, tile, low, width)
        for head in range(heads):
            lanes = slice(head * HEAD_SIZE, (head + 1) * HEAD_SIZE)
            scores = dot_nt(keys[low : low + width], query[first : first + tile, lanes])
            scores = jnp.where(allowed, scores * (SCALE * LOG2E), -jnp.inf)
            most = jnp.max(scores, axis=0, keepdims=True)
            weights = jnp.exp2(scores - most)
            total = jnp.sum(weights, axis=0, keepdims=True)
            out = dot_nn(values_t[:, low : low + width], weights.astype(jnp.bfloat16))
            attended[first : first + tile, lanes] = (out / total).T.astype(jnp.bfloat16)
            log_total[head : head + 1, first : first + tile] = most + jnp.log2(total)


def backward_kernel(
    start, log_total, query, kv2, kv1, key_ref, value_ref, attended, grad,
    query_grad, near, far, own, keys, values, key_sum, value_sum,
):
    rows = query.shape[0]
    heads = query.shape[1] // HEAD_SIZE
    fill_keys(kv2, kv1, key_ref, value_ref, keys, values, rows)
    keys_t = keys[...].T
    key_sum[...] = jnp.zeros_like(key_sum)
    value_sum[...] = jnp.zeros_like(value_sum)
    for first, tile, low, width in windows(rows, keys.shape[0]):
        allowed = mask_of(start[:, first : first + tile], first, tile, low, width)
        for head in range(heads):
            lanes = slice(head * HEAD_SIZE, (head + 1) * HEAD_SIZE)
            query_head = query[first : first + tile, lanes]
            grad_head = grad[first : first + tile, lanes]
            out_head = attended[first : first + tile, lanes]
            scores = dot_nt(keys[low : low + width], query_head) * (SCALE * LOG2E)
            scores = scores - log_total[head : head + 1, first : first + tile]
            weights = jnp.where(allowed, jnp.exp2(scores), 0.0)
            delta = grad_head.astype(jnp.float32) * out_head.astype(jnp.float32)
            delta = jnp.sum(delta.T, axis=0, keepdims=True)
            grad_dots = dot_nt(values[low : low + width], grad_head)
            shifted = (weights * (grad_dots - delta)).astype(jnp.bfloat16)
            value_sum[low : low + width] += dot_nn(weights.astype(jnp.bfloat16), grad_head)
            key_sum[low : low + width] += dot_nn(shifted, query_head)
            back = dot_nn(keys_t[:, low : low + width], shifted) * SCALE
            query_grad[first : first + tile, lanes] = back.T.astype(jnp.bfloat16)
    for place, out in enumerate((far, near, own)):
        part = slice(place * rows, (place + 1) * rows)
        out[:, 0:HEAD_SIZE] = (key_sum[part] * SCALE).astype(out.dtype)
        out[:, HEAD_SIZE:] = value_sum[part].astype(out.dtype)


def whole_vmem(count):
    return [pl.BlockSpec(memory_space=pltpu.VMEM)] * count


def params():
    return pltpu.CompilerParams(vmem_limit_bytes=48 * 1024 * 1024)


def attend(start, query, kv2, kv1, key, value):
    rows, columns = query.shape
    heads = columns // HEAD_SIZE
    cost = rows * (DOC_MOST + rows) * heads
    return pl.pallas_call(
        forward_kernel,
        out_shape=(
            jax.ShapeDtypeStruct((rows, columns), jnp.bfloat16),
            jax.ShapeDtypeStruct((heads, rows), jnp.float32),
        ),
        in_specs=whole_vmem(6),
        out_specs=tuple(whole_vmem(2)),
        scratch_shapes=[pltpu.VMEM((3 * rows, HEAD_SIZE), jnp.bfloat16)] * 2,
        compiler_params=params(),
        cost_estimate=pl.CostEstimate(flops=cost * 512, transcendentals=cost, bytes_accessed=4 * rows * columns),
        name="attend",
    )(start, query, kv2, kv1, key, value)


def attend_back(start, log_total, query, kv2, kv1, key, value, attended, grad):
    rows, columns = query.shape
    heads = columns // HEAD_SIZE
    cost = rows * (DOC_MOST + rows) * heads
    pair = jax.ShapeDtypeStruct((rows, 2 * HEAD_SIZE), jnp.bfloat16)
    return pl.pallas_call(
        backward_kernel,
        out_shape=(
            jax.ShapeDtypeStruct((rows, columns), jnp.bfloat16),
            pair,
            pair,
            jax.ShapeDtypeStruct((rows, 2 * HEAD_SIZE), jnp.float32),
        ),
        in_specs=whole_vmem(9),
        out_specs=tuple(whole_vmem(4)),
        scratch_shapes=[pltpu.VMEM((3 * rows, HEAD_SIZE), jnp.bfloat16)] * 2
        + [pltpu.VMEM((3 * rows, HEAD_SIZE), jnp.float32)] * 2,
        compiler_params=params(),
        cost_estimate=pl.CostEstimate(flops=cost * 1280, transcendentals=cost, bytes_accessed=10 * rows * columns),
        name="attend_back",
    )(start, log_total, query, kv2, kv1, key, value, attended, grad)


def swap_pair(value):
    devices = lax.axis_size("ctx")
    return lax.ppermute(value, "ctx", [(i, i ^ 1) for i in range(devices)])


def shift_line(value, by):
    devices = lax.axis_size("ctx")
    pairs = [(i, i + 2 * by) for i in range(devices) if 0 <= i + 2 * by < devices]
    return lax.ppermute(value, "ctx", pairs)


def swap_heads(value, bit):
    groups = lax.axis_size("hg")
    return lax.ppermute(value, "hg", [(i, i ^ bit) for i in range(groups)])


def line_pairs(pairs):
    return [(2 * a + y, 2 * b + y) for a, b in pairs for y in range(2)]


def along_line(value, pairs):
    return lax.ppermute(value, "ctx", line_pairs(pairs))


OUTER = [(0, 1), (1, 0), (2, 3), (3, 2)]
INNER = [(1, 2), (2, 1)]


def line_groups(line):
    return [[2 * i + y for i in range(line)] for y in range(2)]


def gather_line(value, line, place):
    if line != 4:
        return lax.all_gather(value, "ctx", axis=0, axis_index_groups=line_groups(line))
    end = (place == 0) | (place == 3)
    low = place < 2
    first = along_line(value, OUTER)
    second = along_line(value, INNER)
    third = along_line(first, INNER)
    fourth = along_line(second, OUTER)
    fifth = along_line(third, OUTER)
    near = jnp.where(end, fourth, second)
    far = jnp.where(end, fifth, third)
    even = jnp.where(place % 2 == 0, value, first)
    odd = jnp.where(place % 2 == 0, first, value)
    return jnp.stack([
        jnp.where(low, even, far),
        jnp.where(low, odd, near),
        jnp.where(low, near, even),
        jnp.where(low, far, odd),
    ])


def scatter_line(parts, line, place):
    if line != 4:
        return lax.psum_scatter(parts, "ctx", scatter_dimension=0, axis_index_groups=line_groups(line))
    order = jnp.array([[3, 2, 1, 0], [3, 2, 0, 1], [0, 1, 3, 2], [0, 1, 2, 3]], jnp.int32)[place]
    parts = [lax.dynamic_index_in_dim(parts, order[i], 0, keepdims=False) for i in range(4)]
    wide = [part.astype(jnp.float32) for part in parts]
    first = along_line(parts[0], OUTER)
    second = along_line(parts[1], OUTER)
    inner = along_line((wide[0] + first).astype(jnp.bfloat16), INNER)
    third = along_line((wide[2] + inner).astype(jnp.bfloat16), OUTER)
    other = along_line((wide[1] + second).astype(jnp.bfloat16), INNER)
    return wide[3] + third + other


def body(doc_ids, rotated_queries, rotated_keys, value_matrix, out_proj, cotangent):
    rows = rotated_queries.shape[0]
    columns = rotated_queries.shape[1]
    shard = out_proj.shape[0]
    devices = lax.axis_size("ctx")
    groups = lax.axis_size("hg")
    line = devices // 2
    index = lax.axis_index("ctx")
    parity, place = index % 2, index // 2
    group = lax.axis_index("hg")
    core, column = group % 2, group // 2
    half = line * shard

    kv = jnp.concatenate([rotated_keys, value_matrix], 1)
    docs = jnp.pad(doc_ids.reshape(-1, 2 * HEAD_SIZE), ((0, DOC_ROWS - rows // (2 * HEAD_SIZE)), (0, 0)))
    pack = jnp.concatenate([kv, docs.astype(jnp.bfloat16)], 0)
    far_kv = shift_line(pack, 1)
    near_kv = swap_pair(jnp.where(parity == 0, pack, far_kv))

    def docs_of(received, back):
        found = received[rows : rows + rows // (2 * HEAD_SIZE)].reshape(-1).astype(jnp.int32)
        return jnp.where(index >= back, found, -1)

    doc_window = jnp.concatenate([docs_of(far_kv, 2), docs_of(near_kv, 1), doc_ids])
    start = jnp.sum((doc_window[:, None] < doc_ids[None, :]).astype(jnp.int32), axis=0, keepdims=True)

    blocks = cotangent.reshape(rows, line, 2, shard)
    own_grad = lax.dynamic_index_in_dim(blocks, parity, 2, keepdims=False).reshape(rows, half)
    part = rows // groups
    sent = lax.dynamic_slice(blocks, (group * part, 0, 1 - parity, 0), (part, line, 1, shard)).reshape(part, half)
    quarter = swap_pair(sent)
    across = swap_heads(quarter, 2)
    mine = jnp.stack([jnp.where(column == 0, quarter, across), jnp.where(column == 0, across, quarter)])
    mate = swap_heads(mine, 1)
    pair_grad = jnp.stack([jnp.where(core == 0, mine, mate), jnp.where(core == 0, mate, mine)], 1)
    pair_grad = pair_grad.reshape(rows, half)

    weights = gather_line(out_proj, line, place).reshape(half, columns)

    attended, log_total = attend(start, rotated_queries, far_kv, near_kv, rotated_keys, value_matrix)
    pair_attended = swap_pair(attended)

    proj_parts = (dot_tn(own_grad, attended) + dot_tn(pair_grad, pair_attended)).astype(jnp.bfloat16)
    proj_grad = scatter_line(proj_parts.reshape(line, shard, columns), line, place).astype(jnp.bfloat16)

    pair_part = swap_pair(dot_nn(pair_grad, weights).astype(jnp.bfloat16))
    grad = (dot_nn(own_grad, weights) + pair_part).astype(jnp.bfloat16)

    width = half // groups
    chunks = weights.reshape(2, 2, width, columns)

    def chunk_of(across_at, core_at):
        return lax.dynamic_slice(chunks, (across_at, core_at, 0, 0), (1, 1, width, columns)).reshape(width, columns)

    order = [chunk_of(1 - column, 1 - core), chunk_of(column, 1 - core), chunk_of(1 - column, core), chunk_of(column, core)]

    def reduced(tokens):
        parts = [dot_nt(tokens, item) for item in order]
        mates = swap_heads(jnp.stack(parts[0:2]).astype(jnp.bfloat16), 1)
        across = swap_heads((parts[2] + mates[0]).astype(jnp.bfloat16), 2)
        return (parts[3] + mates[1] + across).astype(jnp.bfloat16)

    other_part = swap_pair(reduced(pair_attended))
    own_part = reduced(attended)
    layer_output = jnp.stack([
        jnp.where(parity == 0, own_part, other_part).reshape(rows, -1, shard),
        jnp.where(parity == 0, other_part, own_part).reshape(rows, -1, shard),
    ], 2).reshape(rows, 2 * width)

    query_grad, near, far, own = attend_back(
        start, log_total, rotated_queries, far_kv, near_kv, rotated_keys, value_matrix, attended, grad
    )
    returned = swap_pair(near)
    passed = far.astype(jnp.float32) + jnp.where(parity == 1, returned, 0)
    arrived = shift_line(passed.astype(jnp.bfloat16), -1)
    own = own + arrived + jnp.where(parity == 0, returned, 0)
    own = own.astype(jnp.bfloat16)
    return (layer_output, query_grad, own[:, 0:HEAD_SIZE], own[:, HEAD_SIZE:], proj_grad)


def solution(mesh):
    split = P("ctx", "hg")
    in_specs = (P("ctx"), split, split, split, split, P("ctx", None))
    return jax.shard_map(body, mesh=mesh, in_specs=in_specs, out_specs=(split,) * 5, check_vma=False)
```

time: 296 us -> 146 us (0.49)
  waiting for transfers between devices: 179 us -> 29.4 us
  matrix products: 42.9 us -> 15.5 us
  starting transfers between devices: 31.4 us -> 48.8 us
  Pallas kernels: 0 us -> 14.1 us
  between operations: 14.3 us -> 8.84 us
  local copies, waits for them, and re-layouts: 15.3 us -> 18.4 us
    reduce_scatter x1 -> x0, waiting for transfers between devices: 109 us -> none  [body(): lax.psum_scatter(contract_first(columns, attended), 'ctx', scatter_dimens...]
    all_gather x2 -> x0, waiting for transfers between devices: 44.6 us -> none  [the longest x1 44.6 us: body(): all_rows = lax.all_gather(out_proj, 'ctx', axis=0, tiled=True)]
    dot_general x27 -> x12, matrix products: 42.9 us -> 15.5 us  [the longest x8 8.09 us: dot_nt(): lax.dot_general(a, b, (((1,), (1,)), ((), ())), preferred_element_type=jn...]
    ppermute x10 -> x24, starting transfers between devices: 26 us -> 48.8 us  [the longest x10 31.5 us: along_line(): return lax.ppermute(value, 'ctx', line_pairs(pairs))]
    pallas_call x0 -> x2, Pallas kernels: none -> 14.1 us  [the longest x1 7.52 us: attend_back(): pl.pallas_call(backward_kernel, out_shape=(jax.ShapeDtypeStruct((rows, co...]
    ppermute x10 -> x24, waiting for transfers between devices: 18.8 us -> 29.4 us  [the longest x10 18.8 us: along_line(): return lax.ppermute(value, 'ctx', line_pairs(pairs))]
    all_to_all x1 -> x0, local copies, waits for them, and re-layouts: 6.3 us -> none  [body(): lax.all_to_all(all_rows, 'hg', split_axis=0, concat_axis=1, tiled=True)]
    all_to_all x1 -> x0, waiting for transfers between devices: 5.5 us -> none  [body(): lax.all_to_all(all_rows, 'hg', split_axis=0, concat_axis=1, tiled=True)]
  transfers between devices with their start and end apart: 14 -> 24, of which waited for: 7 -> 8; matrix products, arithmetic and copies ran while one was open for 19% -> 29% of each run, Pallas kernels for 0% -> 10%
where the time goes in v1:
time: 146 us; the launch traced here: 145 us
  starting transfers between devices  48.8 us (33%)
  waiting for transfers between devices  29.4 us (20%)
  local copies, waits for them, and re-layouts  18.4 us (13%)
  matrix products  15.5 us (11%)
  Pallas kernels  14.1 us (10%)
  other arithmetic  10.2 us (7%)
  between operations  8.84 us (6%)
    ppermute x10, starting transfers between devices, along_line(): return lax.ppermute(value, 'ctx', line_pairs(pairs))  31.5 us
    ppermute x10, waiting for transfers between devices, along_line(): return lax.ppermute(value, 'ctx', line_pairs(pairs))  18.8 us
    dot_general x8, matrix products, dot_nt(): lax.dot_general(a, b, (((1,), (1,)), ((), ())), preferred_element_type=jn...  8.09 us
    unnamed x24, local copies, waits for them, and re-layouts  7.99 us
    ppermute x2, starting transfers between devices, shift_line(): return lax.ppermute(value, 'ctx', pairs)  7.58 us
    pallas_call x1, Pallas kernels, attend_back(): pl.pallas_call(backward_kernel, out_shape=(jax.ShapeDtypeStruct((rows, co...  7.52 us
    pallas_call x1, Pallas kernels, attend(): pl.pallas_call(forward_kernel, out_shape=(jax.ShapeDtypeStruct((rows, col...  6.56 us
    ppermute x6, starting transfers between devices, swap_pair(): return lax.ppermute(value, 'ctx', [(i, i ^ 1) for i in range(devices)])  5.39 us
  transfers between devices with their start and end apart: 24, of which 8 were waited for; matrix products, arithmetic and copies ran while one was open for 29% of the time, Pallas kernels for 10%

profile of v1, /device:TPU:0, one launch (start us, length us, event | category | flops | bytes accessed | tf_op | source)
XLA Modules:
  0.0 145.2 jit_solution(5497599388727269155)
XLA Ops:
  0.6 3.1 %collective-permute-start.2 = (bf16[512,512]{1,0:T(8,128)(2,1)}, bf16[512,512]{1,0:T(8,128)(2,1)S(1)}, u32[]{:S(2)}, u32[]{:S(2)}) collective-permute-start(bf16[512,512]{1,0:T(8,128)(2,1)} %param.11), channel_id=1, source_target_pairs={{0,8},{4,12},{8,0},{12,4},{16,24},{20,28},{24,16},{28,20},{1,9},{5... | collective-permute-start | bytes 1572872 | tf_op jit(solution)/shard_map/ppermute | solution.py:175
  3.7 0.7 collective-permute-start.5
  4.4 0.7 convert.27
  5.1 1.0 fusion.30
  6.1 6.3 %collective-permute-start = (bf16[528,256]{1,0:T(8,128)(2,1)S(1)}, bf16[528,256]{1,0:T(8,128)(2,1)S(1)}, u32[]{:S(2)}, u32[]{:S(2)}) collective-permute-start(bf16[528,256]{1,0:T(8,128)(2,1)S(1)} %fusion.30), channel_id=1, source_target_pairs={{0,8},{4,12},{8,16},{12,20},{16,24},{20,28},{1,9},{5,13},{9,17},{1... | collective-permute-start | bytes 811016 | tf_op jit(solution)/shard_map/ppermute | solution.py:162
  12.4 6.5 %copy.46 = bf16[512,4096]{0,1:T(8,128)(2,1)} copy(bf16[512,4096]{1,0:T(8,128)(2,1)} %param.12) | data formatting | bytes 8388608 | tf_op args[5]
  18.9 1.1 constant_dynamic-slice_fusion.1
  20.0 1.6 %collective-permute-start.13 = (bf16[128,2048]{0,1:T(8,128)(2,1)S(1)}, bf16[128,2048]{0,1:T(8,128)(2,1)}, u32[]{:S(2)}, u32[]{:S(2)}) collective-permute-start(bf16[128,2048]{0,1:T(8,128)(2,1)S(1)} %bitcast.139), channel_id=1, source_target_pairs={{0,4},{4,0},{8,12},{12,8},{16,20},{20,16},{24,28},{28,24},{1,5},{5... | collective-permute-start | bytes 1572872 | tf_op jit(solution)/shard_map/ppermute | solution.py:156
  21.6 0.7 constant_dynamic-slice_fusion
  22.3 3.2 %constant_dynamic-slice_fusion.2 = bf16[512,4,1,512]{0,3,2,1:T(8,128)(2,1)} fusion(bf16[512,4,2,512]{0,3,2,1:T(8,128)(2,1)} %bitcast.132, s32[]{:T(128)S(6)} %select_n.213), kind=kLoop, calls=%fused_computation.84 | loop fusion | bytes 4194308 | tf_op jit(solution)/shard_map/jit(dynamic_index_in_dim)/dynamic_slice | solution.py:249
  25.6 0.6 collective-permute-start.1
  26.2 0.6 fusion.40
  34.6 0.7 collective-permute-start.3
  35.3 4.9 %collective-permute-start.6 = (bf16[512,512]{1,0:T(8,128)(2,1)S(1)}, bf16[512,512]{1,0:T(8,128)(2,1)S(1)}, u32[]{:S(2)}, u32[]{:S(2)}) collective-permute-start(bf16[512,512]{1,0:T(8,128)(2,1)S(1)} %collective-permute-done.5), channel_id=1, source_target_pairs={{0,8},{4,12},{8,0},{12,4},{16,24},{20,28},{24,16},{28,20},{1,9},{5... | collective-permute-start | bytes 1572872 | tf_op jit(solution)/shard_map/ppermute | solution.py:175
  40.2 1.5 %collective-permute-start.14 = (bf16[128,2048]{0,1:T(8,128)(2,1)}, bf16[128,2048]{0,1:T(8,128)(2,1)S(1)}, u32[]{:S(2)}, u32[]{:S(2)}) collective-permute-start(bf16[128,2048]{0,1:T(8,128)(2,1)} %collective-permute-done.13), channel_id=1, source_target_pairs={{0,2},{1,3},{2,0},{3,1},{4,6},{5,7},{6,4},{7,5},{8,10},{9,11},{10,... | collective-permute-start | bytes 1572872 | tf_op jit(solution)/shard_map/ppermute | solution.py:167
  41.8 0.4 convert_reduce_fusion
  42.1 6.6 %attend.1 = (bf16[512,512]{1,0:T(8,128)(2,1)S(1)}, f32[4,512]{1,0:T(4,128)S(1)}) custom-call(s32[1,512]{1,0:T(1,128)S(1)} %bitcast.117, bf16[512,512]{1,0:T(8,128)(2,1)S(1)} %copy-done.2, bf16[528,256]{1,0:T(8,128)(2,1)S(1)} %collective-permute-done.kv2, bf16[528,256]{1,0:T(8,128)(2,1)S(1)} %collective-permute-done.1.kv1, bf16[512,128]{1,0:T(8,128)(2,1)S(1)} %copy-done.1, ...), custom_call_target="tpu_custom_call" | custom-call | flops 1610612736 | bytes 1048576 | tf_op jit(solution)/shard_map/attend/pallas_call | solution.py:116
  48.7 0.6 collective-permute-start.9
  49.3 1.4 collective-permute-start.4
  50.7 1.5 %collective-permute-done.14 = bf16[128,2048]{0,1:T(8,128)(2,1)S(1)} collective-permute-done((bf16[128,2048]{0,1:T(8,128)(2,1)}, bf16[128,2048]{0,1:T(8,128)(2,1)S(1)}, u32[]{:S(2)}, u32[]{:S(2)}) %collective-permute-start.14) | collective-permute-done | bytes 524320 | tf_op jit(solution)/shard_map/ppermute | solution.py:167
  52.2 1.1 select_bitcast_fusion.3
  53.5 8.2 %collective-permute-done.4 = bf16[512,512]{1,0:T(8,128)(2,1)S(1)} collective-permute-done((bf16[512,512]{1,0:T(8,128)(2,1)S(1)}, bf16[512,512]{1,0:T(8,128)(2,1)S(1)}, u32[]{:S(2)}, u32[]{:S(2)}) %collective-permute-start.4) | collective-permute-done | bytes 524320 | tf_op jit(solution)/shard_map/ppermute | solution.py:175
  61.7 0.2 select_bitcast_fusion.9
  62.0 0.3 pad_maximum_fusion
  62.3 0.5 fusion.7
  62.7 0.5 fusion.6
  63.4 0.5 fusion.8
  63.9 0.5 fusion.9
  64.4 1.1 pad_maximum_fusion.3
  65.5 0.5 collective-permute-start.10
  65.9 0.1 select_bitcast_fusion.1
  66.1 1.5 %pad_maximum_fusion.1 = bf16[2,2,128,2048]{2,3,0,1:T(8,128)(2,1)} fusion(bf16[2,1,128,2048]{2,3,0,1:T(8,128)(2,1)S(1)} %get-tuple-element.40, bf16[2,1,128,2048]{2,3,0,1:T(8,128)(2,1)S(1)} %get-tuple-element.39), kind=kLoop, calls=%fused_computation.3 | loop fusion | flops 1048576 | bytes 4194304 | tf_op jit(solution)/shard_map/stack | solution.py:256
  67.6 4.0 %copy.47 = bf16[2,2,128,2048]{3,2,1,0:T(8,128)(2,1)} copy(bf16[2,2,128,2048]{2,3,0,1:T(8,128)(2,1)} %pad_maximum_fusion.1) | data formatting | bytes 4194304 | tf_op jit(solution)/shard_map/stack | solution.py:256
  71.6 3.6 %convolution_convert_fusion = bf16[512,512]{1,0:T(8,128)(2,1)S(1)} fusion(bf16[512,2048]{1,0:T(8,128)(2,1)} %bitcast.133, bf16[2048,512]{1,0:T(8,128)(2,1)} %bitcast.125), kind=kOutput, calls=%fused_computation.12 | convolution fusion | flops 1074003968 | bytes 4718592 | tf_op jit(solution)/shard_map/dot_general | solution.py:19
  75.3 0.6 collective-permute-start.16
  75.9 1.3 fusion.43
  77.2 1.2 add_convert_fusion
  78.5 1.8 %collective-permute-start.19 = (bf16[512,512]{1,0:T(8,128)(2,1)S(1)}, bf16[512,512]{1,0:T(8,128)(2,1)S(1)}, u32[]{:S(2)}, u32[]{:S(2)}) collective-permute-start(bf16[512,512]{1,0:T(8,128)(2,1)S(1)} %get-tuple-element.37), channel_id=1, source_target_pairs={{0,8},{4,12},{8,0},{12,4},{16,24},{20,28},{24,16},{28,20},{1,9},{5... | collective-permute-start | bytes 1572872 | tf_op jit(solution)/shard_map/ppermute | solution.py:175
  80.3 0.3 collective-permute-start.22
  80.6 0.2 copy-done.5
  80.8 1.5 %fusion.4 = bf16[512,512]{0,1:T(8,128)(2,1)S(1)} fusion(bf16[512,512]{1,0:T(8,128)(2,1)S(1)} %get-tuple-element.11.attended, bf16[2,512,512]{1,2,0:T(8,128)(2,1)} %collective-permute-done.7, bf16[2,2,512,512]{3,2,1,0:T(8,128)(2,1)S(1)} %bitcast.126, s32[]{:T(128)S(6)} %select_n.209, s32[]{:T(128)S(6)} %select_n.208), kind=kOutput, calls=%fused_computation.17 | convolution fusion | flops 269221888 | bytes 2097160 | tf_op jit(solution)/shard_map/dot_general | solution.py:23
  82.3 1.6 %collective-permute-start.8 = (bf16[512,512]{0,1:T(8,128)(2,1)S(1)}, bf16[512,512]{0,1:T(8,128)(2,1)S(1)}, u32[]{:S(2)}, u32[]{:S(2)}) collective-permute-start(bf16[512,512]{0,1:T(8,128)(2,1)S(1)} %fusion.4), channel_id=1, source_target_pairs={{0,2},{1,3},{2,0},{3,1},{4,6},{5,7},{6,4},{7,5},{8,10},{9,11},{10,... | collective-permute-start | bytes 1572872 | tf_op jit(solution)/shard_map/ppermute | solution.py:167
  83.9 1.5 %fusion.5 = bf16[512,512]{0,1:T(8,128)(2,1)S(1)} fusion(bf16[512,512]{1,0:T(8,128)(2,1)S(1)} %collective-permute-done.9, bf16[2,512,512]{1,2,0:T(8,128)(2,1)} %collective-permute-done.10, bf16[2,2,512,512]{3,2,1,0:T(8,128)(2,1)S(1)} %bitcast.127, s32[]{:T(128)S(6)} %select_n.209, s32[]{:T(128)S(6)} %select_n.208), kind=kOutput, calls=%fused_computation.18 | convolution fusion | flops 269221888 | bytes 2097160 | tf_op jit(solution)/shard_map/dot_general | solution.py:23
  85.4 0.6 collective-permute-start.11
  86.0 3.2 %collective-permute-done.16 = bf16[512,512]{1,0:T(8,128)(2,1)S(1)} collective-permute-done((bf16[512,512]{1,0:T(8,128)(2,1)S(1)}, bf16[512,512]{1,0:T(8,128)(2,1)S(1)}, u32[]{:S(2)}, u32[]{:S(2)}) %collective-permute-start.16) | collective-permute-done | bytes 524320 | tf_op jit(solution)/shard_map/ppermute | solution.py:156
  89.2 1.3 add_convert_fusion.3.grad
  90.5 7.5 %attend_back.1 = (bf16[512,512]{1,0:T(8,128)(2,1)}, bf16[512,256]{1,0:T(8,128)(2,1)S(1)}, bf16[512,256]{1,0:T(8,128)(2,1)S(1)}, f32[512,256]{1,0:T(8,128)S(1)}) custom-call(s32[1,512]{1,0:T(1,128)S(1)} %bitcast.118, f32[4,512]{1,0:T(4,128)S(1)} %get-tuple-element.12.log_total, bf16[512,512]{1,0:T(8,128)(2,1)S(1)} %copy-done.2, ...), custom_call_target="tpu_custom_call" | custom-call | flops 4026531840 | bytes 2621440 | tf_op jit(solution)/shard_map/attend_back/pallas_call | solution.py:136
  98.0 0.5 collective-permute-start.17
  98.6 0.7 collective-permute-start.20
  99.3 4.1 %collective-permute-done.22 = bf16[512,512]{1,0:T(8,128)(2,1)S(1)} collective-permute-done((bf16[512,512]{1,0:T(8,128)(2,1)S(1)}, bf16[512,512]{1,0:T(8,128)(2,1)S(1)}, u32[]{:S(2)}, u32[]{:S(2)}) %collective-permute-start.22) | collective-permute-done | bytes 524320 | tf_op jit(solution)/shard_map/ppermute | solution.py:175
  103.5 0.7 collective-permute-start.23
  104.2 1.1 collective-permute-done.17
  105.5 1.3 collective-permute-start.18
  106.8 0.4 collective-permute-done.11
  107.2 1.5 %fusion.3 = bf16[512,512]{0,1:T(8,128)(2,1)S(1)} fusion(bf16[512,512]{1,0:T(8,128)(2,1)S(1)} %collective-permute-done.9, bf16[512,512]{0,1:T(8,128)(2,1)S(1)} %collective-permute-done.11, bf16[2,512,512]{1,2,0:T(8,128)(2,1)} %collective-permute-done.10, bf16[2,2,512,512]{3,2,1,0:T(8,128)(2,1)S(1)} %bitcast.129, s32[]{:T(128)S(6)} %select_n.206, ...), kind=kOutput, calls=%fused_computation.11 | convolution fusion | flops 269746176 | bytes 2621448 | tf_op jit(solution)/shard_map/dot_general | solution.py:23
  108.7 1.6 %collective-permute-start.12 = (bf16[512,512]{0,1:T(8,128)(2,1)S(1)}, bf16[512,512]{0,1:T(8,128)(2,1)S(1)}, u32[]{:S(2)}, u32[]{:S(2)}) collective-permute-start(bf16[512,512]{0,1:T(8,128)(2,1)S(1)} %fusion.3), channel_id=1, source_target_pairs={{0,4},{4,0},{8,12},{12,8},{16,20},{20,16},{24,28},{28,24},{1,5},{5... | collective-permute-start | bytes 1572872 | tf_op jit(solution)/shard_map/ppermute | solution.py:156
  110.3 4.3 %collective-permute-done.18 = bf16[512,256]{1,0:T(8,128)(2,1)S(1)} collective-permute-done((bf16[512,256]{1,0:T(8,128)(2,1)S(1)}, bf16[512,256]{1,0:T(8,128)(2,1)S(1)}, u32[]{:S(2)}, u32[]{:S(2)}) %collective-permute-start.18) | collective-permute-done | bytes 262176 | tf_op jit(solution)/shard_map/ppermute | solution.py:162
  114.7 0.9 fusion.10
  115.6 17.3 %collective-permute-start.21 = (bf16[512,512]{1,0:T(8,128)(2,1)}, bf16[512,512]{1,0:T(8,128)(2,1)S(1)}, u32[]{:S(2)}, u32[]{:S(2)}) collective-permute-start(bf16[512,512]{1,0:T(8,128)(2,1)} %fusion.10), channel_id=1, source_target_pairs={{0,8},{4,12},{8,0},{12,4},{16,24},{20,28},{24,16},{28,20},{1,9},{5... | collective-permute-start | bytes 1572872 | tf_op jit(solution)/shard_map/ppermute | solution.py:175
  132.9 0.7 fusion.39
  133.6 1.7 %select_bitcast_fusion.5 = (bf16[512,1,1,512]{0,3,2,1:T(8,128)(2,1)S(1)}, bf16[512,1,1,512]{0,3,2,1:T(8,128)(2,1)S(1)}) fusion(bf16[512,512]{0,1:T(8,128)(2,1)S(1)} %collective-permute-done.12, pred[]{:T(512)S(6)} %eq.32, bf16[512,512]{0,1:T(8,128)(2,1)S(1)} %collective-permute-done.8, bf16[2,512,512]{1,2,0:T(8,128)(2,1)} %collective-permute-done.7, ...), kind=kOutput, calls=%fused_computation.58 | convolution fusion | flops 270270464 | bytes 3670025 | tf_op jit(solution)/shard_map/dot_general | solution.py:23
  135.4 1.3 copy.48
  136.7 6.5 %collective-permute-done.21 = bf16[512,512]{1,0:T(8,128)(2,1)S(1)} collective-permute-done((bf16[512,512]{1,0:T(8,128)(2,1)}, bf16[512,512]{1,0:T(8,128)(2,1)S(1)}, u32[]{:S(2)}, u32[]{:S(2)}) %collective-permute-start.21) | collective-permute-done | bytes 524320 | tf_op jit(solution)/shard_map/ppermute | solution.py:175
  143.2 2.0 %fusion.12 = bf16[512,512]{1,0:T(8,128)(2,1)} fusion(bf16[512,512]{1,0:T(8,128)(2,1)S(1)} %collective-permute-done.23, bf16[512,512]{1,0:T(8,128)(2,1)S(1)} %collective-permute-done.21, bf16[4,512,512]{2,1,0:T(8,128)(2,1)} %bitcast.137, s32[]{:T(128)S(6)} %select_n.227), kind=kLoop, calls=%fused_computation.31 | loop fusion | flops 1572864 | bytes 2097156 | tf_op jit(solution)/shard_map/convert_element_type | solution.py:265
  (52 shorter events, 1.2 us)
Async XLA Ops:
  0.6 33.9 %collective-permute-start.2 = (bf16[512,512]{1,0:T(8,128)(2,1)}, bf16[512,512]{1,0:T(8,128)(2,1)S(1)}, u32[]{:S(2)}, u32[]{:S(2)}) collective-permute-start(bf16[512,512]{1,0:T(8,128)(2,1)} %param.11), channel_id=1, source_target_pairs={{0,8},{4,12},{8,0},{12,4},{16,24},{20,28},{24,16},{28,20},{1,9},{5... | collective-permute-start | bytes 1572872 | tf_op jit(solution)/shard_map/ppermute | solution.py:175
  3.7 31.6 %collective-permute-start.5 = (bf16[512,512]{1,0:T(8,128)(2,1)}, bf16[512,512]{1,0:T(8,128)(2,1)S(1)}, u32[]{:S(2)}, u32[]{:S(2)}) collective-permute-start(bf16[512,512]{1,0:T(8,128)(2,1)} %param.11), channel_id=1, source_target_pairs={{8,16},{12,20},{16,8},{20,12},{9,17},{13,21},{17,9},{21,13},{10,18... | collective-permute-start | bytes 1572872 | tf_op jit(solution)/shard_map/ppermute | solution.py:175
  6.1 19.4 %collective-permute-start = (bf16[528,256]{1,0:T(8,128)(2,1)S(1)}, bf16[528,256]{1,0:T(8,128)(2,1)S(1)}, u32[]{:S(2)}, u32[]{:S(2)}) collective-permute-start(bf16[528,256]{1,0:T(8,128)(2,1)S(1)} %fusion.30), channel_id=1, source_target_pairs={{0,8},{4,12},{8,16},{12,20},{16,24},{20,28},{1,9},{5,13},{9,17},{1... | collective-permute-start | bytes 811016 | tf_op jit(solution)/shard_map/ppermute | solution.py:162
  20.0 20.2 %collective-permute-start.13 = (bf16[128,2048]{0,1:T(8,128)(2,1)S(1)}, bf16[128,2048]{0,1:T(8,128)(2,1)}, u32[]{:S(2)}, u32[]{:S(2)}) collective-permute-start(bf16[128,2048]{0,1:T(8,128)(2,1)S(1)} %bitcast.139), channel_id=1, source_target_pairs={{0,4},{4,0},{8,12},{12,8},{16,20},{20,16},{24,28},{28,24},{1,5},{5... | collective-permute-start | bytes 1572872 | tf_op jit(solution)/shard_map/ppermute | solution.py:156
  22.3 3.2 %copy-start = (bf16[512,128]{1,0:T(8,128)(2,1)S(1)}, bf16[512,128]{1,0:T(8,128)(2,1)}, u32[]{:S(2)}) copy-start(bf16[512,128]{1,0:T(8,128)(2,1)} %value_ref.3) | copy-start | bytes 393220
  22.3 3.2 %copy-start.1 = (bf16[512,128]{1,0:T(8,128)(2,1)S(1)}, bf16[512,128]{1,0:T(8,128)(2,1)}, u32[]{:S(2)}) copy-start(bf16[512,128]{1,0:T(8,128)(2,1)} %key_ref.3) | copy-start | bytes 393220
  22.3 19.4 %copy-start.9 = (s32[512]{0:T(512)S(1)}, s32[512]{0:T(512)}, u32[]{:S(2)}) copy-start(s32[512]{0:T(512)} %param.7) | copy-start | bytes 6148
  22.3 19.8 %copy-start.2 = (bf16[512,512]{1,0:T(8,128)(2,1)S(1)}, bf16[512,512]{1,0:T(8,128)(2,1)}, u32[]{:S(2)}) copy-start(bf16[512,512]{1,0:T(8,128)(2,1)} %query.3) | copy-start | bytes 1572868
  25.6 16.1 %collective-permute-start.1 = (bf16[528,256]{1,0:T(8,128)(2,1)S(1)}, bf16[528,256]{1,0:T(8,128)(2,1)S(1)}, u32[]{:S(2)}, u32[]{:S(2)}) collective-permute-start(bf16[528,256]{1,0:T(8,128)(2,1)S(1)} %broadcast_select_fusion.4), channel_id=1, source_target_pairs={{0,4},{4,0},{8,12},{12,8},{16,20},{20,16},{24,28},{28,24},{1,5},{5... | collective-permute-start | bytes 811016 | tf_op jit(solution)/shard_map/ppermute | solution.py:156
  34.6 14.7 %collective-permute-start.3 = (bf16[512,512]{1,0:T(8,128)(2,1)S(1)}, bf16[512,512]{1,0:T(8,128)(2,1)S(1)}, u32[]{:S(2)}, u32[]{:S(2)}) collective-permute-start(bf16[512,512]{1,0:T(8,128)(2,1)S(1)} %collective-permute-done.2), channel_id=1, source_target_pairs={{8,16},{12,20},{16,8},{20,12},{9,17},{13,21},{17,9},{21,13},{10,18... | collective-permute-start | bytes 1572872 | tf_op jit(solution)/shard_map/ppermute | solution.py:175
  35.3 18.2 %collective-permute-start.6 = (bf16[512,512]{1,0:T(8,128)(2,1)S(1)}, bf16[512,512]{1,0:T(8,128)(2,1)S(1)}, u32[]{:S(2)}, u32[]{:S(2)}) collective-permute-start(bf16[512,512]{1,0:T(8,128)(2,1)S(1)} %collective-permute-done.5), channel_id=1, source_target_pairs={{0,8},{4,12},{8,0},{12,4},{16,24},{20,28},{24,16},{28,20},{1,9},{5... | collective-permute-start | bytes 1572872 | tf_op jit(solution)/shard_map/ppermute | solution.py:175
  40.2 11.9 %collective-permute-start.14 = (bf16[128,2048]{0,1:T(8,128)(2,1)}, bf16[128,2048]{0,1:T(8,128)(2,1)S(1)}, u32[]{:S(2)}, u32[]{:S(2)}) collective-permute-start(bf16[128,2048]{0,1:T(8,128)(2,1)} %collective-permute-done.13), channel_id=1, source_target_pairs={{0,2},{1,3},{2,0},{3,1},{4,6},{5,7},{6,4},{7,5},{8,10},{9,11},{10,... | collective-permute-start | bytes 1572872 | tf_op jit(solution)/shard_map/ppermute | solution.py:167
  48.7 13.0 %copy-start.8 = (bf16[512,512]{1,0:T(8,128)(2,1)S(1)}, bf16[512,512]{1,0:T(8,128)(2,1)}, u32[]{:S(2)}) copy-start(bf16[512,512]{1,0:T(8,128)(2,1)} %param.11) | copy-start | bytes 1572868
  48.7 14.7 %collective-permute-start.9 = (bf16[512,512]{1,0:T(8,128)(2,1)S(1)}, bf16[512,512]{1,0:T(8,128)(2,1)S(1)}, u32[]{:S(2)}, u32[]{:S(2)}) collective-permute-start(bf16[512,512]{1,0:T(8,128)(2,1)S(1)} %get-tuple-element.11.attended), channel_id=1, source_target_pairs={{0,4},{4,0},{8,12},{12,8},{16,20},{20,16},{24,28},{28,24},{1,5},{5... | collective-permute-start | bytes 1572872 | tf_op jit(solution)/shard_map/ppermute | solution.py:156
  49.3 12.4 %collective-permute-start.4 = (bf16[512,512]{1,0:T(8,128)(2,1)S(1)}, bf16[512,512]{1,0:T(8,128)(2,1)S(1)}, u32[]{:S(2)}, u32[]{:S(2)}) collective-permute-start(bf16[512,512]{1,0:T(8,128)(2,1)S(1)} %collective-permute-done.3), channel_id=1, source_target_pairs={{0,8},{4,12},{8,0},{12,4},{16,24},{20,28},{24,16},{28,20},{1,9},{5... | collective-permute-start | bytes 1572872 | tf_op jit(solution)/shard_map/ppermute | solution.py:175
  53.4 12.5 %collective-permute-start.15 = (bf16[2,128,2048]{1,2,0:T(8,128)(2,1)S(1)}, bf16[2,128,2048]{1,2,0:T(8,128)(2,1)S(1)}, u32[]{:S(2)}, u32[]{:S(2)}) collective-permute-start(bf16[2,128,2048]{1,2,0:T(8,128)(2,1)S(1)} %pad_maximum_fusion.5), channel_id=1, source_target_pairs={{0,1},{1,0},{2,3},{3,2},{4,5},{5,4},{6,7},{7,6},{8,9},{9,8},{10,11... | collective-permute-start | bytes 3145736 | tf_op jit(solution)/shard_map/ppermute | solution.py:167
  62.3 1.6 %copy-start.4 = (bf16[4,512,512]{2,1,0:T(8,128)(2,1)}, bf16[4,512,512]{2,1,0:T(8,128)(2,1)S(1)}, u32[]{:S(2)}) copy-start(bf16[4,512,512]{2,1,0:T(8,128)(2,1)S(1)} %pad_maximum_fusion) | copy-start | bytes 6291460
  63.3 17.3 %collective-permute-start.7 = (bf16[2,512,512]{1,2,0:T(8,128)(2,1)S(1)}, bf16[2,512,512]{1,2,0:T(8,128)(2,1)}, u32[]{:S(2)}, u32[]{:S(2)}) collective-permute-start(bf16[2,512,512]{1,2,0:T(8,128)(2,1)S(1)} %pad_maximum_fusion.2), channel_id=1, source_target_pairs={{0,1},{1,0},{2,3},{3,2},{4,5},{5,4},{6,7},{7,6},{8,9},{9,8},{10,11... | collective-permute-start | bytes 3145736 | tf_op jit(solution)/shard_map/ppermute | solution.py:167
  65.5 18.4 %collective-permute-start.10 = (bf16[2,512,512]{1,2,0:T(8,128)(2,1)}, bf16[2,512,512]{1,2,0:T(8,128)(2,1)}, u32[]{:S(2)}, u32[]{:S(2)}) collective-permute-start(bf16[2,512,512]{1,2,0:T(8,128)(2,1)} %pad_maximum_fusion.3), channel_id=1, source_target_pairs={{0,1},{1,0},{2,3},{3,2},{4,5},{5,4},{6,7},{7,6},{8,9},{9,8},{10,11... | collective-permute-start | bytes 3145736 | tf_op jit(solution)/shard_map/ppermute | solution.py:167
  71.6 4.2 %copy-start.6 = (bf16[2,2,128,2048]{3,2,1,0:T(8,128)(2,1)S(1)}, bf16[2,2,128,2048]{3,2,1,0:T(8,128)(2,1)}, u32[]{:S(2)}) copy-start(bf16[2,2,128,2048]{3,2,1,0:T(8,128)(2,1)} %copy.47) | copy-start | bytes 6291460
  75.3 1.9 %copy-start.3 = (bf16[512,4,1,512]{0,3,2,1:T(8,128)(2,1)S(1)}, bf16[512,4,1,512]{0,3,2,1:T(8,128)(2,1)}, u32[]{:S(2)}) copy-start(bf16[512,4,1,512]{0,3,2,1:T(8,128)(2,1)} %constant_dynamic-slice_fusion.2) | copy-start | bytes 6291460
  75.3 13.9 %collective-permute-start.16 = (bf16[512,512]{1,0:T(8,128)(2,1)S(1)}, bf16[512,512]{1,0:T(8,128)(2,1)S(1)}, u32[]{:S(2)}, u32[]{:S(2)}) collective-permute-start(bf16[512,512]{1,0:T(8,128)(2,1)S(1)} %convolution_convert_fusion), channel_id=1, source_target_pairs={{0,4},{4,0},{8,12},{12,8},{16,20},{20,16},{24,28},{28,24},{1,5},{5... | collective-permute-start | bytes 1572872 | tf_op jit(solution)/shard_map/ppermute | solution.py:156
  78.4 36.3 %copy-start.7 = (bf16[2048,512]{1,0:T(8,128)(2,1)}, bf16[2048,512]{1,0:T(8,128)(2,1)S(1)}, u32[]{:S(2)}) copy-start(bf16[2048,512]{1,0:T(8,128)(2,1)S(1)} %add_convert_fusion) | copy-start | bytes 6291460
  78.4 2.3 %copy-start.5 = (bf16[4,512,512]{2,1,0:T(8,128)(2,1)S(1)}, bf16[4,512,512]{2,1,0:T(8,128)(2,1)}, u32[]{:S(2)}) copy-start(bf16[4,512,512]{2,1,0:T(8,128)(2,1)} %copy-done.4) | copy-start | bytes 6291460
  78.5 20.0 %collective-permute-start.19 = (bf16[512,512]{1,0:T(8,128)(2,1)S(1)}, bf16[512,512]{1,0:T(8,128)(2,1)S(1)}, u32[]{:S(2)}, u32[]{:S(2)}) collective-permute-start(bf16[512,512]{1,0:T(8,128)(2,1)S(1)} %get-tuple-element.37), channel_id=1, source_target_pairs={{0,8},{4,12},{8,0},{12,4},{16,24},{20,28},{24,16},{28,20},{1,9},{5... | collective-permute-start | bytes 1572872 | tf_op jit(solution)/shard_map/ppermute | solution.py:175
  80.3 23.1 %collective-permute-start.22 = (bf16[512,512]{1,0:T(8,128)(2,1)S(1)}, bf16[512,512]{1,0:T(8,128)(2,1)S(1)}, u32[]{:S(2)}, u32[]{:S(2)}) collective-permute-start(bf16[512,512]{1,0:T(8,128)(2,1)S(1)} %get-tuple-element.38), channel_id=1, source_target_pairs={{0,8},{4,12},{8,0},{12,4},{16,24},{20,28},{24,16},{28,20},{1,9},{5... | collective-permute-start | bytes 1572872 | tf_op jit(solution)/shard_map/ppermute | solution.py:175
  82.3 51.3 %collective-permute-start.8 = (bf16[512,512]{0,1:T(8,128)(2,1)S(1)}, bf16[512,512]{0,1:T(8,128)(2,1)S(1)}, u32[]{:S(2)}, u32[]{:S(2)}) collective-permute-start(bf16[512,512]{0,1:T(8,128)(2,1)S(1)} %fusion.4), channel_id=1, source_target_pairs={{0,2},{1,3},{2,0},{3,1},{4,6},{5,7},{6,4},{7,5},{8,10},{9,11},{10,... | collective-permute-start | bytes 1572872 | tf_op jit(solution)/shard_map/ppermute | solution.py:167
  85.4 21.8 %collective-permute-start.11 = (bf16[512,512]{0,1:T(8,128)(2,1)S(1)}, bf16[512,512]{0,1:T(8,128)(2,1)S(1)}, u32[]{:S(2)}, u32[]{:S(2)}) collective-permute-start(bf16[512,512]{0,1:T(8,128)(2,1)S(1)} %fusion.5), channel_id=1, source_target_pairs={{0,2},{1,3},{2,0},{3,1},{4,6},{5,7},{6,4},{7,5},{8,10},{9,11},{10,... | collective-permute-start | bytes 1572872 | tf_op jit(solution)/shard_map/ppermute | solution.py:167
  98.0 7.4 %collective-permute-start.17 = (bf16[512,256]{1,0:T(8,128)(2,1)S(1)}, bf16[512,256]{1,0:T(8,128)(2,1)S(1)}, u32[]{:S(2)}, u32[]{:S(2)}) collective-permute-start(bf16[512,256]{1,0:T(8,128)(2,1)S(1)} %get-tuple-element.16), channel_id=1, source_target_pairs={{0,4},{4,0},{8,12},{12,8},{16,20},{20,16},{24,28},{28,24},{1,5},{5... | collective-permute-start | bytes 786440 | tf_op jit(solution)/shard_map/ppermute | solution.py:156
  98.6 16.0 %collective-permute-start.20 = (bf16[512,512]{1,0:T(8,128)(2,1)S(1)}, bf16[512,512]{1,0:T(8,128)(2,1)S(1)}, u32[]{:S(2)}, u32[]{:S(2)}) collective-permute-start(bf16[512,512]{1,0:T(8,128)(2,1)S(1)} %add_convert_fusion.2), channel_id=1, source_target_pairs={{8,16},{12,20},{16,8},{20,12},{9,17},{13,21},{17,9},{21,13},{10,18... | collective-permute-start | bytes 1572872 | tf_op jit(solution)/shard_map/ppermute | solution.py:175
  103.5 33.2 %collective-permute-start.23 = (bf16[512,512]{1,0:T(8,128)(2,1)S(1)}, bf16[512,512]{1,0:T(8,128)(2,1)S(1)}, u32[]{:S(2)}, u32[]{:S(2)}) collective-permute-start(bf16[512,512]{1,0:T(8,128)(2,1)S(1)} %add_convert_fusion.1), channel_id=1, source_target_pairs={{8,16},{12,20},{16,8},{20,12},{9,17},{13,21},{17,9},{21,13},{10,18... | collective-permute-start | bytes 1572872 | tf_op jit(solution)/shard_map/ppermute | solution.py:175
  105.5 9.1 %collective-permute-start.18 = (bf16[512,256]{1,0:T(8,128)(2,1)S(1)}, bf16[512,256]{1,0:T(8,128)(2,1)S(1)}, u32[]{:S(2)}, u32[]{:S(2)}) collective-permute-start(bf16[512,256]{1,0:T(8,128)(2,1)S(1)} %add_convert_fusion.5), channel_id=1, source_target_pairs={{8,0},{12,4},{16,8},{20,12},{24,16},{28,20},{9,1},{13,5},{17,9},{2... | collective-permute-start | bytes 786440 | tf_op jit(solution)/shard_map/ppermute | solution.py:162
  108.7 24.9 %collective-permute-start.12 = (bf16[512,512]{0,1:T(8,128)(2,1)S(1)}, bf16[512,512]{0,1:T(8,128)(2,1)S(1)}, u32[]{:S(2)}, u32[]{:S(2)}) collective-permute-start(bf16[512,512]{0,1:T(8,128)(2,1)S(1)} %fusion.3), channel_id=1, source_target_pairs={{0,4},{4,0},{8,12},{12,8},{16,20},{20,16},{24,28},{28,24},{1,5},{5... | collective-permute-start | bytes 1572872 | tf_op jit(solution)/shard_map/ppermute | solution.py:156
  115.6 27.5 %collective-permute-start.21 = (bf16[512,512]{1,0:T(8,128)(2,1)}, bf16[512,512]{1,0:T(8,128)(2,1)S(1)}, u32[]{:S(2)}, u32[]{:S(2)}) collective-permute-start(bf16[512,512]{1,0:T(8,128)(2,1)} %fusion.10), channel_id=1, source_target_pairs={{0,8},{4,12},{8,0},{12,4},{16,24},{20,28},{24,16},{28,20},{1,9},{5... | collective-permute-start | bytes 1572872 | tf_op jit(solution)/shard_map/ppermute | solution.py:175

commit v2 on v1

--- a/solution.py
+++ b/solution.py
@@ -68,13 +68,14 @@
 
 
 def backward_kernel(
-    start, log_total, query, kv2, kv1, key_ref, value_ref, attended, grad,
-    query_grad, near, far, own, keys, values, key_sum, value_sum,
+    start, log_total, query, kv2, kv1, key_ref, value_ref, attended, own_grad, pair_grad,
+    query_grad, near, far, own, keys, values, key_sum, value_sum, grad,
 ):
     rows = query.shape[0]
     heads = query.shape[1] // HEAD_SIZE
     fill_keys(kv2, kv1, key_ref, value_ref, keys, values, rows)
     keys_t = keys[...].T
+    grad[...] = (own_grad[...] + pair_grad[...]).astype(grad.dtype)
     key_sum[...] = jnp.zeros_like(key_sum)
     value_sum[...] = jnp.zeros_like(value_sum)
     for first, tile, low, width in windows(rows, keys.shape[0]):
@@ -128,7 +129,7 @@
     )(start, query, kv2, kv1, key, value)
 
 
-def attend_back(start, log_total, query, kv2, kv1, key, value, attended, grad):
+def attend_back(start, log_total, query, kv2, kv1, key, value, attended, own_grad, pair_grad):
     rows, columns = query.shape
     heads = columns // HEAD_SIZE
     cost = rows * (DOC_MOST + rows) * heads
@@ -141,14 +142,42 @@
             pair,
             jax.ShapeDtypeStruct((rows, 2 * HEAD_SIZE), jnp.float32),
         ),
-        in_specs=whole_vmem(9),
+        in_specs=whole_vmem(10),
         out_specs=tuple(whole_vmem(4)),
         scratch_shapes=[pltpu.VMEM((3 * rows, HEAD_SIZE), jnp.bfloat16)] * 2
-        + [pltpu.VMEM((3 * rows, HEAD_SIZE), jnp.float32)] * 2,
+        + [pltpu.VMEM((3 * rows, HEAD_SIZE), jnp.float32)] * 2
+        + [pltpu.VMEM((rows, columns), jnp.bfloat16)],
         compiler_params=params(),
         cost_estimate=pl.CostEstimate(flops=cost * 1280, transcendentals=cost, bytes_accessed=10 * rows * columns),
         name="attend_back",
-    )(start, log_total, query, kv2, kv1, key, value, attended, grad)
+    )(start, log_total, query, kv2, kv1, key, value, attended, own_grad, pair_grad)
+
+
+def output_kernel(order, tokens, weights, sent, far, near):
+    sent[0] = dot_nt(tokens[...], weights[order[0]]).astype(sent.dtype)
+    sent[1] = dot_nt(tokens[...], weights[order[1]]).astype(sent.dtype)
+    far[...] = dot_nt(tokens[...], weights[order[2]]).astype(far.dtype)
+    near[...] = dot_nt(tokens[...], weights[order[3]]).astype(near.dtype)
+
+
+def output_parts_of(order, tokens, weights):
+    line, shard, columns = weights.shape
+    rows = tokens.shape[0]
+    return pl.pallas_call(
+        output_kernel,
+        out_shape=(
+            jax.ShapeDtypeStruct((2, rows, shard), jnp.bfloat16),
+            jax.ShapeDtypeStruct((rows, shard), jnp.float32),
+            jax.ShapeDtypeStruct((rows, shard), jnp.float32),
+        ),
+        in_specs=[pl.BlockSpec(memory_space=pltpu.SMEM)] + whole_vmem(2),
+        out_specs=tuple(whole_vmem(3)),
+        compiler_params=params(),
+        cost_estimate=pl.CostEstimate(
+            flops=2 * line * shard * rows * columns, transcendentals=0, bytes_accessed=8 * line * shard * rows
+        ),
+        name="output_parts",
+    )(order, tokens, weights)
 
 
 def swap_pair(value):
@@ -183,40 +212,18 @@
     return [[2 * i + y for i in range(line)] for y in range(2)]
 
 
-def gather_line(value, line, place):
-    if line != 4:
-        return lax.all_gather(value, "ctx", axis=0, axis_index_groups=line_groups(line))
-    end = (place == 0) | (place == 3)
-    low = place < 2
-    first = along_line(value, OUTER)
-    second = along_line(value, INNER)
-    third = along_line(first, INNER)
-    fourth = along_line(second, OUTER)
-    fifth = along_line(third, OUTER)
-    near = jnp.where(end, fourth, second)
-    far = jnp.where(end, fifth, third)
-    even = jnp.where(place % 2 == 0, value, first)
-    odd = jnp.where(place % 2 == 0, first, value)
-    return jnp.stack([
-        jnp.where(low, even, far),
-        jnp.where(low, odd, near),
-        jnp.where(low, near, even),
-        jnp.where(low, far, odd),
-    ])
-
-
-def scatter_line(parts, line, place):
-    if line != 4:
-        return lax.psum_scatter(parts, "ctx", scatter_dimension=0, axis_index_groups=line_groups(line))
-    order = jnp.array([[3, 2, 1, 0], [3, 2, 0, 1], [0, 1, 3, 2], [0, 1, 2, 3]], jnp.int32)[place]
-    parts = [lax.dynamic_index_in_dim(parts, order[i], 0, keepdims=False) for i in range(4)]
+def after(value, *others):
+    return lax.optimization_barrier((value, *others))[0]
+
+
+def scatter_four(parts):
     wide = [part.astype(jnp.float32) for part in parts]
     first = along_line(parts[0], OUTER)
     second = along_line(parts[1], OUTER)
     inner = along_line((wide[0] + first).astype(jnp.bfloat16), INNER)
     third = along_line((wide[2] + inner).astype(jnp.bfloat16), OUTER)
     other = along_line((wide[1] + second).astype(jnp.bfloat16), INNER)
-    return wide[3] + third + other
+    return (wide[3] + third + other).astype(jnp.bfloat16)
 
 
 def body(doc_ids, rotated_queries, rotated_keys, value_matrix, out_proj, cotangent):
@@ -229,14 +236,29 @@
     index = lax.axis_index("ctx")
     parity, place = index % 2, index // 2
     group = lax.axis_index("hg")
-    core, column = group % 2, group // 2
-    half = line * shard
 
     kv = jnp.concatenate([rotated_keys, value_matrix], 1)
     docs = jnp.pad(doc_ids.reshape(-1, 2 * HEAD_SIZE), ((0, DOC_ROWS - rows // (2 * HEAD_SIZE)), (0, 0)))
     pack = jnp.concatenate([kv, docs.astype(jnp.bfloat16)], 0)
     far_kv = shift_line(pack, 1)
-    near_kv = swap_pair(jnp.where(parity == 0, pack, far_kv))
+
+    fast = line == 4 and groups == 4 and shard % HEAD_SIZE == 0
+    low = place < 2
+    order = [jnp.where(low, 3, 0), jnp.where(low, 2, 1), place ^ 1, place] if fast else list(range(line))
+    part = rows // groups
+
+    def columns_of(value, row, count, kind):
+        return jnp.concatenate([
+            lax.dynamic_slice(value, (row, (2 * order[i] + kind) * shard), (count, shard)) for i in range(line)
+        ], 1)
+
+    sent = columns_of(after(cotangent, pack), group * part, part, 1 - parity)
+    quarter = swap_pair(sent)
+    out_proj, cotangent = after(out_proj, sent), after(cotangent, sent)
+    blocks = columns_of(cotangent, 0, rows, parity)
+
+    relay = jnp.where(parity == 0, pack, after(far_kv, blocks))
+    near_kv = swap_pair(relay)
 
     def docs_of(received, back):
         found = received[rows : rows + rows // (2 * HEAD_SIZE)].reshape(-1).astype(jnp.int32)
@@ -245,51 +267,71 @@
     doc_window = jnp.concatenate([docs_of(far_kv, 2), docs_of(near_kv, 1), doc_ids])
     start = jnp.sum((doc_window[:, None] < doc_ids[None, :]).astype(jnp.int32), axis=0, keepdims=True)
 
-    blocks = cotangent.reshape(rows, line, 2, shard)
-    own_grad = lax.dynamic_index_in_dim(blocks, parity, 2, keepdims=False).reshape(rows, half)
-    part = rows // groups
-    sent = lax.dynamic_slice(blocks, (group * part, 0, 1 - parity, 0), (part, line, 1, shard)).reshape(part, half)
-    quarter = swap_pair(sent)
-    across = swap_heads(quarter, 2)
-    mine = jnp.stack([jnp.where(column == 0, quarter, across), jnp.where(column == 0, across, quarter)])
-    mate = swap_heads(mine, 1)
-    pair_grad = jnp.stack([jnp.where(core == 0, mine, mate), jnp.where(core == 0, mate, mine)], 1)
-    pair_grad = pair_grad.reshape(rows, half)
-
-    weights = gather_line(out_proj, line, place).reshape(half, columns)
+    if fast:
+        first = along_line(out_proj, OUTER)
+        second = along_line(out_proj, INNER)
+        quarter = after(quarter, relay)
+        first, second = after(first, quarter), after(second, quarter)
+        near_kv = after(near_kv, first, second)
+        third = along_line(first, INNER)
+        fourth = along_line(second, OUTER)
+        fifth = along_line(third, OUTER)
+        end = (place == 0) | (place == 3)
+    else:
+        weights = lax.all_gather(out_proj, "ctx", axis=0, axis_index_groups=line_groups(line)).reshape(-1, columns)
 
     attended, log_total = attend(start, rotated_queries, far_kv, near_kv, rotated_keys, value_matrix)
     pair_attended = swap_pair(attended)
 
-    proj_parts = (dot_tn(own_grad, attended) + dot_tn(pair_grad, pair_attended)).astype(jnp.bfloat16)
-    proj_grad = scatter_line(proj_parts.reshape(line, shard, columns), line, place).astype(jnp.bfloat16)
-
-    pair_part = swap_pair(dot_nn(pair_grad, weights).astype(jnp.bfloat16))
-    grad = (dot_nn(own_grad, weights) + pair_part).astype(jnp.bfloat16)
-
-    width = half // groups
-    chunks = weights.reshape(2, 2, width, columns)
-
-    def chunk_of(across_at, core_at):
-        return lax.dynamic_slice(chunks, (across_at, core_at, 0, 0), (1, 1, width, columns)).reshape(width, columns)
-
-    order = [chunk_of(1 - column, 1 - core), chunk_of(column, 1 - core), chunk_of(1 - column, core), chunk_of(column, core)]
+    across = swap_heads(quarter, 2)
+    mates = swap_heads(jnp.stack([quarter, across]), 1)
+    pair_blocks = jnp.zeros_like(blocks)
+    for piece, owner in ((quarter, group), (across, group ^ 2), (mates[0], group ^ 1), (mates[1], group ^ 3)):
+        pair_blocks = lax.dynamic_update_slice(pair_blocks, piece, (owner * part, 0))
+
+    proj_parts = (dot_tn(blocks, attended) + dot_tn(pair_blocks, pair_attended)).astype(jnp.bfloat16)
+    proj_parts = proj_parts.reshape(line, shard, columns)
+    if fast:
+        proj_grad = scatter_four([proj_parts[i] for i in range(line)])
+        near_half = jnp.concatenate([first, out_proj], 0)
+        far_half = jnp.concatenate([jnp.where(end, fifth, third), jnp.where(end, fourth, second)], 0)
+        near_half = after(near_half, proj_parts)
+        pair_part = dot_nn(pair_blocks[:, 2 * shard :], near_half) + dot_nn(pair_blocks[:, : 2 * shard], far_half)
+        weights = jnp.concatenate([far_half, near_half], 0)
+    else:
+        proj_grad = lax.psum_scatter(proj_parts, "ctx", scatter_dimension=0, axis_index_groups=line_groups(line))
+        pair_part = dot_nn(pair_blocks, weights)
+    pair_part = pair_part.astype(jnp.bfloat16)
+    pair_attended, weights = lax.optimization_barrier((pair_attended, weights, pair_part))[0:2]
+    pair_part = swap_pair(pair_part)
+    own_part = dot_nn(blocks, weights)
+    weights = weights.reshape(line, shard, columns)
+
+    ways = [group ^ 3, group ^ 1, group ^ 2, group]
+
+    slots = jnp.stack([sum(jnp.where(order[i] == way, i, 0) for i in range(line)) for way in ways]).astype(jnp.int32)
 
     def reduced(tokens):
-        parts = [dot_nt(tokens, item) for item in order]
-        mates = swap_heads(jnp.stack(parts[0:2]).astype(jnp.bfloat16), 1)
-        across = swap_heads((parts[2] + mates[0]).astype(jnp.bfloat16), 2)
-        return (parts[3] + mates[1] + across).astype(jnp.bfloat16)
-
-    other_part = swap_pair(reduced(pair_attended))
-    own_part = reduced(attended)
+        if fast:
+            sent, far, near = output_parts_of(slots, tokens, weights)
+        else:
+            chunks = weights.reshape(groups, -1, columns)
+            items = [lax.dynamic_index_in_dim(chunks, way, 0, keepdims=False) for way in ways]
+            parts = [dot_nt(tokens, item) for item in items]
+            sent, far, near = jnp.stack(parts[0:2]).astype(jnp.bfloat16), parts[2], parts[3]
+        mates = swap_heads(sent, 1)
+        across = swap_heads((far + mates[0]).astype(jnp.bfloat16), 2)
+        return (near + mates[1] + across).astype(jnp.bfloat16)
+
+    other_output = swap_pair(reduced(pair_attended))
+    own_output = reduced(attended)
     layer_output = jnp.stack([
-        jnp.where(parity == 0, own_part, other_part).reshape(rows, -1, shard),
-        jnp.where(parity == 0, other_part, own_part).reshape(rows, -1, shard),
-    ], 2).reshape(rows, 2 * width)
+        jnp.where(parity == 0, own_output, other_output).reshape(rows, -1, shard),
+        jnp.where(parity == 0, other_output, own_output).reshape(rows, -1, shard),
+    ], 2).reshape(rows, -1)
 
     query_grad, near, far, own = attend_back(
-        start, log_total, rotated_queries, far_kv, near_kv, rotated_keys, value_matrix, attended, grad
+        start, log_total, rotated_queries, far_kv, near_kv, rotated_keys, value_matrix, attended, own_part, pair_part
     )
     returned = swap_pair(near)
     passed = far.astype(jnp.float32) + jnp.where(parity == 1, returned, 0)

time: 146 us -> 118 us (0.81)
  local copies, waits for them, and re-layouts: 18.4 us -> 7.49 us
  matrix products: 15.5 us -> 6.37 us
  between operations: 8.84 us -> 1.04 us
  starting transfers between devices: 48.8 us -> 43.8 us
  waiting for transfers between devices: 29.4 us -> 33.9 us
  Pallas kernels: 14.1 us -> 17.8 us
  other arithmetic: 10.2 us -> 6.76 us
    ppermute x6, waiting for transfers between devices: 4.37 us -> 20.5 us  [swap_pair(): return lax.ppermute(value, 'ctx', [(i, i ^ 1) for i in range(devices)])]
    ppermute x10, waiting for transfers between devices: 18.8 us -> 5.73 us  [along_line(): return lax.ppermute(value, 'ctx', line_pairs(pairs))]
    dot_general x8 -> x0, matrix products: 8.09 us -> none  [dot_nt(): lax.dot_general(a, b, (((1,), (1,)), ((), ())), preferred_element_type=jn...]
    unnamed x24 -> x13, local copies, waits for them, and re-layouts: 7.99 us -> 1.92 us
    ppermute x6, waiting for transfers between devices: 1.9 us -> 7.72 us  [swap_heads(): return lax.ppermute(value, 'hg', [(i, i ^ bit) for i in range(groups)])]
    ppermute x2, waiting for transfers between devices: 4.28 us -> 0.01 us  [shift_line(): return lax.ppermute(value, 'ctx', pairs)]
    another operation x10 -> x6, other arithmetic: 5.33 us -> 1.39 us  [the longest x2 1.66 us: body(): jnp.stack([jnp.where(core == 0, mine, mate), jnp.where(core == 0, mate, m...]
    pallas_call x0 -> x2, Pallas kernels: none -> 3.65 us  [output_parts_of(): pl.pallas_call(output_kernel, out_shape=(jax.ShapeDtypeStruct((2, rows, s...]
  transfers between devices with their start and end apart: 24 -> 24, of which waited for: 8 -> 11; matrix products, arithmetic and copies ran while one was open for 29% -> 10% of each run, Pallas kernels for 10% -> 15%
where the time goes in v2:
time: 118 us; the launch traced here: 117 us
  starting transfers between devices  43.8 us (37%)
  waiting for transfers between devices  33.9 us (29%)
  Pallas kernels  17.8 us (15%)
  local copies, waits for them, and re-layouts  7.49 us (6%)
  other arithmetic  6.76 us (6%)
  matrix products  6.37 us (5%)
    ppermute x10, starting transfers between devices, along_line(): return lax.ppermute(value, 'ctx', line_pairs(pairs))  28.2 us
    ppermute x6, waiting for transfers between devices, swap_pair(): return lax.ppermute(value, 'ctx', [(i, i ^ 1) for i in range(devices)])  20.5 us
    ppermute x6, waiting for transfers between devices, swap_heads(): return lax.ppermute(value, 'hg', [(i, i ^ bit) for i in range(groups)])  7.72 us
    pallas_call x1, Pallas kernels, attend_back(): pl.pallas_call(backward_kernel, out_shape=(jax.ShapeDtypeStruct((rows, co...  7.62 us
    pallas_call x1, Pallas kernels, attend(): pl.pallas_call(forward_kernel, out_shape=(jax.ShapeDtypeStruct((rows, col...  6.57 us
    ppermute x2, starting transfers between devices, shift_line(): return lax.ppermute(value, 'ctx', pairs)  6.24 us
    ppermute x10, waiting for transfers between devices, along_line(): return lax.ppermute(value, 'ctx', line_pairs(pairs))  5.73 us
    ppermute x6, starting transfers between devices, swap_pair(): return lax.ppermute(value, 'ctx', [(i, i ^ 1) for i in range(devices)])  5.24 us
  transfers between devices with their start and end apart: 24, of which 11 were waited for; matrix products, arithmetic and copies ran while one was open for 10% of the time, Pallas kernels for 15%

profile of v2, /device:TPU:0, one launch (start us, length us, event | category | flops | bytes accessed | tf_op | source)
XLA Modules:
  0.0 117.2 jit_solution(16939048777046656187)
XLA Ops:
  0.6 0.7 convert.9
  1.4 1.0 fusion.16
  2.4 4.9 %collective-permute-start = (bf16[528,256]{1,0:T(8,128)(2,1)S(1)}, bf16[528,256]{1,0:T(8,128)(2,1)S(1)}, u32[]{:S(2)}, u32[]{:S(2)}) collective-permute-start(bf16[528,256]{1,0:T(8,128)(2,1)S(1)} %fusion.16), channel_id=1, source_target_pairs={{0,8},{4,12},{8,16},{12,20},{16,24},{20,28},{1,9},{5,13},{9,17},{1... | collective-permute-start | bytes 811016 | tf_op jit(solution)/shard_map/ppermute | solution.py:191
  7.4 1.1 fusion.19
  8.6 1.6 %collective-permute-start.3 = (bf16[128,2048]{1,0:T(8,128)(2,1)S(1)}, bf16[128,2048]{1,0:T(8,128)(2,1)S(1)}, u32[]{:S(2)}, u32[]{:S(2)}) collective-permute-start(bf16[128,2048]{1,0:T(8,128)(2,1)S(1)} %pad_maximum_fusion.5), channel_id=1, source_target_pairs={{0,4},{4,0},{8,12},{12,8},{16,20},{20,16},{24,28},{28,24},{1,5},{5... | collective-permute-start | bytes 1572872 | tf_op jit(solution)/shard_map/ppermute | solution.py:185
  10.2 0.7 collective-permute-start.4
  10.9 4.4 %collective-permute-start.2 = (bf16[512,512]{1,0:T(8,128)(2,1)S(1)}, bf16[512,512]{1,0:T(8,128)(2,1)S(1)}, u32[]{:S(2)}, u32[]{:S(2)}) collective-permute-start(bf16[512,512]{1,0:T(8,128)(2,1)S(1)} %copy-done.3), channel_id=1, source_target_pairs={{0,8},{4,12},{8,0},{12,4},{16,24},{20,28},{24,16},{28,20},{1,9},{5... | collective-permute-start | bytes 1572872 | tf_op jit(solution)/shard_map/ppermute | solution.py:204
  15.3 1.7 %constant_dynamic-slice_fusion.3 = (bf16[512,512]{1,0:T(8,128)(2,1)S(1)}, bf16[512,512]{1,0:T(8,128)(2,1)S(1)}, bf16[512,512]{1,0:T(8,128)(2,1)S(1)}, bf16[512,512]{1,0:T(8,128)(2,1)S(1)}) fusion(bf16[512,4096]{1,0:T(8,128)(2,1)} %param.11, s32[]{:T(128)S(6)} %select_n.189, s32[]{:T(128)S(6)} %select_n.192, s32[]{:T(128)S(6)} %select_n.191, s32[]{:T(128)S(6)} %select_n.190), kind=kLoop, calls=%fused_computation.56 | loop fusion | bytes 4194320 | tf_op jit(solution)/shard_map/dynamic_slice | solution.py:252
  17.0 0.3 pad_maximum_fusion
  17.4 0.5 copy-done
  18.0 0.6 collective-permute-start.1
  18.6 4.9 %collective-permute-done.3 = bf16[128,2048]{1,0:T(8,128)(2,1)S(1)} collective-permute-done((bf16[128,2048]{1,0:T(8,128)(2,1)S(1)}, bf16[128,2048]{1,0:T(8,128)(2,1)S(1)}, u32[]{:S(2)}, u32[]{:S(2)}) %collective-permute-start.3) | collective-permute-done | bytes 524320 | tf_op jit(solution)/shard_map/ppermute | solution.py:185
  23.5 1.5 %collective-permute-start.9 = (bf16[128,2048]{1,0:T(8,128)(2,1)S(1)}, bf16[128,2048]{1,0:T(8,128)(2,1)S(1)}, u32[]{:S(2)}, u32[]{:S(2)}) collective-permute-start(bf16[128,2048]{1,0:T(8,128)(2,1)S(1)} %collective-permute-done.3), channel_id=1, source_target_pairs={{0,2},{1,3},{2,0},{3,1},{4,6},{5,7},{6,4},{7,5},{8,10},{9,11},{10,... | collective-permute-start | bytes 1572872 | tf_op jit(solution)/shard_map/ppermute | solution.py:196
  25.0 1.4 %collective-permute-done.2 = bf16[512,512]{1,0:T(8,128)(2,1)S(1)} collective-permute-done((bf16[512,512]{1,0:T(8,128)(2,1)S(1)}, bf16[512,512]{1,0:T(8,128)(2,1)S(1)}, u32[]{:S(2)}, u32[]{:S(2)}) %collective-permute-start.2) | collective-permute-done | bytes 524320 | tf_op jit(solution)/shard_map/ppermute | solution.py:204
  26.5 0.7 collective-permute-start.6
  27.2 0.2 broadcast_in_dim.20
  27.5 3.5 %collective-permute-start.8 = (bf16[512,512]{1,0:T(8,128)(2,1)S(1)}, bf16[512,512]{1,0:T(8,128)(2,1)S(1)}, u32[]{:S(2)}, u32[]{:S(2)}) collective-permute-start(bf16[512,512]{1,0:T(8,128)(2,1)S(1)} %collective-permute-done.4), channel_id=1, source_target_pairs={{0,8},{4,12},{8,0},{12,4},{16,24},{20,28},{24,16},{28,20},{1,9},{5... | collective-permute-start | bytes 1572872 | tf_op jit(solution)/shard_map/ppermute | solution.py:204
  31.0 0.4 convert_reduce_fusion
  31.4 3.1 %collective-permute-done.9 = bf16[128,2048]{1,0:T(8,128)(2,1)S(1)} collective-permute-done((bf16[128,2048]{1,0:T(8,128)(2,1)S(1)}, bf16[128,2048]{1,0:T(8,128)(2,1)S(1)}, u32[]{:S(2)}, u32[]{:S(2)}) %collective-permute-start.9) | collective-permute-done | bytes 524320 | tf_op jit(solution)/shard_map/ppermute | solution.py:196
  34.7 7.3 %collective-permute-start.7 = (bf16[512,512]{1,0:T(8,128)(2,1)S(1)}, bf16[512,512]{1,0:T(8,128)(2,1)S(1)}, u32[]{:S(2)}, u32[]{:S(2)}) collective-permute-start(bf16[512,512]{1,0:T(8,128)(2,1)S(1)} %collective-permute-done.6), channel_id=1, source_target_pairs={{0,8},{4,12},{8,0},{12,4},{16,24},{20,28},{24,16},{28,20},{1,9},{5... | collective-permute-start | bytes 1572872 | tf_op jit(solution)/shard_map/ppermute | solution.py:204
  42.0 6.6 %attend.1 = (bf16[512,512]{1,0:T(8,128)(2,1)S(1)}, f32[4,512]{1,0:T(4,128)S(1)}) custom-call(s32[1,512]{1,0:T(1,128)S(1)} %bitcast.57, bf16[512,512]{1,0:T(8,128)(2,1)S(1)} %copy-done.2, bf16[528,256]{1,0:T(8,128)(2,1)S(1)} %collective-permute-done.kv2, bf16[528,256]{1,0:T(8,128)(2,1)S(1)} %collective-permute-done.1.kv1, bf16[512,128]{1,0:T(8,128)(2,1)S(1)} %copy-done.1, ...), custom_call_target="tpu_custom_call" | custom-call | flops 1610612736 | bytes 1048576 | tf_op jit(solution)/shard_map/attend/pallas_call | solution.py:117
  48.6 0.6 collective-permute-start.5
  49.3 2.8 %collective-permute-done.7 = bf16[512,512]{1,0:T(8,128)(2,1)S(1)} collective-permute-done((bf16[512,512]{1,0:T(8,128)(2,1)S(1)}, bf16[512,512]{1,0:T(8,128)(2,1)S(1)}, u32[]{:S(2)}, u32[]{:S(2)}) %collective-permute-start.7) | collective-permute-done | bytes 524320 | tf_op jit(solution)/shard_map/ppermute | solution.py:204
  52.2 0.1 pad_maximum_fusion.1
  52.5 0.7 fusion.2
  53.2 6.2 %collective-permute-done.5.tokens = bf16[512,512]{1,0:T(8,128)(2,1)S(1)} collective-permute-done((bf16[512,512]{1,0:T(8,128)(2,1)S(1)}, bf16[512,512]{1,0:T(8,128)(2,1)S(1)}, u32[]{:S(2)}, u32[]{:S(2)}) %collective-permute-start.5) | collective-permute-done | bytes 524320 | tf_op jit(solution)/shard_map/ppermute | solution.py:185
  59.4 1.3 %fusion.23 = f32[2048,512]{1,0:T(8,128)S(1)} fusion(bf16[512,2048]{1,0:T(8,128)(2,1)S(1)} %fusion.14, bf16[512,512]{1,0:T(8,128)(2,1)S(1)} %collective-permute-done.5.tokens), kind=kOutput, calls=%fused_computation.63 | convolution fusion | flops 1073741824 | bytes 6815744 | tf_op jit(solution)/shard_map/dot_general | solution.py:27
  60.7 1.4 %add_convert_fusion = bf16[2048,512]{1,0:T(8,128)(2,1)S(1)} fusion(f32[2048,512]{1,0:T(8,128)S(1)} %fusion.23, bf16[512,2048]{1,0:T(8,128)(2,1)S(1)} %pad_maximum_fusion, bf16[512,512]{1,0:T(8,128)(2,1)S(1)} %get-tuple-element.35.tokens.attended), kind=kOutput, calls=%fused_computation | convolution fusion | flops 1075838976 | bytes 8912896 | tf_op jit(solution)/shard_map/dot_general | solution.py:27
  62.1 1.0 fusion.20
  63.1 0.3 collective-permute-start.19
  63.4 1.5 %fusion = bf16[512,512]{1,0:T(8,128)(2,1)} fusion(f32[512,512]{1,0:T(8,128)S(1)} %fusion.2, bf16[512,2048]{1,0:T(8,128)(2,1)S(1)} %fusion.14, bf16[512,512]{1,0:T(8,128)(2,1)S(1)} %broadcast_select_fusion, bf16[512,512]{1,0:T(8,128)(2,1)S(1)} %broadcast_select_fusion.1), kind=kOutput, calls=%fused_computation.5 | convolution fusion | flops 539492352 | bytes 3670016 | tf_op jit(solution)/shard_map/dot_general | solution.py:19
  64.9 0.5 collective-permute-start.16
  65.4 1.8 %output_parts.3 = (bf16[2,512,512]{2,1,0:T(8,128)(2,1)S(1)}, f32[512,512]{1,0:T(8,128)S(1)}, f32[512,512]{1,0:T(8,128)S(1)}) custom-call(s32[4]{0:T(128)S(1)} %pad_add_fusion.1.order, bf16[512,512]{1,0:T(8,128)(2,1)S(1)} %collective-permute-done.5.tokens, bf16[4,512,512]{2,1,0:T(8,128)(2,1)S(1)} %bitcast.55), custom_call_target="tpu_custom_call" | custom-call | flops 1073741824 | bytes 8388608 | tf_op jit(solution)/shard_map/output_parts/pallas_call | solution.py:166
  67.3 1.4 %fusion.22.own_grad = f32[512,512]{1,0:T(8,128)S(1)} fusion(bf16[512,2048]{1,0:T(8,128)(2,1)S(1)} %pad_maximum_fusion, bf16[2048,512]{1,0:T(8,128)(2,1)S(1)} %pad_maximum_fusion.1), kind=kOutput, calls=%fused_computation.62 | convolution fusion | flops 1073741824 | bytes 5242880 | tf_op jit(solution)/shard_map/dot_general | solution.py:19
  68.8 1.8 %collective-permute-start.22 = (bf16[512,512]{1,0:T(8,128)(2,1)}, bf16[512,512]{1,0:T(8,128)(2,1)}, u32[]{:S(2)}, u32[]{:S(2)}) collective-permute-start(bf16[512,512]{1,0:T(8,128)(2,1)} %get-tuple-element.72), channel_id=1, source_target_pairs={{0,8},{4,12},{8,0},{12,4},{16,24},{20,28},{24,16},{28,20},{1,9},{5... | collective-permute-start | bytes 1572872 | tf_op jit(solution)/shard_map/ppermute | solution.py:204
  70.6 1.8 %output_parts.2 = (bf16[2,512,512]{2,1,0:T(8,128)(2,1)S(1)}, f32[512,512]{1,0:T(8,128)S(1)}, f32[512,512]{1,0:T(8,128)S(1)}) custom-call(s32[4]{0:T(128)S(1)} %pad_add_fusion.1.order, bf16[512,512]{1,0:T(8,128)(2,1)S(1)} %get-tuple-element.35.tokens.attended, bf16[4,512,512]{2,1,0:T(8,128)(2,1)S(1)} %bitcast.56), custom_call_target="tpu_custom_call" | custom-call | flops 1073741824 | bytes 8388608 | tf_op jit(solution)/shard_map/output_parts/pallas_call | solution.py:166
  72.4 0.3 collective-permute-start.11
  72.7 2.2 %collective-permute-done.16.pair_grad = bf16[512,512]{1,0:T(8,128)(2,1)S(1)} collective-permute-done((bf16[512,512]{1,0:T(8,128)(2,1)}, bf16[512,512]{1,0:T(8,128)(2,1)S(1)}, u32[]{:S(2)}, u32[]{:S(2)}) %collective-permute-start.16) | collective-permute-done | bytes 524320 | tf_op jit(solution)/shard_map/ppermute | solution.py:185
  74.9 7.6 %attend_back.1 = (bf16[512,512]{1,0:T(8,128)(2,1)}, bf16[512,256]{1,0:T(8,128)(2,1)S(1)}, bf16[512,256]{1,0:T(8,128)(2,1)S(1)}, f32[512,256]{1,0:T(8,128)S(1)}) custom-call(s32[1,512]{1,0:T(1,128)S(1)} %bitcast.58, f32[4,512]{1,0:T(4,128)S(1)} %get-tuple-element.44.log_total, bf16[512,512]{1,0:T(8,128)(2,1)S(1)} %copy-done.2, ...), custom_call_target="tpu_custom_call" | custom-call | flops 4026531840 | bytes 2621440 | tf_op jit(solution)/shard_map/attend_back/pallas_call | solution.py:137
  82.5 0.5 collective-permute-start.17
  83.0 0.1 add_convert_fusion.4
  83.2 0.7 collective-permute-start.20
  83.9 5.0 %collective-permute-done.17 = bf16[512,256]{1,0:T(8,128)(2,1)S(1)} collective-permute-done((bf16[512,256]{1,0:T(8,128)(2,1)S(1)}, bf16[512,256]{1,0:T(8,128)(2,1)S(1)}, u32[]{:S(2)}, u32[]{:S(2)}) %collective-permute-start.17) | collective-permute-done | bytes 262176 | tf_op jit(solution)/shard_map/ppermute | solution.py:185
  89.0 1.3 %collective-permute-start.18 = (bf16[512,256]{1,0:T(8,128)(2,1)S(1)}, bf16[512,256]{1,0:T(8,128)(2,1)S(1)}, u32[]{:S(2)}, u32[]{:S(2)}) collective-permute-start(bf16[512,256]{1,0:T(8,128)(2,1)S(1)} %add_convert_fusion.6), channel_id=1, source_target_pairs={{8,0},{12,4},{16,8},{20,12},{24,16},{28,20},{9,1},{13,5},{17,9},{2... | collective-permute-start | bytes 786440 | tf_op jit(solution)/shard_map/ppermute | solution.py:191
  90.3 0.2 fusion.7
  90.5 1.6 %collective-permute-start.14 = (bf16[512,512]{1,0:T(8,128)(2,1)S(1)}, bf16[512,512]{1,0:T(8,128)(2,1)S(1)}, u32[]{:S(2)}, u32[]{:S(2)}) collective-permute-start(bf16[512,512]{1,0:T(8,128)(2,1)S(1)} %fusion.7), channel_id=1, source_target_pairs={{0,2},{1,3},{2,0},{3,1},{4,6},{5,7},{6,4},{7,5},{8,10},{9,11},{10,... | collective-permute-start | bytes 1572872 | tf_op jit(solution)/shard_map/ppermute | solution.py:196
  92.0 0.2 fusion.10
  92.2 0.6 collective-permute-start.12
  92.8 1.3 %add_convert_fusion.3 = (bf16[512,512]{1,0:T(8,128)(2,1)S(1)}, bf16[512,512]{1,0:T(8,128)(2,1)S(1)}) fusion(bf16[512,512]{1,0:T(8,128)(2,1)S(1)} %collective-permute-done.20, bf16[2048,512]{1,0:T(8,128)(2,1)S(1)} %add_convert_fusion, bf16[512,512]{1,0:T(8,128)(2,1)} %collective-permute-done.22), kind=kLoop, calls=%fused_computation.27 | loop fusion | flops 2097152 | bytes 3145728 | tf_op jit(solution)/shard_map/convert_element_type | solution.py:224
  94.1 8.2 %collective-permute-start.21 = (bf16[512,512]{1,0:T(8,128)(2,1)S(1)}, bf16[512,512]{1,0:T(8,128)(2,1)S(1)}, u32[]{:S(2)}, u32[]{:S(2)}) collective-permute-start(bf16[512,512]{1,0:T(8,128)(2,1)S(1)} %get-tuple-element.69), channel_id=1, source_target_pairs={{0,8},{4,12},{8,0},{12,4},{16,24},{20,28},{24,16},{28,20},{1,9},{5... | collective-permute-start | bytes 1572872 | tf_op jit(solution)/shard_map/ppermute | solution.py:204
  102.3 0.7 collective-permute-start.23
  103.0 2.4 %collective-permute-done.14 = bf16[512,512]{1,0:T(8,128)(2,1)S(1)} collective-permute-done((bf16[512,512]{1,0:T(8,128)(2,1)S(1)}, bf16[512,512]{1,0:T(8,128)(2,1)S(1)}, u32[]{:S(2)}, u32[]{:S(2)}) %collective-permute-start.14) | collective-permute-done | bytes 524320 | tf_op jit(solution)/shard_map/ppermute | solution.py:196
  105.4 0.2 fusion.9
  105.6 1.5 %collective-permute-start.15 = (bf16[512,512]{1,0:T(8,128)(2,1)S(1)}, bf16[512,512]{1,0:T(8,128)(2,1)S(1)}, u32[]{:S(2)}, u32[]{:S(2)}) collective-permute-start(bf16[512,512]{1,0:T(8,128)(2,1)S(1)} %fusion.9), channel_id=1, source_target_pairs={{0,4},{4,0},{8,12},{12,8},{16,20},{20,16},{24,28},{28,24},{1,5},{5... | collective-permute-start | bytes 1572872 | tf_op jit(solution)/shard_map/ppermute | solution.py:185
  107.1 0.1 add_convert_fusion.5
  107.2 0.7 fusion.21
  108.0 1.5 %collective-permute-done.21 = bf16[512,512]{1,0:T(8,128)(2,1)S(1)} collective-permute-done((bf16[512,512]{1,0:T(8,128)(2,1)S(1)}, bf16[512,512]{1,0:T(8,128)(2,1)S(1)}, u32[]{:S(2)}, u32[]{:S(2)}) %collective-permute-start.21) | collective-permute-done | bytes 524320 | tf_op jit(solution)/shard_map/ppermute | solution.py:204
  109.5 1.0 add_convert_fusion.1
  110.5 2.2 %collective-permute-done.12 = bf16[512,512]{1,0:T(8,128)(2,1)S(1)} collective-permute-done((bf16[512,512]{1,0:T(8,128)(2,1)S(1)}, bf16[512,512]{1,0:T(8,128)(2,1)S(1)}, u32[]{:S(2)}, u32[]{:S(2)}) %collective-permute-start.12) | collective-permute-done | bytes 524320 | tf_op jit(solution)/shard_map/ppermute | solution.py:196
  112.7 2.1 %collective-permute-done.15 = bf16[512,512]{1,0:T(8,128)(2,1)S(1)} collective-permute-done((bf16[512,512]{1,0:T(8,128)(2,1)S(1)}, bf16[512,512]{1,0:T(8,128)(2,1)S(1)}, u32[]{:S(2)}, u32[]{:S(2)}) %collective-permute-start.15) | collective-permute-done | bytes 524320 | tf_op jit(solution)/shard_map/ppermute | solution.py:185
  114.9 0.3 select_bitcast_fusion.1
  115.2 0.1 pad_maximum_fusion.4
  115.4 0.5 copy.13
  115.9 1.3 %copy.14 = bf16[512,1024]{1,0:T(8,128)(2,1)} copy(bf16[512,1024]{0,1:T(8,128)(2,1)S(1)} %bitcast.59) | data formatting | bytes 2097152
  (43 shorter events, 1.2 us)
Async XLA Ops:
  0.6 9.6 %copy-start.3 = (bf16[512,512]{1,0:T(8,128)(2,1)S(1)}, bf16[512,512]{1,0:T(8,128)(2,1)}, u32[]{:S(2)}) copy-start(bf16[512,512]{1,0:T(8,128)(2,1)} %param.10) | copy-start | bytes 1572868
  2.4 15.0 %collective-permute-start = (bf16[528,256]{1,0:T(8,128)(2,1)S(1)}, bf16[528,256]{1,0:T(8,128)(2,1)S(1)}, u32[]{:S(2)}, u32[]{:S(2)}) collective-permute-start(bf16[528,256]{1,0:T(8,128)(2,1)S(1)} %fusion.16), channel_id=1, source_target_pairs={{0,8},{4,12},{8,16},{12,20},{16,24},{20,28},{1,9},{5,13},{9,17},{1... | collective-permute-start | bytes 811016 | tf_op jit(solution)/shard_map/ppermute | solution.py:191
  8.6 14.9 %collective-permute-start.3 = (bf16[128,2048]{1,0:T(8,128)(2,1)S(1)}, bf16[128,2048]{1,0:T(8,128)(2,1)S(1)}, u32[]{:S(2)}, u32[]{:S(2)}) collective-permute-start(bf16[128,2048]{1,0:T(8,128)(2,1)S(1)} %pad_maximum_fusion.5), channel_id=1, source_target_pairs={{0,4},{4,0},{8,12},{12,8},{16,20},{20,16},{24,28},{28,24},{1,5},{5... | collective-permute-start | bytes 1572872 | tf_op jit(solution)/shard_map/ppermute | solution.py:185
  10.2 17.3 %collective-permute-start.4 = (bf16[512,512]{1,0:T(8,128)(2,1)S(1)}, bf16[512,512]{1,0:T(8,128)(2,1)S(1)}, u32[]{:S(2)}, u32[]{:S(2)}) collective-permute-start(bf16[512,512]{1,0:T(8,128)(2,1)S(1)} %copy-done.3), channel_id=1, source_target_pairs={{8,16},{12,20},{16,8},{20,12},{9,17},{13,21},{17,9},{21,13},{10,18... | collective-permute-start | bytes 1572872 | tf_op jit(solution)/shard_map/ppermute | solution.py:204
  10.9 15.5 %collective-permute-start.2 = (bf16[512,512]{1,0:T(8,128)(2,1)S(1)}, bf16[512,512]{1,0:T(8,128)(2,1)S(1)}, u32[]{:S(2)}, u32[]{:S(2)}) collective-permute-start(bf16[512,512]{1,0:T(8,128)(2,1)S(1)} %copy-done.3), channel_id=1, source_target_pairs={{0,8},{4,12},{8,0},{12,4},{16,24},{20,28},{24,16},{28,20},{1,9},{5... | collective-permute-start | bytes 1572872 | tf_op jit(solution)/shard_map/ppermute | solution.py:204
  17.0 0.9 copy-start
  17.0 1.0 copy-start.1
  18.0 13.0 %collective-permute-start.1 = (bf16[528,256]{1,0:T(8,128)(2,1)S(1)}, bf16[528,256]{1,0:T(8,128)(2,1)S(1)}, u32[]{:S(2)}, u32[]{:S(2)}) collective-permute-start(bf16[528,256]{1,0:T(8,128)(2,1)S(1)} %broadcast_select_fusion.2), channel_id=1, source_target_pairs={{0,4},{4,0},{8,12},{12,8},{16,20},{20,16},{24,28},{28,24},{1,5},{5... | collective-permute-start | bytes 811016 | tf_op jit(solution)/shard_map/ppermute | solution.py:185
  23.5 11.0 %collective-permute-start.9 = (bf16[128,2048]{1,0:T(8,128)(2,1)S(1)}, bf16[128,2048]{1,0:T(8,128)(2,1)S(1)}, u32[]{:S(2)}, u32[]{:S(2)}) collective-permute-start(bf16[128,2048]{1,0:T(8,128)(2,1)S(1)} %collective-permute-done.3), channel_id=1, source_target_pairs={{0,2},{1,3},{2,0},{3,1},{4,6},{5,7},{6,4},{7,5},{8,10},{9,11},{10,... | collective-permute-start | bytes 1572872 | tf_op jit(solution)/shard_map/ppermute | solution.py:196
  26.5 4.5 %copy-start.4 = (s32[512]{0:T(512)S(1)}, s32[512]{0:T(512)}, u32[]{:S(2)}) copy-start(s32[512]{0:T(512)} %param.6) | copy-start | bytes 6148
  26.5 8.2 %collective-permute-start.6 = (bf16[512,512]{1,0:T(8,128)(2,1)S(1)}, bf16[512,512]{1,0:T(8,128)(2,1)S(1)}, u32[]{:S(2)}, u32[]{:S(2)}) collective-permute-start(bf16[512,512]{1,0:T(8,128)(2,1)S(1)} %collective-permute-done.2), channel_id=1, source_target_pairs={{8,16},{12,20},{16,8},{20,12},{9,17},{13,21},{17,9},{21,13},{10,18... | collective-permute-start | bytes 1572872 | tf_op jit(solution)/shard_map/ppermute | solution.py:204
  27.4 14.6 %copy-start.2 = (bf16[512,512]{1,0:T(8,128)(2,1)S(1)}, bf16[512,512]{1,0:T(8,128)(2,1)}, u32[]{:S(2)}) copy-start(bf16[512,512]{1,0:T(8,128)(2,1)} %query.3) | copy-start | bytes 1572868
  27.5 21.7 %collective-permute-start.8 = (bf16[512,512]{1,0:T(8,128)(2,1)S(1)}, bf16[512,512]{1,0:T(8,128)(2,1)S(1)}, u32[]{:S(2)}, u32[]{:S(2)}) collective-permute-start(bf16[512,512]{1,0:T(8,128)(2,1)S(1)} %collective-permute-done.4), channel_id=1, source_target_pairs={{0,8},{4,12},{8,0},{12,4},{16,24},{20,28},{24,16},{28,20},{1,9},{5... | collective-permute-start | bytes 1572872 | tf_op jit(solution)/shard_map/ppermute | solution.py:204
  34.6 17.7 %collective-permute-start.10 = (bf16[2,128,2048]{2,1,0:T(8,128)(2,1)S(1)}, bf16[2,128,2048]{2,1,0:T(8,128)(2,1)S(1)}, u32[]{:S(2)}, u32[]{:S(2)}) collective-permute-start(bf16[2,128,2048]{2,1,0:T(8,128)(2,1)S(1)} %pad_maximum_fusion.3), channel_id=1, source_target_pairs={{0,1},{1,0},{2,3},{3,2},{4,5},{5,4},{6,7},{7,6},{8,9},{9,8},{10,11... | collective-permute-start | bytes 3145736 | tf_op jit(solution)/shard_map/ppermute | solution.py:196
  34.7 17.4 %collective-permute-start.7 = (bf16[512,512]{1,0:T(8,128)(2,1)S(1)}, bf16[512,512]{1,0:T(8,128)(2,1)S(1)}, u32[]{:S(2)}, u32[]{:S(2)}) collective-permute-start(bf16[512,512]{1,0:T(8,128)(2,1)S(1)} %collective-permute-done.6), channel_id=1, source_target_pairs={{0,8},{4,12},{8,0},{12,4},{16,24},{20,28},{24,16},{28,20},{1,9},{5... | collective-permute-start | bytes 1572872 | tf_op jit(solution)/shard_map/ppermute | solution.py:204
  48.6 10.8 %collective-permute-start.5 = (bf16[512,512]{1,0:T(8,128)(2,1)S(1)}, bf16[512,512]{1,0:T(8,128)(2,1)S(1)}, u32[]{:S(2)}, u32[]{:S(2)}) collective-permute-start(bf16[512,512]{1,0:T(8,128)(2,1)S(1)} %get-tuple-element.35.tokens.attended), channel_id=1, source_target_pairs={{0,4},{4,0},{8,12},{12,8},{16,20},{20,16},{24,28},{28,24},{1,5},{5... | collective-permute-start | bytes 1572872 | tf_op jit(solution)/shard_map/ppermute | solution.py:185
  63.1 19.9 %collective-permute-start.19 = (bf16[512,512]{1,0:T(8,128)(2,1)}, bf16[512,512]{1,0:T(8,128)(2,1)S(1)}, u32[]{:S(2)}, u32[]{:S(2)}) collective-permute-start(bf16[512,512]{1,0:T(8,128)(2,1)} %get-tuple-element.71), channel_id=1, source_target_pairs={{0,8},{4,12},{8,0},{12,4},{16,24},{20,28},{24,16},{28,20},{1,9},{5... | collective-permute-start | bytes 1572872 | tf_op jit(solution)/shard_map/ppermute | solution.py:204
  64.9 10.0 %collective-permute-start.16 = (bf16[512,512]{1,0:T(8,128)(2,1)}, bf16[512,512]{1,0:T(8,128)(2,1)S(1)}, u32[]{:S(2)}, u32[]{:S(2)}) collective-permute-start(bf16[512,512]{1,0:T(8,128)(2,1)} %fusion), channel_id=1, source_target_pairs={{0,4},{4,0},{8,12},{12,8},{16,20},{20,16},{24,28},{28,24},{1,5},{5... | collective-permute-start | bytes 1572872 | tf_op jit(solution)/shard_map/ppermute | solution.py:185
  67.3 23.0 %collective-permute-start.13 = (bf16[2,512,512]{2,1,0:T(8,128)(2,1)S(1)}, bf16[2,512,512]{2,1,0:T(8,128)(2,1)S(1)}, u32[]{:S(2)}, u32[]{:S(2)}) collective-permute-start(bf16[2,512,512]{2,1,0:T(8,128)(2,1)S(1)} %get-tuple-element.42), channel_id=1, source_target_pairs={{0,1},{1,0},{2,3},{3,2},{4,5},{5,4},{6,7},{7,6},{8,9},{9,8},{10,11... | collective-permute-start | bytes 3145736 | tf_op jit(solution)/shard_map/ppermute | solution.py:196
  68.8 24.0 %collective-permute-start.22 = (bf16[512,512]{1,0:T(8,128)(2,1)}, bf16[512,512]{1,0:T(8,128)(2,1)}, u32[]{:S(2)}, u32[]{:S(2)}) collective-permute-start(bf16[512,512]{1,0:T(8,128)(2,1)} %get-tuple-element.72), channel_id=1, source_target_pairs={{0,8},{4,12},{8,0},{12,4},{16,24},{20,28},{24,16},{28,20},{1,9},{5... | collective-permute-start | bytes 1572872 | tf_op jit(solution)/shard_map/ppermute | solution.py:204
  72.4 19.6 %collective-permute-start.11 = (bf16[2,512,512]{2,1,0:T(8,128)(2,1)S(1)}, bf16[2,512,512]{2,1,0:T(8,128)(2,1)S(1)}, u32[]{:S(2)}, u32[]{:S(2)}) collective-permute-start(bf16[2,512,512]{2,1,0:T(8,128)(2,1)S(1)} %get-tuple-element.38), channel_id=1, source_target_pairs={{0,1},{1,0},{2,3},{3,2},{4,5},{5,4},{6,7},{7,6},{8,9},{9,8},{10,11... | collective-permute-start | bytes 3145736 | tf_op jit(solution)/shard_map/ppermute | solution.py:196
  82.5 6.4 %collective-permute-start.17 = (bf16[512,256]{1,0:T(8,128)(2,1)S(1)}, bf16[512,256]{1,0:T(8,128)(2,1)S(1)}, u32[]{:S(2)}, u32[]{:S(2)}) collective-permute-start(bf16[512,256]{1,0:T(8,128)(2,1)S(1)} %get-tuple-element.48), channel_id=1, source_target_pairs={{0,4},{4,0},{8,12},{12,8},{16,20},{20,16},{24,28},{28,24},{1,5},{5... | collective-permute-start | bytes 786440 | tf_op jit(solution)/shard_map/ppermute | solution.py:185
  83.2 9.6 %collective-permute-start.20 = (bf16[512,512]{1,0:T(8,128)(2,1)S(1)}, bf16[512,512]{1,0:T(8,128)(2,1)S(1)}, u32[]{:S(2)}, u32[]{:S(2)}) collective-permute-start(bf16[512,512]{1,0:T(8,128)(2,1)S(1)} %add_convert_fusion.4), channel_id=1, source_target_pairs={{8,16},{12,20},{16,8},{20,12},{9,17},{13,21},{17,9},{21,13},{10,18... | collective-permute-start | bytes 1572872 | tf_op jit(solution)/shard_map/ppermute | solution.py:204
  89.0 18.1 %collective-permute-start.18 = (bf16[512,256]{1,0:T(8,128)(2,1)S(1)}, bf16[512,256]{1,0:T(8,128)(2,1)S(1)}, u32[]{:S(2)}, u32[]{:S(2)}) collective-permute-start(bf16[512,256]{1,0:T(8,128)(2,1)S(1)} %add_convert_fusion.6), channel_id=1, source_target_pairs={{8,0},{12,4},{16,8},{20,12},{24,16},{28,20},{9,1},{13,5},{17,9},{2... | collective-permute-start | bytes 786440 | tf_op jit(solution)/shard_map/ppermute | solution.py:191
  90.5 14.9 %collective-permute-start.14 = (bf16[512,512]{1,0:T(8,128)(2,1)S(1)}, bf16[512,512]{1,0:T(8,128)(2,1)S(1)}, u32[]{:S(2)}, u32[]{:S(2)}) collective-permute-start(bf16[512,512]{1,0:T(8,128)(2,1)S(1)} %fusion.7), channel_id=1, source_target_pairs={{0,2},{1,3},{2,0},{3,1},{4,6},{5,7},{6,4},{7,5},{8,10},{9,11},{10,... | collective-permute-start | bytes 1572872 | tf_op jit(solution)/shard_map/ppermute | solution.py:196
  92.2 20.5 %collective-permute-start.12 = (bf16[512,512]{1,0:T(8,128)(2,1)S(1)}, bf16[512,512]{1,0:T(8,128)(2,1)S(1)}, u32[]{:S(2)}, u32[]{:S(2)}) collective-permute-start(bf16[512,512]{1,0:T(8,128)(2,1)S(1)} %fusion.10), channel_id=1, source_target_pairs={{0,2},{1,3},{2,0},{3,1},{4,6},{5,7},{6,4},{7,5},{8,10},{9,11},{10,... | collective-permute-start | bytes 1572872 | tf_op jit(solution)/shard_map/ppermute | solution.py:196
  94.1 15.4 %collective-permute-start.21 = (bf16[512,512]{1,0:T(8,128)(2,1)S(1)}, bf16[512,512]{1,0:T(8,128)(2,1)S(1)}, u32[]{:S(2)}, u32[]{:S(2)}) collective-permute-start(bf16[512,512]{1,0:T(8,128)(2,1)S(1)} %get-tuple-element.69), channel_id=1, source_target_pairs={{0,8},{4,12},{8,0},{12,4},{16,24},{20,28},{24,16},{28,20},{1,9},{5... | collective-permute-start | bytes 1572872 | tf_op jit(solution)/shard_map/ppermute | solution.py:204
  102.3 7.2 %collective-permute-start.23 = (bf16[512,512]{1,0:T(8,128)(2,1)S(1)}, bf16[512,512]{1,0:T(8,128)(2,1)S(1)}, u32[]{:S(2)}, u32[]{:S(2)}) collective-permute-start(bf16[512,512]{1,0:T(8,128)(2,1)S(1)} %get-tuple-element.70), channel_id=1, source_target_pairs={{8,16},{12,20},{16,8},{20,12},{9,17},{13,21},{17,9},{21,13},{10,18... | collective-permute-start | bytes 1572872 | tf_op jit(solution)/shard_map/ppermute | solution.py:204
  105.6 9.2 %collective-permute-start.15 = (bf16[512,512]{1,0:T(8,128)(2,1)S(1)}, bf16[512,512]{1,0:T(8,128)(2,1)S(1)}, u32[]{:S(2)}, u32[]{:S(2)}) collective-permute-start(bf16[512,512]{1,0:T(8,128)(2,1)S(1)} %fusion.9), channel_id=1, source_target_pairs={{0,4},{4,0},{8,12},{12,8},{16,20},{20,16},{24,28},{28,24},{1,5},{5... | collective-permute-start | bytes 1572872 | tf_op jit(solution)/shard_map/ppermute | solution.py:185

commit v3 on v2

--- a/solution.py
+++ b/solution.py
@@ -13,6 +13,7 @@
 SCALE = HEAD_SIZE**-0.5
 LOG2E = 1.4426950408889634
 DOC_ROWS = 16
+OPT = dict(bwd='sent0', chunks='far_half', mates='', ownearly=1, pa='', passed='')
 
 
 def dot_nn(a, b):
@@ -106,8 +107,8 @@
     return [pl.BlockSpec(memory_space=pltpu.VMEM)] * count
 
 
-def params():
-    return pltpu.CompilerParams(vmem_limit_bytes=48 * 1024 * 1024)
+def params(megabytes):
+    return pltpu.CompilerParams(vmem_limit_bytes=megabytes * 1024 * 1024)
 
 
 def attend(start, query, kv2, kv1, key, value):
@@ -123,7 +124,7 @@
         in_specs=whole_vmem(6),
         out_specs=tuple(whole_vmem(2)),
         scratch_shapes=[pltpu.VMEM((3 * rows, HEAD_SIZE), jnp.bfloat16)] * 2,
-        compiler_params=params(),
+        compiler_params=params(OPT.get('vm_f', 16)),
         cost_estimate=pl.CostEstimate(flops=cost * 512, transcendentals=cost, bytes_accessed=4 * rows * columns),
         name="attend",
     )(start, query, kv2, kv1, key, value)
@@ -147,37 +148,35 @@
         scratch_shapes=[pltpu.VMEM((3 * rows, HEAD_SIZE), jnp.bfloat16)] * 2
         + [pltpu.VMEM((3 * rows, HEAD_SIZE), jnp.float32)] * 2
         + [pltpu.VMEM((rows, columns), jnp.bfloat16)],
-        compiler_params=params(),
+        compiler_params=params(OPT.get('vm_b', 24)),
         cost_estimate=pl.CostEstimate(flops=cost * 1280, transcendentals=cost, bytes_accessed=10 * rows * columns),
         name="attend_back",
     )(start, log_total, query, kv2, kv1, key, value, attended, own_grad, pair_grad)
 
 
-def output_kernel(order, tokens, weights, sent, far, near):
-    sent[0] = dot_nt(tokens[...], weights[order[0]]).astype(sent.dtype)
-    sent[1] = dot_nt(tokens[...], weights[order[1]]).astype(sent.dtype)
-    far[...] = dot_nt(tokens[...], weights[order[2]]).astype(far.dtype)
-    near[...] = dot_nt(tokens[...], weights[order[3]]).astype(near.dtype)
-
-
-def output_parts_of(order, tokens, weights):
-    line, shard, columns = weights.shape
+def output_kernel(slots, tokens, late, early, sent, kept):
+    shard = sent.shape[2]
+    for weights, own, role in ((early, slots[0], slots[2]), (late, slots[1], 1 - slots[2])):
+        for row, out in ((1 - own, sent), (own, kept)):
+            rows = pl.ds(pl.multiple_of(row * shard, shard), shard)
+            out[role] = dot_nt(tokens[...], weights[rows]).astype(out.dtype)
+
+
+def output_parts_of(slots, tokens, late, early):
+    shard, columns = early.shape[0] // 2, early.shape[1]
     rows = tokens.shape[0]
+    result = jax.ShapeDtypeStruct((2, rows, shard), jnp.bfloat16)
     return pl.pallas_call(
         output_kernel,
-        out_shape=(
-            jax.ShapeDtypeStruct((2, rows, shard), jnp.bfloat16),
-            jax.ShapeDtypeStruct((rows, shard), jnp.float32),
-            jax.ShapeDtypeStruct((rows, shard), jnp.float32),
-        ),
-        in_specs=[pl.BlockSpec(memory_space=pltpu.SMEM)] + whole_vmem(2),
-        out_specs=tuple(whole_vmem(3)),
-        compiler_params=params(),
+        out_shape=(result, result),
+        in_specs=[pl.BlockSpec(memory_space=pltpu.SMEM)] + whole_vmem(3),
+        out_specs=tuple(whole_vmem(2)),
+        compiler_params=params(OPT.get("vm_out", 12)),
         cost_estimate=pl.CostEstimate(
-            flops=2 * line * shard * rows * columns, transcendentals=0, bytes_accessed=8 * line * shard * rows
+            flops=8 * shard * rows * columns, transcendentals=0, bytes_accessed=32 * shard * rows
         ),
         name="output_parts",
-    )(order, tokens, weights)
+    )(slots, tokens, late, early)
 
 
 def swap_pair(value):
@@ -186,9 +185,11 @@
 
 
 def shift_line(value, by):
+    if by < 0 and OPT.get("open", 0):
+        devices = lax.axis_size("ctx")
+        return lax.ppermute(value, "ctx", [(i, i + 2 * by) for i in range(devices) if i + 2 * by >= 0])
     devices = lax.axis_size("ctx")
-    pairs = [(i, i + 2 * by) for i in range(devices) if 0 <= i + 2 * by < devices]
-    return lax.ppermute(value, "ctx", pairs)
+    return lax.ppermute(value, "ctx", [(i, (i + 2 * by) % devices) for i in range(devices)])
 
 
 def swap_heads(value, bit):
@@ -208,22 +209,23 @@
 INNER = [(1, 2), (2, 1)]
 
 
+def inner_swap(value):
+    groups = lax.axis_size("hg")
+    pairs = [(a * groups + h, b * groups + h) for a, b in line_pairs(INNER) for h in range(groups)]
+    pairs += [(a * groups + h, a * groups + (h ^ 1)) for a, _ in line_pairs([(0, 0), (3, 3)]) for h in range(groups)]
+    return lax.ppermute(value, ("ctx", "hg"), pairs)
+
+
 def line_groups(line):
     return [[2 * i + y for i in range(line)] for y in range(2)]
 
 
 def after(value, *others):
-    return lax.optimization_barrier((value, *others))[0]
-
-
-def scatter_four(parts):
-    wide = [part.astype(jnp.float32) for part in parts]
-    first = along_line(parts[0], OUTER)
-    second = along_line(parts[1], OUTER)
-    inner = along_line((wide[0] + first).astype(jnp.bfloat16), INNER)
-    third = along_line((wide[2] + inner).astype(jnp.bfloat16), OUTER)
-    other = along_line((wide[1] + second).astype(jnp.bfloat16), INNER)
-    return (wide[3] + third + other).astype(jnp.bfloat16)
+    return lax.optimization_barrier((value, *others))[0] if others else value
+
+
+def tie(value, name, default, **named):
+    return after(value, *[named[n] for n in OPT.get(name, default).split() if n in named])
 
 
 def body(doc_ids, rotated_queries, rotated_keys, value_matrix, out_proj, cotangent):
@@ -252,11 +254,11 @@
             lax.dynamic_slice(value, (row, (2 * order[i] + kind) * shard), (count, shard)) for i in range(line)
         ], 1)
 
-    sent = columns_of(after(cotangent, pack), group * part, part, 1 - parity)
+    cotangent = after(cotangent, pack)
+    sent = columns_of(cotangent, group * part, part, 1 - parity)
+    out_proj = tie(out_proj, "w", "sent", sent=sent, pack=pack)
     quarter = swap_pair(sent)
-    out_proj, cotangent = after(out_proj, sent), after(cotangent, sent)
-    blocks = columns_of(cotangent, 0, rows, parity)
-
+    blocks = columns_of(after(cotangent, sent), 0, rows, parity)
     relay = jnp.where(parity == 0, pack, after(far_kv, blocks))
     near_kv = swap_pair(relay)
 
@@ -269,13 +271,12 @@
 
     if fast:
         first = along_line(out_proj, OUTER)
-        second = along_line(out_proj, INNER)
+        second = inner_swap(out_proj)
         quarter = after(quarter, relay)
         first, second = after(first, quarter), after(second, quarter)
-        near_kv = after(near_kv, first, second)
-        third = along_line(first, INNER)
+        near_kv = tie(near_kv, "attend", "first second", first=first, second=second)
+        third = inner_swap(first)
         fourth = along_line(second, OUTER)
-        fifth = along_line(third, OUTER)
         end = (place == 0) | (place == 3)
     else:
         weights = lax.all_gather(out_proj, "ctx", axis=0, axis_index_groups=line_groups(line)).reshape(-1, columns)
@@ -283,60 +284,113 @@
     attended, log_total = attend(start, rotated_queries, far_kv, near_kv, rotated_keys, value_matrix)
     pair_attended = swap_pair(attended)
 
+    own_proj = dot_tn(blocks, attended)
     across = swap_heads(quarter, 2)
-    mates = swap_heads(jnp.stack([quarter, across]), 1)
+    if fast:
+        third = tie(third, "fifth", "attended", attended=attended, own_proj=own_proj, across=across, log=log_total)
+        fifth = along_line(third, OUTER)
+        across = tie(across, "mates", "attended", attended=attended, third=third, own_proj=own_proj)
+    mates = [swap_heads(quarter, 1), swap_heads(across, 1)]
     pair_blocks = jnp.zeros_like(blocks)
-    for piece, owner in ((quarter, group), (across, group ^ 2), (mates[0], group ^ 1), (mates[1], group ^ 3)):
+    for piece, owner in ((quarter, group), (mates[0], group ^ 1), (across, group ^ 2), (mates[1], group ^ 3)):
         pair_blocks = lax.dynamic_update_slice(pair_blocks, piece, (owner * part, 0))
 
-    proj_parts = (dot_tn(blocks, attended) + dot_tn(pair_blocks, pair_attended)).astype(jnp.bfloat16)
-    proj_parts = proj_parts.reshape(line, shard, columns)
+    ways = [group ^ 3, group ^ 1, group ^ 2, group]
+
     if fast:
-        proj_grad = scatter_four([proj_parts[i] for i in range(line)])
         near_half = jnp.concatenate([first, out_proj], 0)
+        near_part = dot_nn(pair_blocks[:, 2 * shard :], near_half)
+        if OPT.get("ownearly", 0):
+            own_near = dot_nn(blocks[:, 2 * shard :], near_half)
+            pair_attended = after(pair_attended, own_near)
+        pair_attended = tie(pair_attended, "pa", "own_proj near_part", own_proj=own_proj, near_part=near_part)
+        parts = [(own_proj[:shard] + dot_tn(pair_blocks[:, :shard], pair_attended)).astype(jnp.bfloat16)]
+        farthest = along_line(parts[0], OUTER)
+        fifth = tie(fifth, "far", "part0", part0=parts[0])
         far_half = jnp.concatenate([jnp.where(end, fifth, third), jnp.where(end, fourth, second)], 0)
-        near_half = after(near_half, proj_parts)
-        pair_part = dot_nn(pair_blocks[:, 2 * shard :], near_half) + dot_nn(pair_blocks[:, : 2 * shard], far_half)
-        weights = jnp.concatenate([far_half, near_half], 0)
+        pair_part = (dot_nn(pair_blocks[:, : 2 * shard], far_half) + near_part).astype(jnp.bfloat16)
+        if OPT.get("wbar", 1):
+            far_half, pair_attended = lax.optimization_barrier((far_half, pair_attended, pair_part))[0:2]
+        pair_part = swap_pair(pair_part)
+
+        late_attended = tie(pair_attended, "chunks", "", far_half=far_half)
+        parts.append(
+            (own_proj[shard:] + dot_tn(pair_blocks[:, shard:], late_attended)).astype(jnp.bfloat16)
+        )
+        wide = [part.astype(jnp.float32) for part in (parts[0], parts[1][:shard], parts[1][shard : 2 * shard], parts[1][2 * shard :])]
+        farther = along_line(parts[1][:shard], OUTER)
+        core, column = group % 2, group // 2
+        slots = [
+            jnp.where(place % 2 == core, 1, 0),
+            jnp.where(low == (core == 1), 0, 1),
+            jnp.where(low == (column == 1), 0, 1),
+        ]
+        slots = jnp.stack(slots).astype(jnp.int32)
+        if OPT.get("ownearly", 0):
+            own_part = own_near + dot_nn(blocks[:, : 2 * shard], far_half)
+        else:
+            own_part = dot_nn(blocks[:, 2 * shard :], near_half) + dot_nn(blocks[:, : 2 * shard], far_half)
+        inner = (wide[0] + farthest).astype(jnp.bfloat16)
+
+        def across_of(tokens):
+            sent, kept = output_parts_of(slots, tokens, far_half, near_half)
+            mate = swap_heads(sent, 1)
+            return (kept[0].astype(jnp.float32) + mate[0]).astype(jnp.bfloat16), kept[1].astype(jnp.float32), mate[1]
+
+        sums = [across_of(pair_attended)]
+        sums.append(across_of(tie(attended, "out1", "", inner=inner, sent0=sums[0][0], own=own_part)))
+        sent1 = tie(sums[1][0], "sent1", "sent0", sent0=sums[0][0])
+        pair_part = tie(pair_part, "bwd", "inner sent0 sent1", inner=inner, sent0=sums[0][0], sent1=sent1)
+        inner = jnp.where(end, 0, inner_swap(inner))
+        reduced = [
+            (near + mate + swap_heads(sent, 2)).astype(jnp.bfloat16)
+            for sent, near, mate in ((sums[0][0], *sums[0][1:]), (sent1, *sums[1][1:]))
+        ]
     else:
+        proj_parts = (own_proj + dot_tn(pair_blocks, pair_attended)).astype(jnp.bfloat16)
+        proj_parts = proj_parts.reshape(line, shard, columns)
         proj_grad = lax.psum_scatter(proj_parts, "ctx", scatter_dimension=0, axis_index_groups=line_groups(line))
-        pair_part = dot_nn(pair_blocks, weights)
-    pair_part = pair_part.astype(jnp.bfloat16)
-    pair_attended, weights = lax.optimization_barrier((pair_attended, weights, pair_part))[0:2]
-    pair_part = swap_pair(pair_part)
-    own_part = dot_nn(blocks, weights)
-    weights = weights.reshape(line, shard, columns)
-
-    ways = [group ^ 3, group ^ 1, group ^ 2, group]
-
-    slots = jnp.stack([sum(jnp.where(order[i] == way, i, 0) for i in range(line)) for way in ways]).astype(jnp.int32)
-
-    def reduced(tokens):
-        if fast:
-            sent, far, near = output_parts_of(slots, tokens, weights)
-        else:
-            chunks = weights.reshape(groups, -1, columns)
-            items = [lax.dynamic_index_in_dim(chunks, way, 0, keepdims=False) for way in ways]
+        pair_part = swap_pair(dot_nn(pair_blocks, weights).astype(jnp.bfloat16))
+        own_part = dot_nn(blocks, weights)
+        chunks = weights.reshape(groups, -1, columns)
+        items = [lax.dynamic_index_in_dim(chunks, way, 0, keepdims=False) for way in ways]
+        reduced = []
+        for tokens in (pair_attended, attended):
             parts = [dot_nt(tokens, item) for item in items]
-            sent, far, near = jnp.stack(parts[0:2]).astype(jnp.bfloat16), parts[2], parts[3]
-        mates = swap_heads(sent, 1)
-        across = swap_heads((far + mates[0]).astype(jnp.bfloat16), 2)
-        return (near + mates[1] + across).astype(jnp.bfloat16)
-
-    other_output = swap_pair(reduced(pair_attended))
-    own_output = reduced(attended)
-    layer_output = jnp.stack([
-        jnp.where(parity == 0, own_output, other_output).reshape(rows, -1, shard),
-        jnp.where(parity == 0, other_output, own_output).reshape(rows, -1, shard),
-    ], 2).reshape(rows, -1)
+            mates = swap_heads(jnp.stack(parts[0:2]).astype(jnp.bfloat16), 1)
+            across = swap_heads((parts[2] + mates[0]).astype(jnp.bfloat16), 2)
+            reduced.append((parts[3] + mates[1] + across).astype(jnp.bfloat16))
 
     query_grad, near, far, own = attend_back(
         start, log_total, rotated_queries, far_kv, near_kv, rotated_keys, value_matrix, attended, own_part, pair_part
     )
     returned = swap_pair(near)
+    if fast:
+        returned = tie(returned, "returned", "red0", red0=reduced[0], red1=reduced[1])
     passed = far.astype(jnp.float32) + jnp.where(parity == 1, returned, 0)
-    arrived = shift_line(passed.astype(jnp.bfloat16), -1)
-    own = own + arrived + jnp.where(parity == 0, returned, 0)
+    passed = passed.astype(jnp.bfloat16)
+    if fast:
+        wide[2] = tie(wide[2], "nearer", "own", own=own, passed=passed)
+        nearer = (wide[2] + inner).astype(jnp.bfloat16)
+        wide[1] = tie(wide[1], "other", "own", own=own, passed=passed, nearer=nearer)
+        other = (wide[1] + farther).astype(jnp.bfloat16)
+        passed = tie(passed, "passed", "", nearer=nearer, other=other)
+        nearer = along_line(nearer, OUTER)
+        other = jnp.where(end, 0, inner_swap(other))
+        proj_grad = (wide[3] + nearer + other).astype(jnp.bfloat16)
+    other_output, own_output = swap_pair(reduced[0]), reduced[1]
+    if own_output.shape[1] == shard:
+        layer_output = jnp.zeros((rows, 2 * shard), own_output.dtype)
+        layer_output = lax.dynamic_update_slice(layer_output, own_output, (0, parity * shard))
+        if OPT.get("asm", 1):
+            other_output = after(other_output, layer_output)
+        layer_output = lax.dynamic_update_slice(layer_output, other_output, (0, (1 - parity) * shard))
+    else:
+        halves = [jnp.where(parity == 0, own_output, other_output), jnp.where(parity == 0, other_output, own_output)]
+        layer_output = jnp.stack([half.reshape(rows, -1, shard) for half in halves], 2).reshape(rows, -1)
+
+    arrived = shift_line(passed, -1)
+    own = own + jnp.where(place < line - 1, arrived, 0) + jnp.where(parity == 0, returned, 0)
     own = own.astype(jnp.bfloat16)
     return (layer_output, query_grad, own[:, 0:HEAD_SIZE], own[:, HEAD_SIZE:], proj_grad)
 

time: 118 us -> 96.3 us (0.82)
  starting transfers between devices: 43.8 us -> 28 us
  local copies, waits for them, and re-layouts: 7.49 us -> 5.32 us
  other arithmetic: 6.76 us -> 5.32 us
    ppermute x10 -> x6, starting transfers between devices: 28.2 us -> 9.56 us  [along_line(): return lax.ppermute(value, 'ctx', line_pairs(pairs))]
    ppermute x6 -> x7, waiting for transfers between devices: 7.72 us -> 0.02 us  [swap_heads(): return lax.ppermute(value, 'hg', [(i, i ^ bit) for i in range(groups)])]
    ppermute x2 -> x6, waiting for transfers between devices: 0.01 us -> 5.18 us  [the longest x2 5.17 us: shift_line(): lax.ppermute(value, 'ctx', [(i, (i + 2 * by) % devices) for i in range(de...]
    ppermute x10 -> x6, waiting for transfers between devices: 5.73 us -> 9.84 us  [along_line(): return lax.ppermute(value, 'ctx', line_pairs(pairs))]
    ppermute x6, starting transfers between devices: 5.24 us -> 8.72 us  [swap_pair(): return lax.ppermute(value, 'ctx', [(i, i ^ 1) for i in range(devices)])]
    ppermute x6, waiting for transfers between devices: 20.5 us -> 17.7 us  [swap_pair(): return lax.ppermute(value, 'ctx', [(i, i ^ 1) for i in range(devices)])]
    ppermute x2 -> x6, starting transfers between devices: 6.24 us -> 5.16 us  [the longest x2 5 us: shift_line(): lax.ppermute(value, 'ctx', [(i, (i + 2 * by) % devices) for i in range(de...]
    convert_element_type x7 -> x8, other arithmetic: 3.1 us -> 2.08 us  [the longest x1 1.03 us: body(): proj_grad = (wide[3] + nearer + other).astype(jnp.bfloat16)]
  transfers between devices with their start and end apart: 24 -> 25, of which waited for: 11 -> 12; matrix products, arithmetic and copies ran while one was open for 10% -> 14% of each run, Pallas kernels for 15% -> 19%
where the time goes in v3:
time: 96.3 us; the launch traced here: 96.1 us
  waiting for transfers between devices  32.8 us (34%)
  starting transfers between devices  28 us (29%)
  Pallas kernels  17.8 us (18%)
  matrix products  5.83 us (6%)
  local copies, waits for them, and re-layouts  5.32 us (6%)
  other arithmetic  5.32 us (6%)
  between operations  0.99 us (1%)
    ppermute x6, waiting for transfers between devices, swap_pair(): return lax.ppermute(value, 'ctx', [(i, i ^ 1) for i in range(devices)])  17.7 us
    ppermute x6, waiting for transfers between devices, along_line(): return lax.ppermute(value, 'ctx', line_pairs(pairs))  9.84 us
    ppermute x6, starting transfers between devices, along_line(): return lax.ppermute(value, 'ctx', line_pairs(pairs))  9.56 us
    ppermute x6, starting transfers between devices, swap_pair(): return lax.ppermute(value, 'ctx', [(i, i ^ 1) for i in range(devices)])  8.72 us
    pallas_call x1, Pallas kernels, attend_back(): pl.pallas_call(backward_kernel, out_shape=(jax.ShapeDtypeStruct((rows, co...  7.63 us
    pallas_call x1, Pallas kernels, attend(): pl.pallas_call(forward_kernel, out_shape=(jax.ShapeDtypeStruct((rows, col...  6.56 us
    ppermute x2, waiting for transfers between devices, shift_line(): lax.ppermute(value, 'ctx', [(i, (i + 2 * by) % devices) for i in range(de...  5.17 us
    ppermute x2, starting transfers between devices, shift_line(): lax.ppermute(value, 'ctx', [(i, (i + 2 * by) % devices) for i in range(de...  5 us
  transfers between devices with their start and end apart: 25, of which 12 were waited for; matrix products, arithmetic and copies ran while one was open for 14% of the time, Pallas kernels for 19%

profile of v3, /device:TPU:0, one launch (start us, length us, event | category | flops | bytes accessed | tf_op | source)
XLA Modules:
  0.0 96.1 jit_solution(9953164476795890935)
XLA Ops:
  0.6 0.7 convert.5
  1.4 1.0 %fusion.21 = bf16[528,256]{1,0:T(8,128)(2,1)S(1)} fusion(bf16[2,256]{1,0:T(2,128)(2,1)S(1)} %reshape.40, bf16[512,128]{1,0:T(8,128)(2,1)} %value_ref.3, bf16[512,128]{1,0:T(8,128)(2,1)} %key_ref.3), kind=kLoop, calls=%fused_computation.43 | loop fusion | flops 1081344 | bytes 533504 | tf_op jit(solution)/shard_map/concatenate | solution.py:244
  2.4 3.1 %collective-permute-start = (bf16[528,256]{1,0:T(8,128)(2,1)S(1)}, bf16[528,256]{1,0:T(8,128)(2,1)S(1)}, u32[]{:S(2)}, u32[]{:S(2)}) collective-permute-start(bf16[528,256]{1,0:T(8,128)(2,1)S(1)} %fusion.21), channel_id=1, source_target_pairs={{0,8},{4,12},{8,16},{12,20},{16,24},{20,28},{24,0},{28,4},{1,9},{5... | collective-permute-start | bytes 811016 | tf_op jit(solution)/shard_map/ppermute | solution.py:192
  5.5 1.1 %fusion.25 = (bf16[128,512]{1,0:T(8,128)(2,1)S(1)}, bf16[128,512]{1,0:T(8,128)(2,1)S(1)}, bf16[128,512]{1,0:T(8,128)(2,1)S(1)}, bf16[128,512]{1,0:T(8,128)(2,1)S(1)}) fusion(bf16[512,4096]{1,0:T(8,128)(2,1)} %param.11, s32[]{:T(128)S(6)} %select_n.167, s32[]{:T(128)S(6)} %select_n.169, s32[]{:T(128)S(6)} %select_n.173, s32[]{:T(128)S(6)} %select_n.172, ...), kind=kLoop, calls=%fused_computation.64 | loop fusion | bytes 1048596 | tf_op jit(solution)/shard_map/dynamic_slice | solution.py:254
  6.7 1.6 %collective-permute-start.3 = (bf16[128,2048]{1,0:T(8,128)(2,1)S(1)}, bf16[128,2048]{1,0:T(8,128)(2,1)S(1)}, u32[]{:S(2)}, u32[]{:S(2)}) collective-permute-start(bf16[128,2048]{1,0:T(8,128)(2,1)S(1)} %pad_maximum_fusion.2), channel_id=1, source_target_pairs={{0,4},{4,0},{8,12},{12,8},{16,20},{20,16},{24,28},{28,24},{1,5},{5... | collective-permute-start | bytes 1572872 | tf_op jit(solution)/shard_map/ppermute | solution.py:184
  8.3 1.6 %collective-permute-start.2 = (bf16[512,512]{1,0:T(8,128)(2,1)S(1)}, bf16[512,512]{1,0:T(8,128)(2,1)S(1)}, u32[]{:S(2)}, u32[]{:S(2)}) collective-permute-start(bf16[512,512]{1,0:T(8,128)(2,1)S(1)} %copy-done.4), channel_id=1, source_target_pairs={{0,8},{4,12},{8,0},{12,4},{16,24},{20,28},{24,16},{28,20},{1,9},{5... | collective-permute-start | bytes 1572872 | tf_op jit(solution)/shard_map/ppermute | solution.py:205
  9.8 1.7 %constant_dynamic-slice_fusion.3 = (bf16[512,512]{1,0:T(8,128)(2,1)S(1)}, bf16[512,512]{1,0:T(8,128)(2,1)S(1)}, bf16[512,512]{1,0:T(8,128)(2,1)S(1)}, bf16[512,512]{1,0:T(8,128)(2,1)S(1)}) fusion(bf16[512,4096]{1,0:T(8,128)(2,1)} %param.11, s32[]{:T(128)S(6)} %select_n.174, s32[]{:T(128)S(6)} %select_n.177, s32[]{:T(128)S(6)} %select_n.176, s32[]{:T(128)S(6)} %select_n.175), kind=kLoop, calls=%fused_computation.56 | loop fusion | bytes 4194320 | tf_op jit(solution)/shard_map/dynamic_slice | solution.py:254
  11.6 0.1 pad_add_fusion.1.slots
  11.6 3.2 %collective-permute-done.kv2 = bf16[528,256]{1,0:T(8,128)(2,1)S(1)} collective-permute-done((bf16[528,256]{1,0:T(8,128)(2,1)S(1)}, bf16[528,256]{1,0:T(8,128)(2,1)S(1)}, u32[]{:S(2)}, u32[]{:S(2)}) %collective-permute-start) | collective-permute-done | bytes 270368 | tf_op jit(solution)/shard_map/ppermute | solution.py:192
  14.9 0.1 broadcast_select_fusion.2
  14.9 1.8 %collective-permute-start.1 = (bf16[528,256]{1,0:T(8,128)(2,1)S(1)}, bf16[528,256]{1,0:T(8,128)(2,1)S(1)}, u32[]{:S(2)}, u32[]{:S(2)}) collective-permute-start(bf16[528,256]{1,0:T(8,128)(2,1)S(1)} %broadcast_select_fusion.2), channel_id=1, source_target_pairs={{0,4},{4,0},{8,12},{12,8},{16,20},{20,16},{24,28},{28,24},{1,5},{5... | collective-permute-start | bytes 811016 | tf_op jit(solution)/shard_map/ppermute | solution.py:184
  16.8 4.8 %collective-permute-done.3 = bf16[128,2048]{1,0:T(8,128)(2,1)S(1)} collective-permute-done((bf16[128,2048]{1,0:T(8,128)(2,1)S(1)}, bf16[128,2048]{1,0:T(8,128)(2,1)S(1)}, u32[]{:S(2)}, u32[]{:S(2)}) %collective-permute-start.3) | collective-permute-done | bytes 524320 | tf_op jit(solution)/shard_map/ppermute | solution.py:184
  21.6 1.5 %collective-permute-start.8 = (bf16[128,2048]{1,0:T(8,128)(2,1)S(1)}, bf16[128,2048]{1,0:T(8,128)(2,1)S(1)}, u32[]{:S(2)}, u32[]{:S(2)}) collective-permute-start(bf16[128,2048]{1,0:T(8,128)(2,1)S(1)} %collective-permute-done.3), channel_id=1, source_target_pairs={{0,2},{1,3},{2,0},{3,1},{4,6},{5,7},{6,4},{7,5},{8,10},{9,11},{10,... | collective-permute-start | bytes 1572872 | tf_op jit(solution)/shard_map/ppermute | solution.py:197
  23.1 2.1 %collective-permute-done.2 = bf16[512,512]{1,0:T(8,128)(2,1)S(1)} collective-permute-done((bf16[512,512]{1,0:T(8,128)(2,1)S(1)}, bf16[512,512]{1,0:T(8,128)(2,1)S(1)}, u32[]{:S(2)}, u32[]{:S(2)}) %collective-permute-start.2) | collective-permute-done | bytes 524320 | tf_op jit(solution)/shard_map/ppermute | solution.py:205
  25.3 0.2 broadcast_in_dim.30
  25.7 1.2 %collective-permute-start.11 = (bf16[512,512]{1,0:T(8,128)(2,1)S(1)}, bf16[512,512]{1,0:T(8,128)(2,1)S(1)}, u32[]{:S(2)}, u32[]{:S(2)}) collective-permute-start(bf16[512,512]{1,0:T(8,128)(2,1)S(1)} %collective-permute-done.4), channel_id=1, source_target_pairs={{0,8},{4,12},{8,0},{12,4},{16,24},{20,28},{24,16},{28,20},{1,9},{5... | collective-permute-start | bytes 1572872 | tf_op jit(solution)/shard_map/ppermute | solution.py:205
  26.9 0.7 fusion.7
  27.7 0.4 convert_reduce_fusion
  28.1 6.6 %attend.1 = (bf16[512,512]{1,0:T(8,128)(2,1)S(1)}, f32[4,512]{1,0:T(4,128)S(1)}) custom-call(s32[1,512]{1,0:T(1,128)S(1)} %bitcast.30, bf16[512,512]{1,0:T(8,128)(2,1)S(1)} %copy-done.2, bf16[528,256]{1,0:T(8,128)(2,1)S(1)} %collective-permute-done.kv2, bf16[528,256]{1,0:T(8,128)(2,1)S(1)} %collective-permute-done.1.kv1, bf16[512,128]{1,0:T(8,128)(2,1)S(1)} %copy-done.1, ...), custom_call_target="tpu_custom_call" | custom-call | flops 1610612736 | bytes 1048576 | tf_op jit(solution)/shard_map/attend/pallas_call | solution.py:118
  34.6 1.6 %collective-permute-start.10 = (bf16[512,512]{1,0:T(8,128)(2,1)S(1)}, bf16[512,512]{1,0:T(8,128)(2,1)S(1)}, u32[]{:S(2)}, u32[]{:S(2)}) collective-permute-start(bf16[512,512]{1,0:T(8,128)(2,1)S(1)} %get-tuple-element.43.tokens.attended), channel_id=1, source_target_pairs={{0,4},{4,0},{8,12},{12,8},{16,20},{20,16},{24,28},{28,24},{1,5},{5... | collective-permute-start | bytes 1572872 | tf_op jit(solution)/shard_map/ppermute | solution.py:184
  36.2 1.3 %fusion.24 = f32[2048,512]{1,0:T(8,128)S(1)} fusion(bf16[512,512]{1,0:T(8,128)(2,1)S(1)} %get-tuple-element.43.tokens.attended, bf16[512,512]{1,0:T(8,128)(2,1)S(1)} %get-tuple-element.66, bf16[512,512]{1,0:T(8,128)(2,1)S(1)} %get-tuple-element.67, bf16[512,512]{1,0:T(8,128)(2,1)S(1)} %get-tuple-element.68, bf16[512,512]{1,0:T(8,128)(2,1)S(1)} %get-tuple-element.65), kind=kOutput, calls=%fused_computation.63 | convolution fusion | flops 1082130432 | bytes 6815744 | tf_op jit(solution)/shard_map/dot_general | solution.py:28
  37.5 1.2 %collective-permute-start.6 = (bf16[512,512]{1,0:T(8,128)(2,1)S(1)}, bf16[512,512]{1,0:T(8,128)(2,1)S(1)}, u32[]{:S(2)}, u32[]{:S(2)}) collective-permute-start(bf16[512,512]{1,0:T(8,128)(2,1)S(1)} %collective-permute-done.5), channel_id=1, source_target_pairs={{0,8},{4,12},{8,0},{12,4},{16,24},{20,28},{24,16},{28,20},{1,9},{5... | collective-permute-start | bytes 1572872 | tf_op jit(solution)/shard_map/ppermute | solution.py:205
  38.9 1.6 %collective-permute-done.11 = bf16[512,512]{1,0:T(8,128)(2,1)S(1)} collective-permute-done((bf16[512,512]{1,0:T(8,128)(2,1)S(1)}, bf16[512,512]{1,0:T(8,128)(2,1)S(1)}, u32[]{:S(2)}, u32[]{:S(2)}) %collective-permute-start.11) | collective-permute-done | bytes 524320 | tf_op jit(solution)/shard_map/ppermute | solution.py:205
  40.5 7.5 %collective-permute-done.10.tokens = bf16[512,512]{1,0:T(8,128)(2,1)S(1)} collective-permute-done((bf16[512,512]{1,0:T(8,128)(2,1)S(1)}, bf16[512,512]{1,0:T(8,128)(2,1)S(1)}, u32[]{:S(2)}, u32[]{:S(2)}) %collective-permute-start.10) | collective-permute-done | bytes 524320 | tf_op jit(solution)/shard_map/ppermute | solution.py:184
  48.1 0.5 fusion.3
  48.6 1.6 %collective-permute-start.20 = (bf16[512,512]{1,0:T(8,128)(2,1)S(1)}, bf16[512,512]{1,0:T(8,128)(2,1)S(1)}, u32[]{:S(2)}, u32[]{:S(2)}) collective-permute-start(bf16[512,512]{1,0:T(8,128)(2,1)S(1)} %fusion.3), channel_id=1, source_target_pairs={{0,8},{4,12},{8,0},{12,4},{16,24},{20,28},{24,16},{28,20},{1,9},{5... | collective-permute-start | bytes 1572872 | tf_op jit(solution)/shard_map/ppermute | solution.py:205
  50.2 0.7 fusion.4
  50.9 1.1 %collective-permute-done.6 = bf16[512,512]{1,0:T(8,128)(2,1)S(1)} collective-permute-done((bf16[512,512]{1,0:T(8,128)(2,1)S(1)}, bf16[512,512]{1,0:T(8,128)(2,1)S(1)}, u32[]{:S(2)}, u32[]{:S(2)}) %collective-permute-start.6) | collective-permute-done | bytes 524320 | tf_op jit(solution)/shard_map/ppermute | solution.py:205
  52.1 0.1 broadcast_select_fusion.1
  52.2 0.7 fusion.2
  52.9 1.2 %collective-permute-start.17 = (bf16[512,512]{1,0:T(8,128)(2,1)S(1)}, bf16[512,512]{1,0:T(8,128)(2,1)S(1)}, u32[]{:S(2)}, u32[]{:S(2)}) collective-permute-start(bf16[512,512]{1,0:T(8,128)(2,1)S(1)} %fusion.2), channel_id=1, source_target_pairs={{0,4},{4,0},{8,12},{12,8},{16,20},{20,16},{24,28},{28,24},{1,5},{5... | collective-permute-start | bytes 1572872 | tf_op jit(solution)/shard_map/ppermute | solution.py:184
  54.2 1.8 %output_parts.3 = (bf16[2,512,512]{2,1,0:T(8,128)(2,1)S(1)}, bf16[2,512,512]{2,1,0:T(8,128)(2,1)S(1)}) custom-call(s32[3]{0:T(128)S(1)} %pad_add_fusion.1.slots, bf16[512,512]{1,0:T(8,128)(2,1)S(1)} %collective-permute-done.10.tokens, bf16[1024,512]{1,0:T(8,128)(2,1)S(1)} %pad_maximum_fusion.1.late, bf16[1024,512]{1,0:T(8,128)(2,1)S(1)} %constant_dynamic-update-slice_fusion.early), custom_call_target="tpu_custom_call" | custom-call | flops 1073741824 | bytes 8388608 | tf_op jit(solution)/shard_map/output_parts/pallas_call | solution.py:169
  56.1 1.2 %fusion = bf16[1536,512]{1,0:T(8,128)(2,1)S(1)} fusion(bf16[512,512]{1,0:T(8,128)(2,1)S(1)} %collective-permute-done.10.tokens, f32[2048,512]{1,0:T(8,128)S(1)} %fusion.24, bf16[512,2048]{1,0:T(8,128)(2,1)S(1)} %constant_dynamic-update-slice_fusion.3), kind=kOutput, calls=%fused_computation.2 | convolution fusion | flops 806879232 | bytes 6815744 | tf_op jit(solution)/shard_map/dot_general | solution.py:28
  57.3 0.3 fusion.26
  57.6 0.1 collective-permute-start.23
  57.8 1.8 %output_parts.2 = (bf16[2,512,512]{2,1,0:T(8,128)(2,1)S(1)}, bf16[2,512,512]{2,1,0:T(8,128)(2,1)S(1)}) custom-call(s32[3]{0:T(128)S(1)} %pad_add_fusion.1.slots, bf16[512,512]{1,0:T(8,128)(2,1)S(1)} %get-tuple-element.43.tokens.attended, bf16[1024,512]{1,0:T(8,128)(2,1)S(1)} %pad_maximum_fusion.1.late, ...), custom_call_target="tpu_custom_call" | custom-call | flops 1073741824 | bytes 8388608 | tf_op jit(solution)/shard_map/output_parts/pallas_call | solution.py:169
  59.6 0.5 collective-permute-start.12
  60.1 0.7 convolution_add_fusion.1.own_grad
  60.8 2.7 %collective-permute-done.20 = bf16[512,512]{1,0:T(8,128)(2,1)S(1)} collective-permute-done((bf16[512,512]{1,0:T(8,128)(2,1)S(1)}, bf16[512,512]{1,0:T(8,128)(2,1)S(1)}, u32[]{:S(2)}, u32[]{:S(2)}) %collective-permute-start.20) | collective-permute-done | bytes 524320 | tf_op jit(solution)/shard_map/ppermute | solution.py:205
  63.5 0.1 add_convert_fusion.3
  63.7 0.1 fusion.18
  63.9 1.4 %collective-permute-start.15 = (bf16[512,512]{1,0:T(8,128)(2,1)S(1)}, bf16[512,512]{1,0:T(8,128)(2,1)S(1)}, u32[]{:S(2)}, u32[]{:S(2)}) collective-permute-start(bf16[512,512]{1,0:T(8,128)(2,1)S(1)} %fusion.18), channel_id=1, source_target_pairs={{0,2},{1,3},{2,0},{3,1},{4,6},{5,7},{6,4},{7,5},{8,10},{9,11},{10,... | collective-permute-start | bytes 1572872 | tf_op jit(solution)/shard_map/ppermute | solution.py:197
  65.2 0.3 collective-permute-done.17.pair_grad
  65.6 7.6 %attend_back.1 = (bf16[512,512]{1,0:T(8,128)(2,1)}, bf16[512,256]{1,0:T(8,128)(2,1)S(1)}, bf16[512,256]{1,0:T(8,128)(2,1)S(1)}, f32[512,256]{1,0:T(8,128)S(1)}) custom-call(s32[1,512]{1,0:T(1,128)S(1)} %bitcast.31, f32[4,512]{1,0:T(4,128)S(1)} %get-tuple-element.55.log_total, bf16[512,512]{1,0:T(8,128)(2,1)S(1)} %copy-done.2, ...), custom_call_target="tpu_custom_call" | custom-call | flops 4026531840 | bytes 2621440 | tf_op jit(solution)/shard_map/attend_back/pallas_call | solution.py:138
  73.2 0.6 collective-permute-done.23
  73.8 0.2 add_convert_fusion.1
  74.0 0.2 add_convert_fusion.2
  74.2 3.8 %collective-permute-start.22 = (bf16[512,512]{1,0:T(8,128)(2,1)S(1)}, bf16[512,512]{1,0:T(8,128)(2,1)S(1)}, u32[]{:S(2)}, u32[]{:S(2)}) collective-permute-start(bf16[512,512]{1,0:T(8,128)(2,1)S(1)} %add_convert_fusion.2), channel_id=1, source_target_pairs={{0,8},{4,12},{8,0},{12,4},{16,24},{20,28},{24,16},{28,20},{1,9},{5... | collective-permute-start | bytes 1572872 | tf_op jit(solution)/shard_map/ppermute | solution.py:205
  78.0 0.6 collective-permute-start.18
  78.7 0.1 fusion.17
  78.8 1.1 %collective-permute-start.14 = (bf16[512,512]{1,0:T(8,128)(2,1)S(1)}, bf16[512,512]{1,0:T(8,128)(2,1)S(1)}, u32[]{:S(2)}, u32[]{:S(2)}) collective-permute-start(bf16[512,512]{1,0:T(8,128)(2,1)S(1)} %fusion.17), channel_id=1, source_target_pairs={{0,2},{1,3},{2,0},{3,1},{4,6},{5,7},{6,4},{7,5},{8,10},{9,11},{10,... | collective-permute-start | bytes 1572872 | tf_op jit(solution)/shard_map/ppermute | solution.py:197
  79.9 0.2 fusion.14
  80.2 1.8 %collective-permute-start.16 = (bf16[512,512]{1,0:T(8,128)(2,1)S(1)}, bf16[512,512]{1,0:T(8,128)(2,1)S(1)}, u32[]{:S(2)}, u32[]{:S(2)}) collective-permute-start(bf16[512,512]{1,0:T(8,128)(2,1)S(1)} %fusion.14), channel_id=1, source_target_pairs={{0,4},{4,0},{8,12},{12,8},{16,20},{20,16},{24,28},{28,24},{1,5},{5... | collective-permute-start | bytes 1572872 | tf_op jit(solution)/shard_map/ppermute | solution.py:184
  82.0 5.1 %collective-permute-done.18 = bf16[512,256]{1,0:T(8,128)(2,1)S(1)} collective-permute-done((bf16[512,256]{1,0:T(8,128)(2,1)S(1)}, bf16[512,256]{1,0:T(8,128)(2,1)S(1)}, u32[]{:S(2)}, u32[]{:S(2)}) %collective-permute-start.18) | collective-permute-done | bytes 262176 | tf_op jit(solution)/shard_map/ppermute | solution.py:184
  87.2 0.1 add_convert_fusion.7
  87.2 1.9 %collective-permute-start.19 = (bf16[512,256]{1,0:T(8,128)(2,1)S(1)}, bf16[512,256]{1,0:T(8,128)(2,1)S(1)}, u32[]{:S(2)}, u32[]{:S(2)}) collective-permute-start(bf16[512,256]{1,0:T(8,128)(2,1)S(1)} %add_convert_fusion.7), channel_id=1, source_target_pairs={{0,24},{4,28},{8,0},{12,4},{16,8},{20,12},{24,16},{28,20},{1,25},{... | collective-permute-start | bytes 786440 | tf_op jit(solution)/shard_map/ppermute | solution.py:192
  89.2 1.7 %collective-permute-done.22 = bf16[512,512]{1,0:T(8,128)(2,1)S(1)} collective-permute-done((bf16[512,512]{1,0:T(8,128)(2,1)S(1)}, bf16[512,512]{1,0:T(8,128)(2,1)S(1)}, u32[]{:S(2)}, u32[]{:S(2)}) %collective-permute-start.22) | collective-permute-done | bytes 524320 | tf_op jit(solution)/shard_map/ppermute | solution.py:205
  90.9 1.0 %add_convert_fusion = bf16[512,512]{1,0:T(8,128)(2,1)} fusion(bf16[512,512]{1,0:T(8,128)(2,1)S(1)} %collective-permute-done.22, bf16[1536,512]{1,0:T(8,128)(2,1)S(1)} %fusion, bf16[512,512]{1,0:T(8,128)(2,1)S(1)} %collective-permute-done.24, pred[]{:T(512)S(6)} %or.3), kind=kLoop, calls=%fused_computation.25 | loop fusion | flops 1835008 | bytes 2097153 | tf_op jit(solution)/shard_map/convert_element_type | solution.py:380
  91.9 0.1 broadcast_in_dim.27
  92.0 0.2 fusion.19
  92.3 2.0 %collective-permute-done.19 = bf16[512,256]{1,0:T(8,128)(2,1)S(1)} collective-permute-done((bf16[512,256]{1,0:T(8,128)(2,1)S(1)}, bf16[512,256]{1,0:T(8,128)(2,1)S(1)}, u32[]{:S(2)}, u32[]{:S(2)}) %collective-permute-start.19) | collective-permute-done | bytes 262176 | tf_op jit(solution)/shard_map/ppermute | solution.py:192
  94.2 0.1 add_convert_fusion.6
  94.3 0.7 fusion.27
  95.1 1.0 %copy-done.3 = bf16[512,1024]{1,0:T(8,128)(2,1)} copy-done((bf16[512,1024]{1,0:T(8,128)(2,1)}, bf16[512,1024]{1,0:T(8,128)(2,1)S(1)}, u32[]{:S(2)}) %copy-start.3) | copy-done | bytes 1048600
  (47 shorter events, 0.9 us)
Async XLA Ops:
  0.6 7.6 %copy-start.4 = (bf16[512,512]{1,0:T(8,128)(2,1)S(1)}, bf16[512,512]{1,0:T(8,128)(2,1)}, u32[]{:S(2)}) copy-start(bf16[512,512]{1,0:T(8,128)(2,1)} %param.10) | copy-start | bytes 1572868
  2.4 12.4 %collective-permute-start = (bf16[528,256]{1,0:T(8,128)(2,1)S(1)}, bf16[528,256]{1,0:T(8,128)(2,1)S(1)}, u32[]{:S(2)}, u32[]{:S(2)}) collective-permute-start(bf16[528,256]{1,0:T(8,128)(2,1)S(1)} %fusion.21), channel_id=1, source_target_pairs={{0,8},{4,12},{8,16},{12,20},{16,24},{20,28},{24,0},{28,4},{1,9},{5... | collective-permute-start | bytes 811016 | tf_op jit(solution)/shard_map/ppermute | solution.py:192
  6.7 14.9 %collective-permute-start.3 = (bf16[128,2048]{1,0:T(8,128)(2,1)S(1)}, bf16[128,2048]{1,0:T(8,128)(2,1)S(1)}, u32[]{:S(2)}, u32[]{:S(2)}) collective-permute-start(bf16[128,2048]{1,0:T(8,128)(2,1)S(1)} %pad_maximum_fusion.2), channel_id=1, source_target_pairs={{0,4},{4,0},{8,12},{12,8},{16,20},{20,16},{24,28},{28,24},{1,5},{5... | collective-permute-start | bytes 1572872 | tf_op jit(solution)/shard_map/ppermute | solution.py:184
  8.3 17.0 %collective-permute-start.2 = (bf16[512,512]{1,0:T(8,128)(2,1)S(1)}, bf16[512,512]{1,0:T(8,128)(2,1)S(1)}, u32[]{:S(2)}, u32[]{:S(2)}) collective-permute-start(bf16[512,512]{1,0:T(8,128)(2,1)S(1)} %copy-done.4), channel_id=1, source_target_pairs={{0,8},{4,12},{8,0},{12,4},{16,24},{20,28},{24,16},{28,20},{1,9},{5... | collective-permute-start | bytes 1572872 | tf_op jit(solution)/shard_map/ppermute | solution.py:205
  9.8 15.8 %collective-permute-start.4 = (bf16[512,512]{1,0:T(8,128)(2,1)S(1)}, bf16[512,512]{1,0:T(8,128)(2,1)S(1)}, u32[]{:S(2)}, u32[]{:S(2)}) collective-permute-start(bf16[512,512]{1,0:T(8,128)(2,1)S(1)} %copy-done.4), channel_id=1, source_target_pairs={{8,16},{9,17},{10,18},{11,19},{12,20},{13,21},{14,22},{15,23},{16,... | collective-permute-start | bytes 1572872 | tf_op jit(solution)/shard_map/ppermute | solution.py:216
  9.8 5.0 %copy-start = (bf16[512,128]{1,0:T(8,128)(2,1)S(1)}, bf16[512,128]{1,0:T(8,128)(2,1)}, u32[]{:S(2)}) copy-start(bf16[512,128]{1,0:T(8,128)(2,1)} %value_ref.3) | copy-start | bytes 393220
  9.8 5.0 %copy-start.1 = (bf16[512,128]{1,0:T(8,128)(2,1)S(1)}, bf16[512,128]{1,0:T(8,128)(2,1)}, u32[]{:S(2)}) copy-start(bf16[512,128]{1,0:T(8,128)(2,1)} %key_ref.3) | copy-start | bytes 393220
  14.9 12.7 %collective-permute-start.1 = (bf16[528,256]{1,0:T(8,128)(2,1)S(1)}, bf16[528,256]{1,0:T(8,128)(2,1)S(1)}, u32[]{:S(2)}, u32[]{:S(2)}) collective-permute-start(bf16[528,256]{1,0:T(8,128)(2,1)S(1)} %broadcast_select_fusion.2), channel_id=1, source_target_pairs={{0,4},{4,0},{8,12},{12,8},{16,20},{20,16},{24,28},{28,24},{1,5},{5... | collective-permute-start | bytes 811016 | tf_op jit(solution)/shard_map/ppermute | solution.py:184
  21.6 17.1 %collective-permute-start.7 = (bf16[128,2048]{1,0:T(8,128)(2,1)S(1)}, bf16[128,2048]{1,0:T(8,128)(2,1)S(1)}, u32[]{:S(2)}, u32[]{:S(2)}) collective-permute-start(bf16[128,2048]{1,0:T(8,128)(2,1)S(1)} %collective-permute-done.3), channel_id=1, source_target_pairs={{0,1},{1,0},{2,3},{3,2},{4,5},{5,4},{6,7},{7,6},{8,9},{9,8},{10,11... | collective-permute-start | bytes 1572872 | tf_op jit(solution)/shard_map/ppermute | solution.py:197
  21.6 17.1 %collective-permute-start.8 = (bf16[128,2048]{1,0:T(8,128)(2,1)S(1)}, bf16[128,2048]{1,0:T(8,128)(2,1)S(1)}, u32[]{:S(2)}, u32[]{:S(2)}) collective-permute-start(bf16[128,2048]{1,0:T(8,128)(2,1)S(1)} %collective-permute-done.3), channel_id=1, source_target_pairs={{0,2},{1,3},{2,0},{3,1},{4,6},{5,7},{6,4},{7,5},{8,10},{9,11},{10,... | collective-permute-start | bytes 1572872 | tf_op jit(solution)/shard_map/ppermute | solution.py:197
  25.2 12.3 %collective-permute-start.5 = (bf16[512,512]{1,0:T(8,128)(2,1)S(1)}, bf16[512,512]{1,0:T(8,128)(2,1)S(1)}, u32[]{:S(2)}, u32[]{:S(2)}) collective-permute-start(bf16[512,512]{1,0:T(8,128)(2,1)S(1)} %collective-permute-done.2), channel_id=1, source_target_pairs={{8,16},{9,17},{10,18},{11,19},{12,20},{13,21},{14,22},{15,23},{16,... | collective-permute-start | bytes 1572872 | tf_op jit(solution)/shard_map/ppermute | solution.py:216
  25.6 2.0 %copy-start.5 = (s32[512]{0:T(512)S(1)}, s32[512]{0:T(512)}, u32[]{:S(2)}) copy-start(s32[512]{0:T(512)} %param.6) | copy-start | bytes 6148
  25.7 2.4 %copy-start.2 = (bf16[512,512]{1,0:T(8,128)(2,1)S(1)}, bf16[512,512]{1,0:T(8,128)(2,1)}, u32[]{:S(2)}) copy-start(bf16[512,512]{1,0:T(8,128)(2,1)} %query.3) | copy-start | bytes 1572868
  25.7 14.8 %collective-permute-start.11 = (bf16[512,512]{1,0:T(8,128)(2,1)S(1)}, bf16[512,512]{1,0:T(8,128)(2,1)S(1)}, u32[]{:S(2)}, u32[]{:S(2)}) collective-permute-start(bf16[512,512]{1,0:T(8,128)(2,1)S(1)} %collective-permute-done.4), channel_id=1, source_target_pairs={{0,8},{4,12},{8,0},{12,4},{16,24},{20,28},{24,16},{28,20},{1,9},{5... | collective-permute-start | bytes 1572872 | tf_op jit(solution)/shard_map/ppermute | solution.py:205
  34.6 13.4 %collective-permute-start.10 = (bf16[512,512]{1,0:T(8,128)(2,1)S(1)}, bf16[512,512]{1,0:T(8,128)(2,1)S(1)}, u32[]{:S(2)}, u32[]{:S(2)}) collective-permute-start(bf16[512,512]{1,0:T(8,128)(2,1)S(1)} %get-tuple-element.43.tokens.attended), channel_id=1, source_target_pairs={{0,4},{4,0},{8,12},{12,8},{16,20},{20,16},{24,28},{28,24},{1,5},{5... | collective-permute-start | bytes 1572872 | tf_op jit(solution)/shard_map/ppermute | solution.py:184
  37.5 14.6 %collective-permute-start.6 = (bf16[512,512]{1,0:T(8,128)(2,1)S(1)}, bf16[512,512]{1,0:T(8,128)(2,1)S(1)}, u32[]{:S(2)}, u32[]{:S(2)}) collective-permute-start(bf16[512,512]{1,0:T(8,128)(2,1)S(1)} %collective-permute-done.5), channel_id=1, source_target_pairs={{0,8},{4,12},{8,0},{12,4},{16,24},{20,28},{24,16},{28,20},{1,9},{5... | collective-permute-start | bytes 1572872 | tf_op jit(solution)/shard_map/ppermute | solution.py:205
  38.7 9.3 %collective-permute-start.9 = (bf16[128,2048]{1,0:T(8,128)(2,1)S(1)}, bf16[128,2048]{1,0:T(8,128)(2,1)S(1)}, u32[]{:S(2)}, u32[]{:S(2)}) collective-permute-start(bf16[128,2048]{1,0:T(8,128)(2,1)S(1)} %collective-permute-done.8), channel_id=1, source_target_pairs={{0,1},{1,0},{2,3},{3,2},{4,5},{5,4},{6,7},{7,6},{8,9},{9,8},{10,11... | collective-permute-start | bytes 1572872 | tf_op jit(solution)/shard_map/ppermute | solution.py:197
  48.6 14.9 %collective-permute-start.20 = (bf16[512,512]{1,0:T(8,128)(2,1)S(1)}, bf16[512,512]{1,0:T(8,128)(2,1)S(1)}, u32[]{:S(2)}, u32[]{:S(2)}) collective-permute-start(bf16[512,512]{1,0:T(8,128)(2,1)S(1)} %fusion.3), channel_id=1, source_target_pairs={{0,8},{4,12},{8,0},{12,4},{16,24},{20,28},{24,16},{28,20},{1,9},{5... | collective-permute-start | bytes 1572872 | tf_op jit(solution)/shard_map/ppermute | solution.py:205
  52.9 12.6 %collective-permute-start.17 = (bf16[512,512]{1,0:T(8,128)(2,1)S(1)}, bf16[512,512]{1,0:T(8,128)(2,1)S(1)}, u32[]{:S(2)}, u32[]{:S(2)}) collective-permute-start(bf16[512,512]{1,0:T(8,128)(2,1)S(1)} %fusion.2), channel_id=1, source_target_pairs={{0,4},{4,0},{8,12},{12,8},{16,20},{20,16},{24,28},{28,24},{1,5},{5... | collective-permute-start | bytes 1572872 | tf_op jit(solution)/shard_map/ppermute | solution.py:184
  56.0 7.7 %collective-permute-start.13 = (bf16[2,512,512]{2,1,0:T(8,128)(2,1)S(1)}, bf16[2,512,512]{2,1,0:T(8,128)(2,1)S(1)}, u32[]{:S(2)}, u32[]{:S(2)}) collective-permute-start(bf16[2,512,512]{2,1,0:T(8,128)(2,1)S(1)} %get-tuple-element.52), channel_id=1, source_target_pairs={{0,1},{1,0},{2,3},{3,2},{4,5},{5,4},{6,7},{7,6},{8,9},{9,8},{10,11... | collective-permute-start | bytes 3145736 | tf_op jit(solution)/shard_map/ppermute | solution.py:197
  57.6 16.1 %collective-permute-start.23 = (bf16[512,512]{1,0:T(8,128)(2,1)S(1)}, bf16[512,512]{1,0:T(8,128)(2,1)S(1)}, u32[]{:S(2)}, u32[]{:S(2)}) collective-permute-start(bf16[512,512]{1,0:T(8,128)(2,1)S(1)} %get-tuple-element.73), channel_id=1, source_target_pairs={{0,8},{4,12},{8,0},{12,4},{16,24},{20,28},{24,16},{28,20},{1,9},{5... | collective-permute-start | bytes 1572872 | tf_op jit(solution)/shard_map/ppermute | solution.py:205
  59.6 19.1 %collective-permute-start.12 = (bf16[2,512,512]{2,1,0:T(8,128)(2,1)S(1)}, bf16[2,512,512]{2,1,0:T(8,128)(2,1)S(1)}, u32[]{:S(2)}, u32[]{:S(2)}) collective-permute-start(bf16[2,512,512]{2,1,0:T(8,128)(2,1)S(1)} %get-tuple-element.49), channel_id=1, source_target_pairs={{0,1},{1,0},{2,3},{3,2},{4,5},{5,4},{6,7},{7,6},{8,9},{9,8},{10,11... | collective-permute-start | bytes 3145736 | tf_op jit(solution)/shard_map/ppermute | solution.py:197
  63.6 10.4 %collective-permute-start.21 = (bf16[512,512]{1,0:T(8,128)(2,1)S(1)}, bf16[512,512]{1,0:T(8,128)(2,1)S(1)}, u32[]{:S(2)}, u32[]{:S(2)}) collective-permute-start(bf16[512,512]{1,0:T(8,128)(2,1)S(1)} %add_convert_fusion.3), channel_id=1, source_target_pairs={{8,16},{9,17},{10,18},{11,19},{12,20},{13,21},{14,22},{15,23},{16,... | collective-permute-start | bytes 1572872 | tf_op jit(solution)/shard_map/ppermute | solution.py:216
  63.9 16.1 %collective-permute-start.15 = (bf16[512,512]{1,0:T(8,128)(2,1)S(1)}, bf16[512,512]{1,0:T(8,128)(2,1)S(1)}, u32[]{:S(2)}, u32[]{:S(2)}) collective-permute-start(bf16[512,512]{1,0:T(8,128)(2,1)S(1)} %fusion.18), channel_id=1, source_target_pairs={{0,2},{1,3},{2,0},{3,1},{4,6},{5,7},{6,4},{7,5},{8,10},{9,11},{10,... | collective-permute-start | bytes 1572872 | tf_op jit(solution)/shard_map/ppermute | solution.py:197
  73.9 15.2 %collective-permute-start.24 = (bf16[512,512]{1,0:T(8,128)(2,1)S(1)}, bf16[512,512]{1,0:T(8,128)(2,1)S(1)}, u32[]{:S(2)}, u32[]{:S(2)}) collective-permute-start(bf16[512,512]{1,0:T(8,128)(2,1)S(1)} %add_convert_fusion.1), channel_id=1, source_target_pairs={{8,16},{9,17},{10,18},{11,19},{12,20},{13,21},{14,22},{15,23},{16,... | collective-permute-start | bytes 1572872 | tf_op jit(solution)/shard_map/ppermute | solution.py:216
  74.2 16.6 %collective-permute-start.22 = (bf16[512,512]{1,0:T(8,128)(2,1)S(1)}, bf16[512,512]{1,0:T(8,128)(2,1)S(1)}, u32[]{:S(2)}, u32[]{:S(2)}) collective-permute-start(bf16[512,512]{1,0:T(8,128)(2,1)S(1)} %add_convert_fusion.2), channel_id=1, source_target_pairs={{0,8},{4,12},{8,0},{12,4},{16,24},{20,28},{24,16},{28,20},{1,9},{5... | collective-permute-start | bytes 1572872 | tf_op jit(solution)/shard_map/ppermute | solution.py:205
  78.0 9.1 %collective-permute-start.18 = (bf16[512,256]{1,0:T(8,128)(2,1)S(1)}, bf16[512,256]{1,0:T(8,128)(2,1)S(1)}, u32[]{:S(2)}, u32[]{:S(2)}) collective-permute-start(bf16[512,256]{1,0:T(8,128)(2,1)S(1)} %get-tuple-element.60), channel_id=1, source_target_pairs={{0,4},{4,0},{8,12},{12,8},{16,20},{20,16},{24,28},{28,24},{1,5},{5... | collective-permute-start | bytes 786440 | tf_op jit(solution)/shard_map/ppermute | solution.py:184
  78.8 13.1 %collective-permute-start.14 = (bf16[512,512]{1,0:T(8,128)(2,1)S(1)}, bf16[512,512]{1,0:T(8,128)(2,1)S(1)}, u32[]{:S(2)}, u32[]{:S(2)}) collective-permute-start(bf16[512,512]{1,0:T(8,128)(2,1)S(1)} %fusion.17), channel_id=1, source_target_pairs={{0,2},{1,3},{2,0},{3,1},{4,6},{5,7},{6,4},{7,5},{8,10},{9,11},{10,... | collective-permute-start | bytes 1572872 | tf_op jit(solution)/shard_map/ppermute | solution.py:197
  80.2 14.9 %collective-permute-start.16 = (bf16[512,512]{1,0:T(8,128)(2,1)S(1)}, bf16[512,512]{1,0:T(8,128)(2,1)S(1)}, u32[]{:S(2)}, u32[]{:S(2)}) collective-permute-start(bf16[512,512]{1,0:T(8,128)(2,1)S(1)} %fusion.14), channel_id=1, source_target_pairs={{0,4},{4,0},{8,12},{12,8},{16,20},{20,16},{24,28},{28,24},{1,5},{5... | collective-permute-start | bytes 1572872 | tf_op jit(solution)/shard_map/ppermute | solution.py:184
  87.2 7.0 %collective-permute-start.19 = (bf16[512,256]{1,0:T(8,128)(2,1)S(1)}, bf16[512,256]{1,0:T(8,128)(2,1)S(1)}, u32[]{:S(2)}, u32[]{:S(2)}) collective-permute-start(bf16[512,256]{1,0:T(8,128)(2,1)S(1)} %add_convert_fusion.7), channel_id=1, source_target_pairs={{0,24},{4,28},{8,0},{12,4},{16,8},{20,12},{24,16},{28,20},{1,25},{... | collective-permute-start | bytes 786440 | tf_op jit(solution)/shard_map/ppermute | solution.py:192
  95.1 1.0 %copy-start.3 = (bf16[512,1024]{1,0:T(8,128)(2,1)}, bf16[512,1024]{1,0:T(8,128)(2,1)S(1)}, u32[]{:S(2)}) copy-start(bf16[512,1024]{1,0:T(8,128)(2,1)S(1)} %constant_dynamic-update-slice_fusion.2) | copy-start | bytes 3145732

commit v4 on v3

--- a/solution.py
+++ b/solution.py
@@ -1,3 +1,5 @@
+import functools
+
 import functools
 
 import jax
@@ -13,7 +15,6 @@
 SCALE = HEAD_SIZE**-0.5
 LOG2E = 1.4426950408889634
 DOC_ROWS = 16
-OPT = dict(bwd='sent0', chunks='far_half', mates='', ownearly=1, pa='', passed='')
 
 
 def dot_nn(a, b):
@@ -62,24 +63,32 @@
             scores = jnp.where(allowed, scores * (SCALE * LOG2E), -jnp.inf)
             most = jnp.max(scores, axis=0, keepdims=True)
             weights = jnp.exp2(scores - most)
-            total = jnp.sum(weights, axis=0, keepdims=True)
-            out = dot_nn(values_t[:, low : low + width], weights.astype(jnp.bfloat16))
+            weights = weights.astype(jnp.bfloat16)
+            out = dot_nn(values_t[:, low : low + width], weights)
+            total = dot_nn(jnp.ones((8, width), jnp.bfloat16), weights)[0:1]
             attended[first : first + tile, lanes] = (out / total).T.astype(jnp.bfloat16)
             log_total[head : head + 1, first : first + tile] = most + jnp.log2(total)
 
 
 def backward_kernel(
-    start, log_total, query, kv2, kv1, key_ref, value_ref, attended, own_grad, pair_grad,
-    query_grad, near, far, own, keys, values, key_sum, value_sum, grad,
+    halo, start, log_total, query, kv2, kv1, key_ref, value_ref, attended, own_grad, pair_grad, *rest
 ):
     rows = query.shape[0]
     heads = query.shape[1] // HEAD_SIZE
+    if halo:
+        partial, near, far, keys, values, key_sum, value_sum, grad = rest
+    else:
+        partial, query_grad, own, keys, values, key_sum, value_sum, grad = rest
     fill_keys(kv2, kv1, key_ref, value_ref, keys, values, rows)
     keys_t = keys[...].T
     grad[...] = (own_grad[...] + pair_grad[...]).astype(grad.dtype)
     key_sum[...] = jnp.zeros_like(key_sum)
     value_sum[...] = jnp.zeros_like(value_sum)
     for first, tile, low, width in windows(rows, keys.shape[0]):
+        if halo:
+            width = DOC_MOST - low
+        else:
+            low, width = DOC_MOST, low + width - DOC_MOST
         allowed = mask_of(start[:, first : first + tile], first, tile, low, width)
         for head in range(heads):
             lanes = slice(head * HEAD_SIZE, (head + 1) * HEAD_SIZE)
@@ -96,8 +105,12 @@
             value_sum[low : low + width] += dot_nn(weights.astype(jnp.bfloat16), grad_head)
             key_sum[low : low + width] += dot_nn(shifted, query_head)
             back = dot_nn(keys_t[:, low : low + width], shifted) * SCALE
-            query_grad[first : first + tile, lanes] = back.T.astype(jnp.bfloat16)
-    for place, out in enumerate((far, near, own)):
+            if halo:
+                partial[lanes, first : first + tile] = back
+            else:
+                back += partial[lanes, first : first + tile]
+                query_grad[first : first + tile, lanes] = back.T.astype(jnp.bfloat16)
+    for place, out in ((0, far), (1, near)) if halo else ((2, own),):
         part = slice(place * rows, (place + 1) * rows)
         out[:, 0:HEAD_SIZE] = (key_sum[part] * SCALE).astype(out.dtype)
         out[:, HEAD_SIZE:] = value_sum[part].astype(out.dtype)
@@ -124,34 +137,35 @@
         in_specs=whole_vmem(6),
         out_specs=tuple(whole_vmem(2)),
         scratch_shapes=[pltpu.VMEM((3 * rows, HEAD_SIZE), jnp.bfloat16)] * 2,
-        compiler_params=params(OPT.get('vm_f', 16)),
+        compiler_params=params(16),
         cost_estimate=pl.CostEstimate(flops=cost * 512, transcendentals=cost, bytes_accessed=4 * rows * columns),
         name="attend",
     )(start, query, kv2, kv1, key, value)
 
 
-def attend_back(start, log_total, query, kv2, kv1, key, value, attended, own_grad, pair_grad):
+def attend_back(halo, start, log_total, query, *others):
     rows, columns = query.shape
     heads = columns // HEAD_SIZE
-    cost = rows * (DOC_MOST + rows) * heads
+    cost = rows * (DOC_MOST + rows) * heads // 2
     pair = jax.ShapeDtypeStruct((rows, 2 * HEAD_SIZE), jnp.bfloat16)
+    result = jax.ShapeDtypeStruct((rows, columns), jnp.bfloat16)
+    own = jax.ShapeDtypeStruct((rows, 2 * HEAD_SIZE), jnp.float32)
+    if halo:
+        outs = (jax.ShapeDtypeStruct((columns, rows), jnp.float32), pair, pair)
+    else:
+        outs = (result, own)
     return pl.pallas_call(
-        backward_kernel,
-        out_shape=(
-            jax.ShapeDtypeStruct((rows, columns), jnp.bfloat16),
-            pair,
-            pair,
-            jax.ShapeDtypeStruct((rows, 2 * HEAD_SIZE), jnp.float32),
-        ),
-        in_specs=whole_vmem(10),
-        out_specs=tuple(whole_vmem(4)),
+        functools.partial(backward_kernel, halo),
+        out_shape=outs,
+        in_specs=whole_vmem(3 + len(others)),
+        out_specs=tuple(whole_vmem(len(outs))),
         scratch_shapes=[pltpu.VMEM((3 * rows, HEAD_SIZE), jnp.bfloat16)] * 2
         + [pltpu.VMEM((3 * rows, HEAD_SIZE), jnp.float32)] * 2
         + [pltpu.VMEM((rows, columns), jnp.bfloat16)],
-        compiler_params=params(OPT.get('vm_b', 24)),
+        compiler_params=params(24),
         cost_estimate=pl.CostEstimate(flops=cost * 1280, transcendentals=cost, bytes_accessed=10 * rows * columns),
-        name="attend_back",
-    )(start, log_total, query, kv2, kv1, key, value, attended, own_grad, pair_grad)
+        name="attend_back_halo" if halo else "attend_back_own",
+    )(start, log_total, query, *others)
 
 
 def output_kernel(slots, tokens, late, early, sent, kept):
@@ -171,7 +185,7 @@
         out_shape=(result, result),
         in_specs=[pl.BlockSpec(memory_space=pltpu.SMEM)] + whole_vmem(3),
         out_specs=tuple(whole_vmem(2)),
-        compiler_params=params(OPT.get("vm_out", 12)),
+        compiler_params=params(12),
         cost_estimate=pl.CostEstimate(
             flops=8 * shard * rows * columns, transcendentals=0, bytes_accessed=32 * shard * rows
         ),
@@ -185,9 +199,6 @@
 
 
 def shift_line(value, by):
-    if by < 0 and OPT.get("open", 0):
-        devices = lax.axis_size("ctx")
-        return lax.ppermute(value, "ctx", [(i, i + 2 * by) for i in range(devices) if i + 2 * by >= 0])
     devices = lax.axis_size("ctx")
     return lax.ppermute(value, "ctx", [(i, (i + 2 * by) % devices) for i in range(devices)])
 
@@ -206,6 +217,8 @@
 
 
 OUTER = [(0, 1), (1, 0), (2, 3), (3, 2)]
+OUTWARD = [(1, 0), (2, 3)]
+INWARD = [(0, 1), (3, 2)]
 INNER = [(1, 2), (2, 1)]
 
 
@@ -221,11 +234,7 @@
 
 
 def after(value, *others):
-    return lax.optimization_barrier((value, *others))[0] if others else value
-
-
-def tie(value, name, default, **named):
-    return after(value, *[named[n] for n in OPT.get(name, default).split() if n in named])
+    return lax.optimization_barrier((value, *others))[0]
 
 
 def body(doc_ids, rotated_queries, rotated_keys, value_matrix, out_proj, cotangent):
@@ -239,9 +248,9 @@
     parity, place = index % 2, index // 2
     group = lax.axis_index("hg")
 
-    kv = jnp.concatenate([rotated_keys, value_matrix], 1)
-    docs = jnp.pad(doc_ids.reshape(-1, 2 * HEAD_SIZE), ((0, DOC_ROWS - rows // (2 * HEAD_SIZE)), (0, 0)))
-    pack = jnp.concatenate([kv, docs.astype(jnp.bfloat16)], 0)
+    doc_rows = rows // HEAD_SIZE
+    docs = jnp.pad(doc_ids.reshape(doc_rows, HEAD_SIZE), ((0, DOC_ROWS - doc_rows), (0, HEAD_SIZE))).astype(jnp.bfloat16)
+    pack = jnp.concatenate([jnp.concatenate([rotated_keys, value_matrix], 1), docs], 0)
     far_kv = shift_line(pack, 1)
 
     fast = line == 4 and groups == 4 and shard % HEAD_SIZE == 0
@@ -256,27 +265,25 @@
 
     cotangent = after(cotangent, pack)
     sent = columns_of(cotangent, group * part, part, 1 - parity)
-    out_proj = tie(out_proj, "w", "sent", sent=sent, pack=pack)
+    out_proj = after(out_proj, sent)
     quarter = swap_pair(sent)
     blocks = columns_of(after(cotangent, sent), 0, rows, parity)
     relay = jnp.where(parity == 0, pack, after(far_kv, blocks))
     near_kv = swap_pair(relay)
 
     def docs_of(received, back):
-        found = received[rows : rows + rows // (2 * HEAD_SIZE)].reshape(-1).astype(jnp.int32)
+        found = received[rows : rows + doc_rows, :HEAD_SIZE].astype(jnp.int32).reshape(-1)
         return jnp.where(index >= back, found, -1)
 
     doc_window = jnp.concatenate([docs_of(far_kv, 2), docs_of(near_kv, 1), doc_ids])
     start = jnp.sum((doc_window[:, None] < doc_ids[None, :]).astype(jnp.int32), axis=0, keepdims=True)
 
     if fast:
-        first = along_line(out_proj, OUTER)
-        second = inner_swap(out_proj)
+        first, second = along_line(out_proj, OUTER), inner_swap(out_proj)
         quarter = after(quarter, relay)
         first, second = after(first, quarter), after(second, quarter)
-        near_kv = tie(near_kv, "attend", "first second", first=first, second=second)
-        third = inner_swap(first)
-        fourth = along_line(second, OUTER)
+        near_kv = after(near_kv, first, second)
+        third, fourth = inner_swap(first), along_line(second, OUTER)
         end = (place == 0) | (place == 3)
     else:
         weights = lax.all_gather(out_proj, "ctx", axis=0, axis_index_groups=line_groups(line)).reshape(-1, columns)
@@ -287,9 +294,7 @@
     own_proj = dot_tn(blocks, attended)
     across = swap_heads(quarter, 2)
     if fast:
-        third = tie(third, "fifth", "attended", attended=attended, own_proj=own_proj, across=across, log=log_total)
-        fifth = along_line(third, OUTER)
-        across = tie(across, "mates", "attended", attended=attended, third=third, own_proj=own_proj)
+        fifth = along_line(after(third, attended), OUTWARD)
     mates = [swap_heads(quarter, 1), swap_heads(across, 1)]
     pair_blocks = jnp.zeros_like(blocks)
     for piece, owner in ((quarter, group), (mates[0], group ^ 1), (across, group ^ 2), (mates[1], group ^ 3)):
@@ -300,20 +305,17 @@
     if fast:
         near_half = jnp.concatenate([first, out_proj], 0)
         near_part = dot_nn(pair_blocks[:, 2 * shard :], near_half)
-        if OPT.get("ownearly", 0):
-            own_near = dot_nn(blocks[:, 2 * shard :], near_half)
-            pair_attended = after(pair_attended, own_near)
-        pair_attended = tie(pair_attended, "pa", "own_proj near_part", own_proj=own_proj, near_part=near_part)
+        own_near = dot_nn(blocks[:, 2 * shard :], near_half)
+        pair_attended = after(pair_attended, own_near)
         parts = [(own_proj[:shard] + dot_tn(pair_blocks[:, :shard], pair_attended)).astype(jnp.bfloat16)]
-        farthest = along_line(parts[0], OUTER)
-        fifth = tie(fifth, "far", "part0", part0=parts[0])
+        farthest = along_line(parts[0], INWARD)
+        fifth = after(fifth, parts[0])
         far_half = jnp.concatenate([jnp.where(end, fifth, third), jnp.where(end, fourth, second)], 0)
         pair_part = (dot_nn(pair_blocks[:, : 2 * shard], far_half) + near_part).astype(jnp.bfloat16)
-        if OPT.get("wbar", 1):
-            far_half, pair_attended = lax.optimization_barrier((far_half, pair_attended, pair_part))[0:2]
+        far_half, pair_attended = lax.optimization_barrier((far_half, pair_attended, pair_part))[0:2]
         pair_part = swap_pair(pair_part)
 
-        late_attended = tie(pair_attended, "chunks", "", far_half=far_half)
+        late_attended = after(pair_attended, far_half)
         parts.append(
             (own_proj[shard:] + dot_tn(pair_blocks[:, shard:], late_attended)).astype(jnp.bfloat16)
         )
@@ -326,10 +328,7 @@
             jnp.where(low == (column == 1), 0, 1),
         ]
         slots = jnp.stack(slots).astype(jnp.int32)
-        if OPT.get("ownearly", 0):
-            own_part = own_near + dot_nn(blocks[:, : 2 * shard], far_half)
-        else:
-            own_part = dot_nn(blocks[:, 2 * shard :], near_half) + dot_nn(blocks[:, : 2 * shard], far_half)
+        own_part = own_near + dot_nn(blocks[:, : 2 * shard], far_half)
         inner = (wide[0] + farthest).astype(jnp.bfloat16)
 
         def across_of(tokens):
@@ -338,9 +337,9 @@
             return (kept[0].astype(jnp.float32) + mate[0]).astype(jnp.bfloat16), kept[1].astype(jnp.float32), mate[1]
 
         sums = [across_of(pair_attended)]
-        sums.append(across_of(tie(attended, "out1", "", inner=inner, sent0=sums[0][0], own=own_part)))
-        sent1 = tie(sums[1][0], "sent1", "sent0", sent0=sums[0][0])
-        pair_part = tie(pair_part, "bwd", "inner sent0 sent1", inner=inner, sent0=sums[0][0], sent1=sent1)
+        sums.append(across_of(attended))
+        sent1 = after(sums[1][0], sums[0][0])
+        pair_part = after(pair_part, inner, sums[0][0])
         inner = jnp.where(end, 0, inner_swap(inner))
         reduced = [
             (near + mate + swap_heads(sent, 2)).astype(jnp.bfloat16)
@@ -361,20 +360,19 @@
             across = swap_heads((parts[2] + mates[0]).astype(jnp.bfloat16), 2)
             reduced.append((parts[3] + mates[1] + across).astype(jnp.bfloat16))
 
-    query_grad, near, far, own = attend_back(
-        start, log_total, rotated_queries, far_kv, near_kv, rotated_keys, value_matrix, attended, own_part, pair_part
-    )
+    operands = (start, log_total, rotated_queries, far_kv, near_kv, rotated_keys, value_matrix, attended, own_part, pair_part)
+    partial, near, far = attend_back(True, *operands)
+    query_grad, own = attend_back(False, *operands, partial)
     returned = swap_pair(near)
     if fast:
-        returned = tie(returned, "returned", "red0", red0=reduced[0], red1=reduced[1])
+        returned = after(returned, reduced[0])
     passed = far.astype(jnp.float32) + jnp.where(parity == 1, returned, 0)
     passed = passed.astype(jnp.bfloat16)
     if fast:
-        wide[2] = tie(wide[2], "nearer", "own", own=own, passed=passed)
+        wide[2] = after(wide[2], own)
         nearer = (wide[2] + inner).astype(jnp.bfloat16)
-        wide[1] = tie(wide[1], "other", "own", own=own, passed=passed, nearer=nearer)
+        wide[1] = after(wide[1], own)
         other = (wide[1] + farther).astype(jnp.bfloat16)
-        passed = tie(passed, "passed", "", nearer=nearer, other=other)
         nearer = along_line(nearer, OUTER)
         other = jnp.where(end, 0, inner_swap(other))
         proj_grad = (wide[3] + nearer + other).astype(jnp.bfloat16)
@@ -382,8 +380,7 @@
     if own_output.shape[1] == shard:
         layer_output = jnp.zeros((rows, 2 * shard), own_output.dtype)
         layer_output = lax.dynamic_update_slice(layer_output, own_output, (0, parity * shard))
-        if OPT.get("asm", 1):
-            other_output = after(other_output, layer_output)
+        other_output = after(other_output, layer_output)
         layer_output = lax.dynamic_update_slice(layer_output, other_output, (0, (1 - parity) * shard))
     else:
         halves = [jnp.where(parity == 0, own_output, other_output), jnp.where(parity == 0, other_output, own_output)]

time: 96.3 us -> 95.5 us (level)
  starting transfers between devices: 28 us -> 32.1 us
  waiting for transfers between devices: 32.8 us -> 29.8 us
  Pallas kernels: 17.8 us -> 16.1 us
    pallas_call x1, Pallas kernels: 6.56 us -> 4.2 us  [attend(): pl.pallas_call(forward_kernel, out_shape=(jax.ShapeDtypeStruct((rows, col...]
    ppermute x6, starting transfers between devices: 9.56 us -> 11.8 us  [along_line(): return lax.ppermute(value, 'ctx', line_pairs(pairs))]
    ppermute x6, waiting for transfers between devices: 17.7 us -> 16 us  [swap_pair(): return lax.ppermute(value, 'ctx', [(i, i ^ 1) for i in range(devices)])]
    ppermute x6, waiting for transfers between devices: 9.84 us -> 8.72 us  [along_line(): return lax.ppermute(value, 'ctx', line_pairs(pairs))]
    ppermute x6, starting transfers between devices: 8.72 us -> 9.77 us  [swap_pair(): return lax.ppermute(value, 'ctx', [(i, i ^ 1) for i in range(devices)])]
    ppermute x2, starting transfers between devices: 5 us -> 6.01 us  [shift_line(): lax.ppermute(value, 'ctx', [(i, (i + 2 * by) % devices) for i in range(de...]
    pallas_call x1 -> x2, Pallas kernels: 7.63 us -> 8.21 us  [attend_back(): pl.pallas_call(functools.partial(backward_kernel, halo), out_shape=outs,...]
  transfers between devices with their start and end apart: 25 -> 25, of which waited for: 12 -> 11; matrix products, arithmetic and copies ran while one was open for 14% -> 14% of each run, Pallas kernels for 19% -> 17%
where the time goes in v4:
time: 95.5 us; the launch traced here: 95.3 us
  starting transfers between devices  32.1 us (34%)
  waiting for transfers between devices  29.8 us (31%)
  Pallas kernels  16.1 us (17%)
  matrix products  5.64 us (6%)
  other arithmetic  5.32 us (6%)
  local copies, waits for them, and re-layouts  5.29 us (6%)
  between operations  1.03 us (1%)
    ppermute x6, waiting for transfers between devices, swap_pair(): return lax.ppermute(value, 'ctx', [(i, i ^ 1) for i in range(devices)])  16 us
    ppermute x6, starting transfers between devices, along_line(): return lax.ppermute(value, 'ctx', line_pairs(pairs))  11.8 us
    ppermute x6, starting transfers between devices, swap_pair(): return lax.ppermute(value, 'ctx', [(i, i ^ 1) for i in range(devices)])  9.77 us
    ppermute x6, waiting for transfers between devices, along_line(): return lax.ppermute(value, 'ctx', line_pairs(pairs))  8.72 us
    pallas_call x2, Pallas kernels, attend_back(): pl.pallas_call(functools.partial(backward_kernel, halo), out_shape=outs,...  8.21 us
    ppermute x2, starting transfers between devices, shift_line(): lax.ppermute(value, 'ctx', [(i, (i + 2 * by) % devices) for i in range(de...  6.01 us
    ppermute x2, waiting for transfers between devices, shift_line(): lax.ppermute(value, 'ctx', [(i, (i + 2 * by) % devices) for i in range(de...  5.1 us
    ppermute x7, starting transfers between devices, swap_heads(): return lax.ppermute(value, 'hg', [(i, i ^ bit) for i in range(groups)])  4.36 us
  transfers between devices with their start and end apart: 25, of which 11 were waited for; matrix products, arithmetic and copies ran while one was open for 14% of the time, Pallas kernels for 17%

profile of v4, /device:TPU:0, one launch (start us, length us, event | category | flops | bytes accessed | tf_op | source)
XLA Modules:
  0.0 95.3 jit_solution(5922750388976354197)
XLA Ops:
  0.6 0.7 convert_bitcast_fusion
  1.4 1.0 %fusion.21 = bf16[528,256]{1,0:T(8,128)(2,1)S(1)} fusion(bf16[4,128]{1,0:T(4,128)(2,1)S(1)} %convert_bitcast_fusion, bf16[512,128]{1,0:T(8,128)(2,1)} %value_ref.5, bf16[512,128]{1,0:T(8,128)(2,1)} %key_ref.5), kind=kLoop, calls=%fused_computation.43 | loop fusion | flops 1081344 | bytes 533504 | tf_op jit(solution)/shard_map/concatenate | solution.py:253
  2.4 3.1 %collective-permute-start = (bf16[528,256]{1,0:T(8,128)(2,1)S(1)}, bf16[528,256]{1,0:T(8,128)(2,1)S(1)}, u32[]{:S(2)}, u32[]{:S(2)}) collective-permute-start(bf16[528,256]{1,0:T(8,128)(2,1)S(1)} %fusion.21), channel_id=1, source_target_pairs={{0,8},{4,12},{8,16},{12,20},{16,24},{20,28},{24,0},{28,4},{1,9},{5... | collective-permute-start | bytes 811016 | tf_op jit(solution)/shard_map/ppermute | solution.py:203
  5.5 1.1 %fusion.25 = (bf16[128,512]{1,0:T(8,128)(2,1)S(1)}, bf16[128,512]{1,0:T(8,128)(2,1)S(1)}, bf16[128,512]{1,0:T(8,128)(2,1)S(1)}, bf16[128,512]{1,0:T(8,128)(2,1)S(1)}) fusion(bf16[512,4096]{1,0:T(8,128)(2,1)} %param.11, s32[]{:T(128)S(6)} %select_n.167, s32[]{:T(128)S(6)} %select_n.169, s32[]{:T(128)S(6)} %select_n.173, s32[]{:T(128)S(6)} %select_n.172, ...), kind=kLoop, calls=%fused_computation.65 | loop fusion | bytes 1048596 | tf_op jit(solution)/shard_map/dynamic_slice | solution.py:263
  6.7 1.6 %collective-permute-start.3 = (bf16[128,2048]{1,0:T(8,128)(2,1)S(1)}, bf16[128,2048]{1,0:T(8,128)(2,1)S(1)}, u32[]{:S(2)}, u32[]{:S(2)}) collective-permute-start(bf16[128,2048]{1,0:T(8,128)(2,1)S(1)} %pad_maximum_fusion.2), channel_id=1, source_target_pairs={{0,4},{4,0},{8,12},{12,8},{16,20},{20,16},{24,28},{28,24},{1,5},{5... | collective-permute-start | bytes 1572872 | tf_op jit(solution)/shard_map/ppermute | solution.py:198
  8.2 1.6 %collective-permute-start.2 = (bf16[512,512]{1,0:T(8,128)(2,1)S(1)}, bf16[512,512]{1,0:T(8,128)(2,1)S(1)}, u32[]{:S(2)}, u32[]{:S(2)}) collective-permute-start(bf16[512,512]{1,0:T(8,128)(2,1)S(1)} %copy-done.4), channel_id=1, source_target_pairs={{0,8},{4,12},{8,0},{12,4},{16,24},{20,28},{24,16},{28,20},{1,9},{5... | collective-permute-start | bytes 1572872 | tf_op jit(solution)/shard_map/ppermute | solution.py:216
  9.8 1.7 %constant_dynamic-slice_fusion.3 = (bf16[512,512]{1,0:T(8,128)(2,1)S(1)}, bf16[512,512]{1,0:T(8,128)(2,1)S(1)}, bf16[512,512]{1,0:T(8,128)(2,1)S(1)}, bf16[512,512]{1,0:T(8,128)(2,1)S(1)}) fusion(bf16[512,4096]{1,0:T(8,128)(2,1)} %param.11, s32[]{:T(128)S(6)} %select_n.174, s32[]{:T(128)S(6)} %select_n.177, s32[]{:T(128)S(6)} %select_n.176, s32[]{:T(128)S(6)} %select_n.175), kind=kLoop, calls=%fused_computation.56 | loop fusion | bytes 4194320 | tf_op jit(solution)/shard_map/dynamic_slice | solution.py:263
  11.5 0.1 pad_add_fusion.1.slots
  11.6 3.2 %collective-permute-done.kv2 = bf16[528,256]{1,0:T(8,128)(2,1)S(1)} collective-permute-done((bf16[528,256]{1,0:T(8,128)(2,1)S(1)}, bf16[528,256]{1,0:T(8,128)(2,1)S(1)}, u32[]{:S(2)}, u32[]{:S(2)}) %collective-permute-start) | collective-permute-done | bytes 270368 | tf_op jit(solution)/shard_map/ppermute | solution.py:203
  14.8 0.1 broadcast_select_fusion.2
  14.9 1.8 %collective-permute-start.1 = (bf16[528,256]{1,0:T(8,128)(2,1)S(1)}, bf16[528,256]{1,0:T(8,128)(2,1)S(1)}, u32[]{:S(2)}, u32[]{:S(2)}) collective-permute-start(bf16[528,256]{1,0:T(8,128)(2,1)S(1)} %broadcast_select_fusion.2), channel_id=1, source_target_pairs={{0,4},{4,0},{8,12},{12,8},{16,20},{20,16},{24,28},{28,24},{1,5},{5... | collective-permute-start | bytes 811016 | tf_op jit(solution)/shard_map/ppermute | solution.py:198
  16.8 4.8 %collective-permute-done.3 = bf16[128,2048]{1,0:T(8,128)(2,1)S(1)} collective-permute-done((bf16[128,2048]{1,0:T(8,128)(2,1)S(1)}, bf16[128,2048]{1,0:T(8,128)(2,1)S(1)}, u32[]{:S(2)}, u32[]{:S(2)}) %collective-permute-start.3) | collective-permute-done | bytes 524320 | tf_op jit(solution)/shard_map/ppermute | solution.py:198
  21.6 1.5 %collective-permute-start.8 = (bf16[128,2048]{1,0:T(8,128)(2,1)S(1)}, bf16[128,2048]{1,0:T(8,128)(2,1)S(1)}, u32[]{:S(2)}, u32[]{:S(2)}) collective-permute-start(bf16[128,2048]{1,0:T(8,128)(2,1)S(1)} %collective-permute-done.3), channel_id=1, source_target_pairs={{0,2},{1,3},{2,0},{3,1},{4,6},{5,7},{6,4},{7,5},{8,10},{9,11},{10,... | collective-permute-start | bytes 1572872 | tf_op jit(solution)/shard_map/ppermute | solution.py:208
  23.1 2.1 %collective-permute-done.2 = bf16[512,512]{1,0:T(8,128)(2,1)S(1)} collective-permute-done((bf16[512,512]{1,0:T(8,128)(2,1)S(1)}, bf16[512,512]{1,0:T(8,128)(2,1)S(1)}, u32[]{:S(2)}, u32[]{:S(2)}) %collective-permute-start.2) | collective-permute-done | bytes 524320 | tf_op jit(solution)/shard_map/ppermute | solution.py:216
  25.3 0.2 broadcast_in_dim.30
  25.7 1.2 %collective-permute-start.11 = (bf16[512,512]{1,0:T(8,128)(2,1)S(1)}, bf16[512,512]{1,0:T(8,128)(2,1)S(1)}, u32[]{:S(2)}, u32[]{:S(2)}) collective-permute-start(bf16[512,512]{1,0:T(8,128)(2,1)S(1)} %collective-permute-done.4), channel_id=1, source_target_pairs={{0,8},{4,12},{8,0},{12,4},{16,24},{20,28},{24,16},{28,20},{1,9},{5... | collective-permute-start | bytes 1572872 | tf_op jit(solution)/shard_map/ppermute | solution.py:216
  26.9 0.7 fusion.7
  27.6 0.4 convert_reduce_fusion
  28.0 4.2 %attend.1 = (bf16[512,512]{1,0:T(8,128)(2,1)S(1)}, f32[4,512]{1,0:T(4,128)S(1)}) custom-call(s32[1,512]{1,0:T(1,128)S(1)} %bitcast.30, bf16[512,512]{1,0:T(8,128)(2,1)S(1)} %copy-done.2, bf16[528,256]{1,0:T(8,128)(2,1)S(1)} %collective-permute-done.kv2, bf16[528,256]{1,0:T(8,128)(2,1)S(1)} %collective-permute-done.1.kv1, bf16[512,128]{1,0:T(8,128)(2,1)S(1)} %copy-done.1, ...), custom_call_target="tpu_custom_call" | custom-call | flops 1610612736 | bytes 1048576 | tf_op jit(solution)/shard_map/attend/pallas_call | solution.py:131
  32.2 1.6 %collective-permute-start.10 = (bf16[512,512]{1,0:T(8,128)(2,1)S(1)}, bf16[512,512]{1,0:T(8,128)(2,1)S(1)}, u32[]{:S(2)}, u32[]{:S(2)}) collective-permute-start(bf16[512,512]{1,0:T(8,128)(2,1)S(1)} %get-tuple-element.44.tokens.attended), channel_id=1, source_target_pairs={{0,4},{4,0},{8,12},{12,8},{16,20},{20,16},{24,28},{28,24},{1,5},{5... | collective-permute-start | bytes 1572872 | tf_op jit(solution)/shard_map/ppermute | solution.py:198
  33.8 1.3 %fusion.24 = f32[2048,512]{1,0:T(8,128)S(1)} fusion(bf16[512,512]{1,0:T(8,128)(2,1)S(1)} %get-tuple-element.44.tokens.attended, bf16[512,512]{1,0:T(8,128)(2,1)S(1)} %get-tuple-element.68, bf16[512,512]{1,0:T(8,128)(2,1)S(1)} %get-tuple-element.69, bf16[512,512]{1,0:T(8,128)(2,1)S(1)} %get-tuple-element.70, bf16[512,512]{1,0:T(8,128)(2,1)S(1)} %get-tuple-element.67), kind=kOutput, calls=%fused_computation.64 | convolution fusion | flops 1082130432 | bytes 6815744 | tf_op jit(solution)/shard_map/dot_general | solution.py:29
  35.1 1.3 %collective-permute-start.6 = (bf16[512,512]{1,0:T(8,128)(2,1)S(1)}, bf16[512,512]{1,0:T(8,128)(2,1)S(1)}, u32[]{:S(2)}, u32[]{:S(2)}) collective-permute-start(bf16[512,512]{1,0:T(8,128)(2,1)S(1)} %collective-permute-done.5), channel_id=1, source_target_pairs={{8,0},{12,4},{16,24},{20,28},{9,1},{13,5},{17,25},{21,29},{10,2},{... | collective-permute-start | bytes 1572872 | tf_op jit(solution)/shard_map/ppermute | solution.py:216
  36.6 3.5 %collective-permute-done.11 = bf16[512,512]{1,0:T(8,128)(2,1)S(1)} collective-permute-done((bf16[512,512]{1,0:T(8,128)(2,1)S(1)}, bf16[512,512]{1,0:T(8,128)(2,1)S(1)}, u32[]{:S(2)}, u32[]{:S(2)}) %collective-permute-start.11) | collective-permute-done | bytes 524320 | tf_op jit(solution)/shard_map/ppermute | solution.py:216
  40.1 0.1 broadcast_select_fusion
  40.2 5.4 %collective-permute-done.10.tokens = bf16[512,512]{1,0:T(8,128)(2,1)S(1)} collective-permute-done((bf16[512,512]{1,0:T(8,128)(2,1)S(1)}, bf16[512,512]{1,0:T(8,128)(2,1)S(1)}, u32[]{:S(2)}, u32[]{:S(2)}) %collective-permute-start.10) | collective-permute-done | bytes 524320 | tf_op jit(solution)/shard_map/ppermute | solution.py:198
  45.7 0.5 fusion.3
  46.2 3.7 %collective-permute-start.18 = (bf16[512,512]{1,0:T(8,128)(2,1)S(1)}, bf16[512,512]{1,0:T(8,128)(2,1)S(1)}, u32[]{:S(2)}, u32[]{:S(2)}) collective-permute-start(bf16[512,512]{1,0:T(8,128)(2,1)S(1)} %fusion.3), channel_id=1, source_target_pairs={{0,8},{4,12},{24,16},{28,20},{1,9},{5,13},{25,17},{29,21},{2,10},{... | collective-permute-start | bytes 1572872 | tf_op jit(solution)/shard_map/ppermute | solution.py:216
  49.9 0.7 fusion.4
  50.6 0.7 collective-permute-done.6
  51.3 0.1 broadcast_select_fusion.1
  51.4 0.7 fusion.2
  52.2 1.6 %collective-permute-start.17 = (bf16[512,512]{1,0:T(8,128)(2,1)S(1)}, bf16[512,512]{1,0:T(8,128)(2,1)S(1)}, u32[]{:S(2)}, u32[]{:S(2)}) collective-permute-start(bf16[512,512]{1,0:T(8,128)(2,1)S(1)} %fusion.2), channel_id=1, source_target_pairs={{0,4},{4,0},{8,12},{12,8},{16,20},{20,16},{24,28},{28,24},{1,5},{5... | collective-permute-start | bytes 1572872 | tf_op jit(solution)/shard_map/ppermute | solution.py:198
  53.7 1.8 %output_parts.3 = (bf16[2,512,512]{2,1,0:T(8,128)(2,1)S(1)}, bf16[2,512,512]{2,1,0:T(8,128)(2,1)S(1)}) custom-call(s32[3]{0:T(128)S(1)} %pad_add_fusion.1.slots, bf16[512,512]{1,0:T(8,128)(2,1)S(1)} %collective-permute-done.10.tokens, bf16[1024,512]{1,0:T(8,128)(2,1)S(1)} %pad_maximum_fusion.1.late, bf16[1024,512]{1,0:T(8,128)(2,1)S(1)} %constant_dynamic-update-slice_fusion.early), custom_call_target="tpu_custom_call" | custom-call | flops 1073741824 | bytes 8388608 | tf_op jit(solution)/shard_map/output_parts/pallas_call | solution.py:183
  55.7 1.1 %fusion = bf16[1536,512]{1,0:T(8,128)(2,1)S(1)} fusion(bf16[512,512]{1,0:T(8,128)(2,1)S(1)} %collective-permute-done.10.tokens, f32[2048,512]{1,0:T(8,128)S(1)} %fusion.24, bf16[512,2048]{1,0:T(8,128)(2,1)S(1)} %constant_dynamic-update-slice_fusion.3), kind=kOutput, calls=%fused_computation.2 | convolution fusion | flops 806879232 | bytes 6815744 | tf_op jit(solution)/shard_map/dot_general | solution.py:29
  56.7 0.3 fusion.26
  57.1 1.8 %output_parts.2 = (bf16[2,512,512]{2,1,0:T(8,128)(2,1)S(1)}, bf16[2,512,512]{2,1,0:T(8,128)(2,1)S(1)}) custom-call(s32[3]{0:T(128)S(1)} %pad_add_fusion.1.slots, bf16[512,512]{1,0:T(8,128)(2,1)S(1)} %get-tuple-element.44.tokens.attended, bf16[1024,512]{1,0:T(8,128)(2,1)S(1)} %pad_maximum_fusion.1.late, ...), custom_call_target="tpu_custom_call" | custom-call | flops 1073741824 | bytes 8388608 | tf_op jit(solution)/shard_map/output_parts/pallas_call | solution.py:183
  59.0 0.6 collective-permute-start.12
  59.5 0.7 convolution_add_fusion.1.own_grad
  60.2 1.8 %collective-permute-done.18 = bf16[512,512]{1,0:T(8,128)(2,1)S(1)} collective-permute-done((bf16[512,512]{1,0:T(8,128)(2,1)S(1)}, bf16[512,512]{1,0:T(8,128)(2,1)S(1)}, u32[]{:S(2)}, u32[]{:S(2)}) %collective-permute-start.18) | collective-permute-done | bytes 524320 | tf_op jit(solution)/shard_map/ppermute | solution.py:216
  62.0 0.1 add_convert_fusion.3
  62.3 0.1 fusion.18
  62.4 1.6 %collective-permute-start.15 = (bf16[512,512]{1,0:T(8,128)(2,1)S(1)}, bf16[512,512]{1,0:T(8,128)(2,1)S(1)}, u32[]{:S(2)}, u32[]{:S(2)}) collective-permute-start(bf16[512,512]{1,0:T(8,128)(2,1)S(1)} %fusion.18), channel_id=1, source_target_pairs={{0,2},{1,3},{2,0},{3,1},{4,6},{5,7},{6,4},{7,5},{8,10},{9,11},{10,... | collective-permute-start | bytes 1572872 | tf_op jit(solution)/shard_map/ppermute | solution.py:208
  64.0 0.7 collective-permute-done.17.pair_grad
  64.6 4.8 %attend_back_halo.1 = (f32[512,512]{1,0:T(8,128)S(1)}, bf16[512,256]{1,0:T(8,128)(2,1)S(1)}, bf16[512,256]{1,0:T(8,128)(2,1)S(1)}) custom-call(s32[1,512]{1,0:T(1,128)S(1)} %bitcast.31, f32[4,512]{1,0:T(4,128)S(1)} %get-tuple-element.56.log_total, bf16[512,512]{1,0:T(8,128)(2,1)S(1)} %copy-done.2, bf16[528,256]{1,0:T(8,128)(2,1)S(1)} %collective-permute-done.kv2, ...), custom_call_target="tpu_custom_call" | custom-call | flops 2013265920 | bytes 2621440 | tf_op jit(solution)/shard_map/attend_back_halo/pallas_call | solution.py:157
  69.5 3.4 %attend_back_own.1 = (bf16[512,512]{1,0:T(8,128)(2,1)}, f32[512,256]{1,0:T(8,128)S(1)}) custom-call(s32[1,512]{1,0:T(1,128)S(1)} %bitcast.32, f32[4,512]{1,0:T(4,128)S(1)} %get-tuple-element.56.log_total, bf16[512,512]{1,0:T(8,128)(2,1)S(1)} %copy-done.2, bf16[528,256]{1,0:T(8,128)(2,1)S(1)} %collective-permute-done.kv2, ...), custom_call_target="tpu_custom_call" | custom-call | flops 2013265920 | bytes 2621440 | tf_op jit(solution)/shard_map/attend_back_own/pallas_call | solution.py:157
  72.9 0.2 add_convert_fusion.1
  73.1 0.2 add_convert_fusion.2
  73.3 4.0 %collective-permute-start.22 = (bf16[512,512]{1,0:T(8,128)(2,1)S(1)}, bf16[512,512]{1,0:T(8,128)(2,1)S(1)}, u32[]{:S(2)}, u32[]{:S(2)}) collective-permute-start(bf16[512,512]{1,0:T(8,128)(2,1)S(1)} %add_convert_fusion.2), channel_id=1, source_target_pairs={{0,8},{4,12},{8,0},{12,4},{16,24},{20,28},{24,16},{28,20},{1,9},{5... | collective-permute-start | bytes 1572872 | tf_op jit(solution)/shard_map/ppermute | solution.py:216
  77.3 1.4 %collective-permute-start.19 = (bf16[512,256]{1,0:T(8,128)(2,1)S(1)}, bf16[512,256]{1,0:T(8,128)(2,1)S(1)}, u32[]{:S(2)}, u32[]{:S(2)}) collective-permute-start(bf16[512,256]{1,0:T(8,128)(2,1)S(1)} %get-tuple-element.62), channel_id=1, source_target_pairs={{0,4},{4,0},{8,12},{12,8},{16,20},{20,16},{24,28},{28,24},{1,5},{5... | collective-permute-start | bytes 786440 | tf_op jit(solution)/shard_map/ppermute | solution.py:198
  78.7 0.1 fusion.17
  78.8 0.6 collective-permute-start.14
  79.4 0.2 fusion.14
  79.6 1.8 %collective-permute-start.16 = (bf16[512,512]{1,0:T(8,128)(2,1)S(1)}, bf16[512,512]{1,0:T(8,128)(2,1)S(1)}, u32[]{:S(2)}, u32[]{:S(2)}) collective-permute-start(bf16[512,512]{1,0:T(8,128)(2,1)S(1)} %fusion.14), channel_id=1, source_target_pairs={{0,4},{4,0},{8,12},{12,8},{16,20},{20,16},{24,28},{28,24},{1,5},{5... | collective-permute-start | bytes 1572872 | tf_op jit(solution)/shard_map/ppermute | solution.py:198
  81.4 5.1 %collective-permute-done.19 = bf16[512,256]{1,0:T(8,128)(2,1)S(1)} collective-permute-done((bf16[512,256]{1,0:T(8,128)(2,1)S(1)}, bf16[512,256]{1,0:T(8,128)(2,1)S(1)}, u32[]{:S(2)}, u32[]{:S(2)}) %collective-permute-start.19) | collective-permute-done | bytes 262176 | tf_op jit(solution)/shard_map/ppermute | solution.py:198
  86.5 0.1 add_convert_fusion.7
  86.6 2.9 %collective-permute-start.20 = (bf16[512,256]{1,0:T(8,128)(2,1)S(1)}, bf16[512,256]{1,0:T(8,128)(2,1)S(1)}, u32[]{:S(2)}, u32[]{:S(2)}) collective-permute-start(bf16[512,256]{1,0:T(8,128)(2,1)S(1)} %add_convert_fusion.7), channel_id=1, source_target_pairs={{0,24},{4,28},{8,0},{12,4},{16,8},{20,12},{24,16},{28,20},{1,25},{... | collective-permute-start | bytes 786440 | tf_op jit(solution)/shard_map/ppermute | solution.py:203
  89.5 0.6 collective-permute-done.22
  90.1 1.0 %add_convert_fusion = bf16[512,512]{1,0:T(8,128)(2,1)} fusion(bf16[512,512]{1,0:T(8,128)(2,1)S(1)} %collective-permute-done.22, bf16[1536,512]{1,0:T(8,128)(2,1)S(1)} %fusion, bf16[512,512]{1,0:T(8,128)(2,1)S(1)} %collective-permute-done.24, pred[]{:T(512)S(6)} %or.3), kind=kLoop, calls=%fused_computation.25 | loop fusion | flops 1835008 | bytes 2097153 | tf_op jit(solution)/shard_map/convert_element_type | solution.py:378
  91.1 0.1 broadcast_in_dim.27
  91.3 0.2 fusion.19
  91.5 1.9 %collective-permute-done.20 = bf16[512,256]{1,0:T(8,128)(2,1)S(1)} collective-permute-done((bf16[512,256]{1,0:T(8,128)(2,1)S(1)}, bf16[512,256]{1,0:T(8,128)(2,1)S(1)}, u32[]{:S(2)}, u32[]{:S(2)}) %collective-permute-start.20) | collective-permute-done | bytes 262176 | tf_op jit(solution)/shard_map/ppermute | solution.py:203
  93.4 0.1 add_convert_fusion.6
  93.5 0.7 fusion.27
  94.3 1.0 %copy-done.3 = bf16[512,1024]{1,0:T(8,128)(2,1)} copy-done((bf16[512,1024]{1,0:T(8,128)(2,1)}, bf16[512,1024]{1,0:T(8,128)(2,1)S(1)}, u32[]{:S(2)}) %copy-start.3) | copy-done | bytes 1048600
  (45 shorter events, 1.0 us)
Async XLA Ops:
  0.6 7.6 %copy-start.4 = (bf16[512,512]{1,0:T(8,128)(2,1)S(1)}, bf16[512,512]{1,0:T(8,128)(2,1)}, u32[]{:S(2)}) copy-start(bf16[512,512]{1,0:T(8,128)(2,1)} %param.10) | copy-start | bytes 1572868
  2.4 12.4 %collective-permute-start = (bf16[528,256]{1,0:T(8,128)(2,1)S(1)}, bf16[528,256]{1,0:T(8,128)(2,1)S(1)}, u32[]{:S(2)}, u32[]{:S(2)}) collective-permute-start(bf16[528,256]{1,0:T(8,128)(2,1)S(1)} %fusion.21), channel_id=1, source_target_pairs={{0,8},{4,12},{8,16},{12,20},{16,24},{20,28},{24,0},{28,4},{1,9},{5... | collective-permute-start | bytes 811016 | tf_op jit(solution)/shard_map/ppermute | solution.py:203
  6.7 14.9 %collective-permute-start.3 = (bf16[128,2048]{1,0:T(8,128)(2,1)S(1)}, bf16[128,2048]{1,0:T(8,128)(2,1)S(1)}, u32[]{:S(2)}, u32[]{:S(2)}) collective-permute-start(bf16[128,2048]{1,0:T(8,128)(2,1)S(1)} %pad_maximum_fusion.2), channel_id=1, source_target_pairs={{0,4},{4,0},{8,12},{12,8},{16,20},{20,16},{24,28},{28,24},{1,5},{5... | collective-permute-start | bytes 1572872 | tf_op jit(solution)/shard_map/ppermute | solution.py:198
  8.2 17.0 %collective-permute-start.2 = (bf16[512,512]{1,0:T(8,128)(2,1)S(1)}, bf16[512,512]{1,0:T(8,128)(2,1)S(1)}, u32[]{:S(2)}, u32[]{:S(2)}) collective-permute-start(bf16[512,512]{1,0:T(8,128)(2,1)S(1)} %copy-done.4), channel_id=1, source_target_pairs={{0,8},{4,12},{8,0},{12,4},{16,24},{20,28},{24,16},{28,20},{1,9},{5... | collective-permute-start | bytes 1572872 | tf_op jit(solution)/shard_map/ppermute | solution.py:216
  9.8 15.8 %collective-permute-start.4 = (bf16[512,512]{1,0:T(8,128)(2,1)S(1)}, bf16[512,512]{1,0:T(8,128)(2,1)S(1)}, u32[]{:S(2)}, u32[]{:S(2)}) collective-permute-start(bf16[512,512]{1,0:T(8,128)(2,1)S(1)} %copy-done.4), channel_id=1, source_target_pairs={{8,16},{9,17},{10,18},{11,19},{12,20},{13,21},{14,22},{15,23},{16,... | collective-permute-start | bytes 1572872 | tf_op jit(solution)/shard_map/ppermute | solution.py:229
  9.8 5.0 %copy-start = (bf16[512,128]{1,0:T(8,128)(2,1)S(1)}, bf16[512,128]{1,0:T(8,128)(2,1)}, u32[]{:S(2)}) copy-start(bf16[512,128]{1,0:T(8,128)(2,1)} %value_ref.5) | copy-start | bytes 393220
  9.8 5.0 %copy-start.1 = (bf16[512,128]{1,0:T(8,128)(2,1)S(1)}, bf16[512,128]{1,0:T(8,128)(2,1)}, u32[]{:S(2)}) copy-start(bf16[512,128]{1,0:T(8,128)(2,1)} %key_ref.5) | copy-start | bytes 393220
  14.9 12.7 %collective-permute-start.1 = (bf16[528,256]{1,0:T(8,128)(2,1)S(1)}, bf16[528,256]{1,0:T(8,128)(2,1)S(1)}, u32[]{:S(2)}, u32[]{:S(2)}) collective-permute-start(bf16[528,256]{1,0:T(8,128)(2,1)S(1)} %broadcast_select_fusion.2), channel_id=1, source_target_pairs={{0,4},{4,0},{8,12},{12,8},{16,20},{20,16},{24,28},{28,24},{1,5},{5... | collective-permute-start | bytes 811016 | tf_op jit(solution)/shard_map/ppermute | solution.py:198
  21.6 14.9 %collective-permute-start.7 = (bf16[128,2048]{1,0:T(8,128)(2,1)S(1)}, bf16[128,2048]{1,0:T(8,128)(2,1)S(1)}, u32[]{:S(2)}, u32[]{:S(2)}) collective-permute-start(bf16[128,2048]{1,0:T(8,128)(2,1)S(1)} %collective-permute-done.3), channel_id=1, source_target_pairs={{0,1},{1,0},{2,3},{3,2},{4,5},{5,4},{6,7},{7,6},{8,9},{9,8},{10,11... | collective-permute-start | bytes 1572872 | tf_op jit(solution)/shard_map/ppermute | solution.py:208
  21.6 14.8 %collective-permute-start.8 = (bf16[128,2048]{1,0:T(8,128)(2,1)S(1)}, bf16[128,2048]{1,0:T(8,128)(2,1)S(1)}, u32[]{:S(2)}, u32[]{:S(2)}) collective-permute-start(bf16[128,2048]{1,0:T(8,128)(2,1)S(1)} %collective-permute-done.3), channel_id=1, source_target_pairs={{0,2},{1,3},{2,0},{3,1},{4,6},{5,7},{6,4},{7,5},{8,10},{9,11},{10,... | collective-permute-start | bytes 1572872 | tf_op jit(solution)/shard_map/ppermute | solution.py:208
  25.2 9.9 %collective-permute-start.5 = (bf16[512,512]{1,0:T(8,128)(2,1)S(1)}, bf16[512,512]{1,0:T(8,128)(2,1)S(1)}, u32[]{:S(2)}, u32[]{:S(2)}) collective-permute-start(bf16[512,512]{1,0:T(8,128)(2,1)S(1)} %collective-permute-done.2), channel_id=1, source_target_pairs={{8,16},{9,17},{10,18},{11,19},{12,20},{13,21},{14,22},{15,23},{16,... | collective-permute-start | bytes 1572872 | tf_op jit(solution)/shard_map/ppermute | solution.py:229
  25.6 2.0 %copy-start.5 = (s32[512]{0:T(512)S(1)}, s32[512]{0:T(512)}, u32[]{:S(2)}) copy-start(s32[512]{0:T(512)} %param.6) | copy-start | bytes 6148
  25.6 2.4 %copy-start.2 = (bf16[512,512]{1,0:T(8,128)(2,1)S(1)}, bf16[512,512]{1,0:T(8,128)(2,1)}, u32[]{:S(2)}) copy-start(bf16[512,512]{1,0:T(8,128)(2,1)} %query.5) | copy-start | bytes 1572868
  25.7 14.5 %collective-permute-start.11 = (bf16[512,512]{1,0:T(8,128)(2,1)S(1)}, bf16[512,512]{1,0:T(8,128)(2,1)S(1)}, u32[]{:S(2)}, u32[]{:S(2)}) collective-permute-start(bf16[512,512]{1,0:T(8,128)(2,1)S(1)} %collective-permute-done.4), channel_id=1, source_target_pairs={{0,8},{4,12},{8,0},{12,4},{16,24},{20,28},{24,16},{28,20},{1,9},{5... | collective-permute-start | bytes 1572872 | tf_op jit(solution)/shard_map/ppermute | solution.py:216
  32.2 13.4 %collective-permute-start.10 = (bf16[512,512]{1,0:T(8,128)(2,1)S(1)}, bf16[512,512]{1,0:T(8,128)(2,1)S(1)}, u32[]{:S(2)}, u32[]{:S(2)}) collective-permute-start(bf16[512,512]{1,0:T(8,128)(2,1)S(1)} %get-tuple-element.44.tokens.attended), channel_id=1, source_target_pairs={{0,4},{4,0},{8,12},{12,8},{16,20},{20,16},{24,28},{28,24},{1,5},{5... | collective-permute-start | bytes 1572872 | tf_op jit(solution)/shard_map/ppermute | solution.py:198
  35.1 16.2 %collective-permute-start.6 = (bf16[512,512]{1,0:T(8,128)(2,1)S(1)}, bf16[512,512]{1,0:T(8,128)(2,1)S(1)}, u32[]{:S(2)}, u32[]{:S(2)}) collective-permute-start(bf16[512,512]{1,0:T(8,128)(2,1)S(1)} %collective-permute-done.5), channel_id=1, source_target_pairs={{8,0},{12,4},{16,24},{20,28},{9,1},{13,5},{17,25},{21,29},{10,2},{... | collective-permute-start | bytes 1572872 | tf_op jit(solution)/shard_map/ppermute | solution.py:216
  36.4 9.2 %collective-permute-start.9 = (bf16[128,2048]{1,0:T(8,128)(2,1)S(1)}, bf16[128,2048]{1,0:T(8,128)(2,1)S(1)}, u32[]{:S(2)}, u32[]{:S(2)}) collective-permute-start(bf16[128,2048]{1,0:T(8,128)(2,1)S(1)} %collective-permute-done.8), channel_id=1, source_target_pairs={{0,1},{1,0},{2,3},{3,2},{4,5},{5,4},{6,7},{7,6},{8,9},{9,8},{10,11... | collective-permute-start | bytes 1572872 | tf_op jit(solution)/shard_map/ppermute | solution.py:208
  46.2 15.8 %collective-permute-start.18 = (bf16[512,512]{1,0:T(8,128)(2,1)S(1)}, bf16[512,512]{1,0:T(8,128)(2,1)S(1)}, u32[]{:S(2)}, u32[]{:S(2)}) collective-permute-start(bf16[512,512]{1,0:T(8,128)(2,1)S(1)} %fusion.3), channel_id=1, source_target_pairs={{0,8},{4,12},{24,16},{28,20},{1,9},{5,13},{25,17},{29,21},{2,10},{... | collective-permute-start | bytes 1572872 | tf_op jit(solution)/shard_map/ppermute | solution.py:216
  52.2 12.5 %collective-permute-start.17 = (bf16[512,512]{1,0:T(8,128)(2,1)S(1)}, bf16[512,512]{1,0:T(8,128)(2,1)S(1)}, u32[]{:S(2)}, u32[]{:S(2)}) collective-permute-start(bf16[512,512]{1,0:T(8,128)(2,1)S(1)} %fusion.2), channel_id=1, source_target_pairs={{0,4},{4,0},{8,12},{12,8},{16,20},{20,16},{24,28},{28,24},{1,5},{5... | collective-permute-start | bytes 1572872 | tf_op jit(solution)/shard_map/ppermute | solution.py:198
  55.6 6.7 %collective-permute-start.13 = (bf16[2,512,512]{2,1,0:T(8,128)(2,1)S(1)}, bf16[2,512,512]{2,1,0:T(8,128)(2,1)S(1)}, u32[]{:S(2)}, u32[]{:S(2)}) collective-permute-start(bf16[2,512,512]{2,1,0:T(8,128)(2,1)S(1)} %get-tuple-element.53), channel_id=1, source_target_pairs={{0,1},{1,0},{2,3},{3,2},{4,5},{5,4},{6,7},{7,6},{8,9},{9,8},{10,11... | collective-permute-start | bytes 3145736 | tf_op jit(solution)/shard_map/ppermute | solution.py:208
  57.0 15.8 %collective-permute-start.23 = (bf16[512,512]{1,0:T(8,128)(2,1)S(1)}, bf16[512,512]{1,0:T(8,128)(2,1)S(1)}, u32[]{:S(2)}, u32[]{:S(2)}) collective-permute-start(bf16[512,512]{1,0:T(8,128)(2,1)S(1)} %get-tuple-element.75), channel_id=1, source_target_pairs={{0,8},{4,12},{8,0},{12,4},{16,24},{20,28},{24,16},{28,20},{1,9},{5... | collective-permute-start | bytes 1572872 | tf_op jit(solution)/shard_map/ppermute | solution.py:216
  59.0 19.7 %collective-permute-start.12 = (bf16[2,512,512]{2,1,0:T(8,128)(2,1)S(1)}, bf16[2,512,512]{2,1,0:T(8,128)(2,1)S(1)}, u32[]{:S(2)}, u32[]{:S(2)}) collective-permute-start(bf16[2,512,512]{2,1,0:T(8,128)(2,1)S(1)} %get-tuple-element.50), channel_id=1, source_target_pairs={{0,1},{1,0},{2,3},{3,2},{4,5},{5,4},{6,7},{7,6},{8,9},{9,8},{10,11... | collective-permute-start | bytes 3145736 | tf_op jit(solution)/shard_map/ppermute | solution.py:208
  62.2 10.9 %collective-permute-start.21 = (bf16[512,512]{1,0:T(8,128)(2,1)S(1)}, bf16[512,512]{1,0:T(8,128)(2,1)S(1)}, u32[]{:S(2)}, u32[]{:S(2)}) collective-permute-start(bf16[512,512]{1,0:T(8,128)(2,1)S(1)} %add_convert_fusion.3), channel_id=1, source_target_pairs={{8,16},{9,17},{10,18},{11,19},{12,20},{13,21},{14,22},{15,23},{16,... | collective-permute-start | bytes 1572872 | tf_op jit(solution)/shard_map/ppermute | solution.py:229
  62.4 17.0 %collective-permute-start.15 = (bf16[512,512]{1,0:T(8,128)(2,1)S(1)}, bf16[512,512]{1,0:T(8,128)(2,1)S(1)}, u32[]{:S(2)}, u32[]{:S(2)}) collective-permute-start(bf16[512,512]{1,0:T(8,128)(2,1)S(1)} %fusion.18), channel_id=1, source_target_pairs={{0,2},{1,3},{2,0},{3,1},{4,6},{5,7},{6,4},{7,5},{8,10},{9,11},{10,... | collective-permute-start | bytes 1572872 | tf_op jit(solution)/shard_map/ppermute | solution.py:208
  73.0 16.5 %collective-permute-start.24 = (bf16[512,512]{1,0:T(8,128)(2,1)S(1)}, bf16[512,512]{1,0:T(8,128)(2,1)S(1)}, u32[]{:S(2)}, u32[]{:S(2)}) collective-permute-start(bf16[512,512]{1,0:T(8,128)(2,1)S(1)} %add_convert_fusion.1), channel_id=1, source_target_pairs={{8,16},{9,17},{10,18},{11,19},{12,20},{13,21},{14,22},{15,23},{16,... | collective-permute-start | bytes 1572872 | tf_op jit(solution)/shard_map/ppermute | solution.py:229
  73.3 16.8 %collective-permute-start.22 = (bf16[512,512]{1,0:T(8,128)(2,1)S(1)}, bf16[512,512]{1,0:T(8,128)(2,1)S(1)}, u32[]{:S(2)}, u32[]{:S(2)}) collective-permute-start(bf16[512,512]{1,0:T(8,128)(2,1)S(1)} %add_convert_fusion.2), channel_id=1, source_target_pairs={{0,8},{4,12},{8,0},{12,4},{16,24},{20,28},{24,16},{28,20},{1,9},{5... | collective-permute-start | bytes 1572872 | tf_op jit(solution)/shard_map/ppermute | solution.py:216
  77.3 9.2 %collective-permute-start.19 = (bf16[512,256]{1,0:T(8,128)(2,1)S(1)}, bf16[512,256]{1,0:T(8,128)(2,1)S(1)}, u32[]{:S(2)}, u32[]{:S(2)}) collective-permute-start(bf16[512,256]{1,0:T(8,128)(2,1)S(1)} %get-tuple-element.62), channel_id=1, source_target_pairs={{0,4},{4,0},{8,12},{12,8},{16,20},{20,16},{24,28},{28,24},{1,5},{5... | collective-permute-start | bytes 786440 | tf_op jit(solution)/shard_map/ppermute | solution.py:198
  78.8 12.3 %collective-permute-start.14 = (bf16[512,512]{1,0:T(8,128)(2,1)S(1)}, bf16[512,512]{1,0:T(8,128)(2,1)S(1)}, u32[]{:S(2)}, u32[]{:S(2)}) collective-permute-start(bf16[512,512]{1,0:T(8,128)(2,1)S(1)} %fusion.17), channel_id=1, source_target_pairs={{0,2},{1,3},{2,0},{3,1},{4,6},{5,7},{6,4},{7,5},{8,10},{9,11},{10,... | collective-permute-start | bytes 1572872 | tf_op jit(solution)/shard_map/ppermute | solution.py:208
  79.6 14.6 %collective-permute-start.16 = (bf16[512,512]{1,0:T(8,128)(2,1)S(1)}, bf16[512,512]{1,0:T(8,128)(2,1)S(1)}, u32[]{:S(2)}, u32[]{:S(2)}) collective-permute-start(bf16[512,512]{1,0:T(8,128)(2,1)S(1)} %fusion.14), channel_id=1, source_target_pairs={{0,4},{4,0},{8,12},{12,8},{16,20},{20,16},{24,28},{28,24},{1,5},{5... | collective-permute-start | bytes 1572872 | tf_op jit(solution)/shard_map/ppermute | solution.py:198
  86.6 6.8 %collective-permute-start.20 = (bf16[512,256]{1,0:T(8,128)(2,1)S(1)}, bf16[512,256]{1,0:T(8,128)(2,1)S(1)}, u32[]{:S(2)}, u32[]{:S(2)}) collective-permute-start(bf16[512,256]{1,0:T(8,128)(2,1)S(1)} %add_convert_fusion.7), channel_id=1, source_target_pairs={{0,24},{4,28},{8,0},{12,4},{16,8},{20,12},{24,16},{28,20},{1,25},{... | collective-permute-start | bytes 786440 | tf_op jit(solution)/shard_map/ppermute | solution.py:203
  94.3 1.0 %copy-start.3 = (bf16[512,1024]{1,0:T(8,128)(2,1)}, bf16[512,1024]{1,0:T(8,128)(2,1)S(1)}, u32[]{:S(2)}) copy-start(bf16[512,1024]{1,0:T(8,128)(2,1)S(1)} %constant_dynamic-update-slice_fusion.2) | copy-start | bytes 3145732

commit v5 on v4

--- a/solution.py
+++ b/solution.py
@@ -377,13 +377,10 @@
         other = jnp.where(end, 0, inner_swap(other))
         proj_grad = (wide[3] + nearer + other).astype(jnp.bfloat16)
     other_output, own_output = swap_pair(reduced[0]), reduced[1]
+    halves = [jnp.where(parity == 0, own_output, other_output), jnp.where(parity == 0, other_output, own_output)]
     if own_output.shape[1] == shard:
-        layer_output = jnp.zeros((rows, 2 * shard), own_output.dtype)
-        layer_output = lax.dynamic_update_slice(layer_output, own_output, (0, parity * shard))
-        other_output = after(other_output, layer_output)
-        layer_output = lax.dynamic_update_slice(layer_output, other_output, (0, (1 - parity) * shard))
-    else:
-        halves = [jnp.where(parity == 0, own_output, other_output), jnp.where(parity == 0, other_output, own_output)]
+        layer_output = jnp.concatenate(halves, 1)
+    else:
         layer_output = jnp.stack([half.reshape(rows, -1, shard) for half in halves], 2).reshape(rows, -1)
 
     arrived = shift_line(passed, -1)

time: 95.5 us -> 101 us (1.058)
  waiting for transfers between devices: 29.8 us -> 39.2 us
  starting transfers between devices: 32.1 us -> 28.2 us
  other arithmetic: 5.32 us -> 6.52 us
  local copies, waits for them, and re-layouts: 5.29 us -> 4.14 us
    ppermute x6, waiting for transfers between devices: 16 us -> 27.7 us  [swap_pair(): return lax.ppermute(value, 'ctx', [(i, i ^ 1) for i in range(devices)])]
    ppermute x6, waiting for transfers between devices: 8.72 us -> 5.22 us  [along_line(): return lax.ppermute(value, 'ctx', line_pairs(pairs))]
    ppermute x2, starting transfers between devices: 6.01 us -> 4.31 us  [shift_line(): lax.ppermute(value, 'ctx', [(i, (i + 2 * by) % devices) for i in range(de...]
    ppermute x2, waiting for transfers between devices: 5.1 us -> 6.31 us  [shift_line(): lax.ppermute(value, 'ctx', [(i, (i + 2 * by) % devices) for i in range(de...]
    ppermute x6, starting transfers between devices: 9.77 us -> 8.6 us  [swap_pair(): return lax.ppermute(value, 'ctx', [(i, i ^ 1) for i in range(devices)])]
    concatenate x0 -> x1, other arithmetic: none -> 1.1 us  [body(): layer_output = jnp.concatenate(halves, 1)]
  transfers between devices with their start and end apart: 25 -> 25, of which waited for: 11 -> 10; matrix products, arithmetic and copies ran while one was open for 14% -> 13% of each run, Pallas kernels for 17% -> 16%
where the time goes in v5:
time: 101 us
  waiting for transfers between devices  39.2 us (39%)
  starting transfers between devices  28.2 us (28%)
  Pallas kernels  16.1 us (16%)
  other arithmetic  6.52 us (6%)
  matrix products  5.64 us (6%)
  local copies, waits for them, and re-layouts  4.14 us (4%)
    ppermute x6, waiting for transfers between devices, swap_pair(): return lax.ppermute(value, 'ctx', [(i, i ^ 1) for i in range(devices)])  27.7 us
    ppermute x6, starting transfers between devices, along_line(): return lax.ppermute(value, 'ctx', line_pairs(pairs))  11.1 us
    ppermute x6, starting transfers between devices, swap_pair(): return lax.ppermute(value, 'ctx', [(i, i ^ 1) for i in range(devices)])  8.6 us
    pallas_call x2, Pallas kernels, attend_back(): pl.pallas_call(functools.partial(backward_kernel, halo), out_shape=outs,...  8.21 us
    ppermute x2, waiting for transfers between devices, shift_line(): lax.ppermute(value, 'ctx', [(i, (i + 2 * by) % devices) for i in range(de...  6.31 us
    ppermute x6, waiting for transfers between devices, along_line(): return lax.ppermute(value, 'ctx', line_pairs(pairs))  5.22 us
    ppermute x2, starting transfers between devices, shift_line(): lax.ppermute(value, 'ctx', [(i, (i + 2 * by) % devices) for i in range(de...  4.31 us
    pallas_call x1, Pallas kernels, attend(): pl.pallas_call(forward_kernel, out_shape=(jax.ShapeDtypeStruct((rows, col...  4.2 us
  transfers between devices with their start and end apart: 25, of which 10 were waited for; matrix products, arithmetic and copies ran while one was open for 13% of the time, Pallas kernels for 16%

profile of v5, /device:TPU:0, one launch (start us, length us, event | category | flops | bytes accessed | tf_op | source)
XLA Modules:
  0.0 100.7 jit_solution(10965744542381079607)
XLA Ops:
  0.6 0.7 convert_bitcast_fusion
  1.4 1.0 fusion.20
  2.4 3.1 %collective-permute-start = (bf16[528,256]{1,0:T(8,128)(2,1)S(1)}, bf16[528,256]{1,0:T(8,128)(2,1)S(1)}, u32[]{:S(2)}, u32[]{:S(2)}) collective-permute-start(bf16[528,256]{1,0:T(8,128)(2,1)S(1)} %fusion.20), channel_id=1, source_target_pairs={{0,8},{4,12},{8,16},{12,20},{16,24},{20,28},{24,0},{28,4},{1,9},{5... | collective-permute-start | bytes 811016 | tf_op jit(solution)/shard_map/ppermute | solution.py:203
  5.5 1.1 %fusion.24 = (bf16[128,512]{1,0:T(8,128)(2,1)S(1)}, bf16[128,512]{1,0:T(8,128)(2,1)S(1)}, bf16[128,512]{1,0:T(8,128)(2,1)S(1)}, bf16[128,512]{1,0:T(8,128)(2,1)S(1)}) fusion(bf16[512,4096]{1,0:T(8,128)(2,1)} %param.11, s32[]{:T(128)S(6)} %select_n.172, s32[]{:T(128)S(6)} %select_n.174, s32[]{:T(128)S(6)} %select_n.178, s32[]{:T(128)S(6)} %select_n.177, ...), kind=kLoop, calls=%fused_computation.66 | loop fusion | bytes 1048596 | tf_op jit(solution)/shard_map/dynamic_slice | solution.py:263
  6.7 0.1 collective-permute-start.4
  6.7 3.1 %collective-permute-start.2 = (bf16[512,512]{1,0:T(8,128)(2,1)S(1)}, bf16[512,512]{1,0:T(8,128)(2,1)S(1)}, u32[]{:S(2)}, u32[]{:S(2)}) collective-permute-start(bf16[512,512]{1,0:T(8,128)(2,1)S(1)} %copy-done.3), channel_id=1, source_target_pairs={{0,8},{4,12},{8,0},{12,4},{16,24},{20,28},{24,16},{28,20},{1,9},{5... | collective-permute-start | bytes 1572872 | tf_op jit(solution)/shard_map/ppermute | solution.py:216
  9.9 1.5 %collective-permute-start.3 = (bf16[128,2048]{1,0:T(8,128)(2,1)S(1)}, bf16[128,2048]{1,0:T(8,128)(2,1)S(1)}, u32[]{:S(2)}, u32[]{:S(2)}) collective-permute-start(bf16[128,2048]{1,0:T(8,128)(2,1)S(1)} %pad_maximum_fusion.3), channel_id=1, source_target_pairs={{0,4},{4,0},{8,12},{12,8},{16,20},{20,16},{24,28},{28,24},{1,5},{5... | collective-permute-start | bytes 1572872 | tf_op jit(solution)/shard_map/ppermute | solution.py:198
  11.4 1.7 %constant_dynamic-slice_fusion.3 = (bf16[512,512]{1,0:T(8,128)(2,1)S(1)}, bf16[512,512]{1,0:T(8,128)(2,1)S(1)}, bf16[512,512]{1,0:T(8,128)(2,1)S(1)}, bf16[512,512]{1,0:T(8,128)(2,1)S(1)}) fusion(bf16[512,4096]{1,0:T(8,128)(2,1)} %param.11, s32[]{:T(128)S(6)} %select_n.179, s32[]{:T(128)S(6)} %select_n.182, s32[]{:T(128)S(6)} %select_n.181, s32[]{:T(128)S(6)} %select_n.180), kind=kLoop, calls=%fused_computation.59 | loop fusion | bytes 4194320 | tf_op jit(solution)/shard_map/dynamic_slice | solution.py:263
  13.1 0.1 pad_add_fusion.1.slots
  13.2 1.6 %collective-permute-done.kv2 = bf16[528,256]{1,0:T(8,128)(2,1)S(1)} collective-permute-done((bf16[528,256]{1,0:T(8,128)(2,1)S(1)}, bf16[528,256]{1,0:T(8,128)(2,1)S(1)}, u32[]{:S(2)}, u32[]{:S(2)}) %collective-permute-start) | collective-permute-done | bytes 270368 | tf_op jit(solution)/shard_map/ppermute | solution.py:203
  14.9 0.1 broadcast_select_fusion.4
  14.9 1.8 %collective-permute-start.1 = (bf16[528,256]{1,0:T(8,128)(2,1)S(1)}, bf16[528,256]{1,0:T(8,128)(2,1)S(1)}, u32[]{:S(2)}, u32[]{:S(2)}) collective-permute-start(bf16[528,256]{1,0:T(8,128)(2,1)S(1)} %broadcast_select_fusion.4), channel_id=1, source_target_pairs={{0,4},{4,0},{8,12},{12,8},{16,20},{20,16},{24,28},{28,24},{1,5},{5... | collective-permute-start | bytes 811016 | tf_op jit(solution)/shard_map/ppermute | solution.py:198
  16.8 8.0 %collective-permute-done.3 = bf16[128,2048]{1,0:T(8,128)(2,1)S(1)} collective-permute-done((bf16[128,2048]{1,0:T(8,128)(2,1)S(1)}, bf16[128,2048]{1,0:T(8,128)(2,1)S(1)}, u32[]{:S(2)}, u32[]{:S(2)}) %collective-permute-start.3) | collective-permute-done | bytes 524320 | tf_op jit(solution)/shard_map/ppermute | solution.py:198
  24.7 1.5 %collective-permute-start.8 = (bf16[128,2048]{1,0:T(8,128)(2,1)S(1)}, bf16[128,2048]{1,0:T(8,128)(2,1)S(1)}, u32[]{:S(2)}, u32[]{:S(2)}) collective-permute-start(bf16[128,2048]{1,0:T(8,128)(2,1)S(1)} %collective-permute-done.3), channel_id=1, source_target_pairs={{0,2},{1,3},{2,0},{3,1},{4,6},{5,7},{6,4},{7,5},{8,10},{9,11},{10,... | collective-permute-start | bytes 1572872 | tf_op jit(solution)/shard_map/ppermute | solution.py:208
  26.2 0.5 collective-permute-start.5
  26.8 0.1 collective-permute-start.11
  26.9 0.2 broadcast_in_dim.26
  27.3 0.7 fusion.7
  28.0 0.5 collective-permute-done.1.kv1
  28.5 0.4 convert_reduce_fusion
  28.9 4.2 %attend.1 = (bf16[512,512]{1,0:T(8,128)(2,1)S(1)}, f32[4,512]{1,0:T(4,128)S(1)}) custom-call(s32[1,512]{1,0:T(1,128)S(1)} %bitcast.32, bf16[512,512]{1,0:T(8,128)(2,1)S(1)} %copy-done.2, bf16[528,256]{1,0:T(8,128)(2,1)S(1)} %collective-permute-done.kv2, bf16[528,256]{1,0:T(8,128)(2,1)S(1)} %collective-permute-done.1.kv1, bf16[512,128]{1,0:T(8,128)(2,1)S(1)} %copy-done.1, ...), custom_call_target="tpu_custom_call" | custom-call | flops 1610612736 | bytes 1048576 | tf_op jit(solution)/shard_map/attend/pallas_call | solution.py:131
  33.1 1.6 %collective-permute-start.10 = (bf16[512,512]{1,0:T(8,128)(2,1)S(1)}, bf16[512,512]{1,0:T(8,128)(2,1)S(1)}, u32[]{:S(2)}, u32[]{:S(2)}) collective-permute-start(bf16[512,512]{1,0:T(8,128)(2,1)S(1)} %get-tuple-element.43.tokens.attended), channel_id=1, source_target_pairs={{0,4},{4,0},{8,12},{12,8},{16,20},{20,16},{24,28},{28,24},{1,5},{5... | collective-permute-start | bytes 1572872 | tf_op jit(solution)/shard_map/ppermute | solution.py:198
  34.7 1.3 %fusion.23 = f32[2048,512]{1,0:T(8,128)S(1)} fusion(bf16[512,512]{1,0:T(8,128)(2,1)S(1)} %get-tuple-element.43.tokens.attended, bf16[512,512]{1,0:T(8,128)(2,1)S(1)} %get-tuple-element.66, bf16[512,512]{1,0:T(8,128)(2,1)S(1)} %get-tuple-element.67, bf16[512,512]{1,0:T(8,128)(2,1)S(1)} %get-tuple-element.68, bf16[512,512]{1,0:T(8,128)(2,1)S(1)} %get-tuple-element.65), kind=kOutput, calls=%fused_computation.65 | convolution fusion | flops 1082130432 | bytes 6815744 | tf_op jit(solution)/shard_map/dot_general | solution.py:29
  36.0 1.3 %collective-permute-start.6 = (bf16[512,512]{1,0:T(8,128)(2,1)S(1)}, bf16[512,512]{1,0:T(8,128)(2,1)S(1)}, u32[]{:S(2)}, u32[]{:S(2)}) collective-permute-start(bf16[512,512]{1,0:T(8,128)(2,1)S(1)} %collective-permute-done.5), channel_id=1, source_target_pairs={{8,0},{12,4},{16,24},{20,28},{9,1},{13,5},{17,25},{21,29},{10,2},{... | collective-permute-start | bytes 1572872 | tf_op jit(solution)/shard_map/ppermute | solution.py:216
  37.5 3.2 %collective-permute-done.11 = bf16[512,512]{1,0:T(8,128)(2,1)S(1)} collective-permute-done((bf16[512,512]{1,0:T(8,128)(2,1)S(1)}, bf16[512,512]{1,0:T(8,128)(2,1)S(1)}, u32[]{:S(2)}, u32[]{:S(2)}) %collective-permute-start.11) | collective-permute-done | bytes 524320 | tf_op jit(solution)/shard_map/ppermute | solution.py:216
  40.7 0.1 broadcast_select_fusion
  40.8 5.7 %collective-permute-done.10.tokens = bf16[512,512]{1,0:T(8,128)(2,1)S(1)} collective-permute-done((bf16[512,512]{1,0:T(8,128)(2,1)S(1)}, bf16[512,512]{1,0:T(8,128)(2,1)S(1)}, u32[]{:S(2)}, u32[]{:S(2)}) %collective-permute-start.10) | collective-permute-done | bytes 524320 | tf_op jit(solution)/shard_map/ppermute | solution.py:198
  46.6 0.5 fusion.3
  47.1 3.8 %collective-permute-start.18 = (bf16[512,512]{1,0:T(8,128)(2,1)S(1)}, bf16[512,512]{1,0:T(8,128)(2,1)S(1)}, u32[]{:S(2)}, u32[]{:S(2)}) collective-permute-start(bf16[512,512]{1,0:T(8,128)(2,1)S(1)} %fusion.3), channel_id=1, source_target_pairs={{0,8},{4,12},{24,16},{28,20},{1,9},{5,13},{25,17},{29,21},{2,10},{... | collective-permute-start | bytes 1572872 | tf_op jit(solution)/shard_map/ppermute | solution.py:216
  50.9 0.7 fusion.4
  51.6 2.0 %collective-permute-done.6 = bf16[512,512]{1,0:T(8,128)(2,1)S(1)} collective-permute-done((bf16[512,512]{1,0:T(8,128)(2,1)S(1)}, bf16[512,512]{1,0:T(8,128)(2,1)S(1)}, u32[]{:S(2)}, u32[]{:S(2)}) %collective-permute-start.6) | collective-permute-done | bytes 524320 | tf_op jit(solution)/shard_map/ppermute | solution.py:216
  53.8 0.7 fusion.2
  54.5 1.6 %collective-permute-start.17 = (bf16[512,512]{1,0:T(8,128)(2,1)S(1)}, bf16[512,512]{1,0:T(8,128)(2,1)S(1)}, u32[]{:S(2)}, u32[]{:S(2)}) collective-permute-start(bf16[512,512]{1,0:T(8,128)(2,1)S(1)} %fusion.2), channel_id=1, source_target_pairs={{0,4},{4,0},{8,12},{12,8},{16,20},{20,16},{24,28},{28,24},{1,5},{5... | collective-permute-start | bytes 1572872 | tf_op jit(solution)/shard_map/ppermute | solution.py:198
  56.1 1.8 %output_parts.3 = (bf16[2,512,512]{2,1,0:T(8,128)(2,1)S(1)}, bf16[2,512,512]{2,1,0:T(8,128)(2,1)S(1)}) custom-call(s32[3]{0:T(128)S(1)} %pad_add_fusion.1.slots, bf16[512,512]{1,0:T(8,128)(2,1)S(1)} %collective-permute-done.10.tokens, bf16[1024,512]{1,0:T(8,128)(2,1)S(1)} %pad_maximum_fusion.1.late, bf16[1024,512]{1,0:T(8,128)(2,1)S(1)} %constant_dynamic-update-slice_fusion.early), custom_call_target="tpu_custom_call" | custom-call | flops 1073741824 | bytes 8388608 | tf_op jit(solution)/shard_map/output_parts/pallas_call | solution.py:183
  58.0 1.1 %fusion = bf16[1536,512]{1,0:T(8,128)(2,1)S(1)} fusion(bf16[512,512]{1,0:T(8,128)(2,1)S(1)} %collective-permute-done.10.tokens, f32[2048,512]{1,0:T(8,128)S(1)} %fusion.23, bf16[512,2048]{1,0:T(8,128)(2,1)S(1)} %constant_dynamic-update-slice_fusion.2), kind=kOutput, calls=%fused_computation.2 | convolution fusion | flops 806879232 | bytes 6815744 | tf_op jit(solution)/shard_map/dot_general | solution.py:29
  59.1 1.8 %output_parts.2 = (bf16[2,512,512]{2,1,0:T(8,128)(2,1)S(1)}, bf16[2,512,512]{2,1,0:T(8,128)(2,1)S(1)}) custom-call(s32[3]{0:T(128)S(1)} %pad_add_fusion.1.slots, bf16[512,512]{1,0:T(8,128)(2,1)S(1)} %get-tuple-element.43.tokens.attended, bf16[1024,512]{1,0:T(8,128)(2,1)S(1)} %pad_maximum_fusion.1.late, ...), custom_call_target="tpu_custom_call" | custom-call | flops 1073741824 | bytes 8388608 | tf_op jit(solution)/shard_map/output_parts/pallas_call | solution.py:183
  60.9 0.6 collective-permute-start.12
  61.5 0.3 fusion.25
  61.9 0.7 convolution_add_fusion.1.own_grad
  62.6 0.1 add_convert_fusion.3
  62.7 0.1 collective-permute-start.21
  62.8 0.1 fusion.18
  63.0 0.6 collective-permute-start.15
  63.6 4.0 %collective-permute-done.17.pair_grad = bf16[512,512]{1,0:T(8,128)(2,1)S(1)} collective-permute-done((bf16[512,512]{1,0:T(8,128)(2,1)S(1)}, bf16[512,512]{1,0:T(8,128)(2,1)S(1)}, u32[]{:S(2)}, u32[]{:S(2)}) %collective-permute-start.17) | collective-permute-done | bytes 524320 | tf_op jit(solution)/shard_map/ppermute | solution.py:198
  67.6 4.8 %attend_back_halo.1 = (f32[512,512]{1,0:T(8,128)S(1)}, bf16[512,256]{1,0:T(8,128)(2,1)S(1)}, bf16[512,256]{1,0:T(8,128)(2,1)S(1)}) custom-call(s32[1,512]{1,0:T(1,128)S(1)} %bitcast.33, f32[4,512]{1,0:T(4,128)S(1)} %get-tuple-element.54.log_total, bf16[512,512]{1,0:T(8,128)(2,1)S(1)} %copy-done.2, bf16[528,256]{1,0:T(8,128)(2,1)S(1)} %collective-permute-done.kv2, ...), custom_call_target="tpu_custom_call" | custom-call | flops 2013265920 | bytes 2621440 | tf_op jit(solution)/shard_map/attend_back_halo/pallas_call | solution.py:157
  72.4 3.4 %attend_back_own.1 = (bf16[512,512]{1,0:T(8,128)(2,1)}, f32[512,256]{1,0:T(8,128)S(1)}) custom-call(s32[1,512]{1,0:T(1,128)S(1)} %bitcast.34, f32[4,512]{1,0:T(4,128)S(1)} %get-tuple-element.54.log_total, bf16[512,512]{1,0:T(8,128)(2,1)S(1)} %copy-done.2, bf16[528,256]{1,0:T(8,128)(2,1)S(1)} %collective-permute-done.kv2, ...), custom_call_target="tpu_custom_call" | custom-call | flops 2013265920 | bytes 2621440 | tf_op jit(solution)/shard_map/attend_back_own/pallas_call | solution.py:157
  75.8 0.2 add_convert_fusion.2
  76.0 2.7 %collective-permute-start.22 = (bf16[512,512]{1,0:T(8,128)(2,1)S(1)}, bf16[512,512]{1,0:T(8,128)(2,1)S(1)}, u32[]{:S(2)}, u32[]{:S(2)}) collective-permute-start(bf16[512,512]{1,0:T(8,128)(2,1)S(1)} %add_convert_fusion.2), channel_id=1, source_target_pairs={{0,8},{4,12},{8,0},{12,4},{16,24},{20,28},{24,16},{28,20},{1,9},{5... | collective-permute-start | bytes 1572872 | tf_op jit(solution)/shard_map/ppermute | solution.py:216
  78.6 0.2 add_convert_fusion.1
  78.9 0.1 fusion.17
  79.0 0.6 collective-permute-start.14
  79.6 0.5 collective-permute-start.19
  80.1 0.2 fusion.14
  80.4 1.6 %collective-permute-start.16 = (bf16[512,512]{1,0:T(8,128)(2,1)S(1)}, bf16[512,512]{1,0:T(8,128)(2,1)S(1)}, u32[]{:S(2)}, u32[]{:S(2)}) collective-permute-start(bf16[512,512]{1,0:T(8,128)(2,1)S(1)} %fusion.14), channel_id=1, source_target_pairs={{0,4},{4,0},{8,12},{12,8},{16,20},{20,16},{24,28},{28,24},{1,5},{5... | collective-permute-start | bytes 1572872 | tf_op jit(solution)/shard_map/ppermute | solution.py:198
  82.0 6.8 %collective-permute-done.19 = bf16[512,256]{1,0:T(8,128)(2,1)S(1)} collective-permute-done((bf16[512,256]{1,0:T(8,128)(2,1)S(1)}, bf16[512,256]{1,0:T(8,128)(2,1)S(1)}, u32[]{:S(2)}, u32[]{:S(2)}) %collective-permute-start.19) | collective-permute-done | bytes 262176 | tf_op jit(solution)/shard_map/ppermute | solution.py:198
  88.8 0.1 add_convert_fusion.7
  88.9 1.2 %collective-permute-start.20 = (bf16[512,256]{1,0:T(8,128)(2,1)S(1)}, bf16[512,256]{1,0:T(8,128)(2,1)S(1)}, u32[]{:S(2)}, u32[]{:S(2)}) collective-permute-start(bf16[512,256]{1,0:T(8,128)(2,1)S(1)} %add_convert_fusion.7), channel_id=1, source_target_pairs={{0,24},{4,28},{8,0},{12,4},{16,8},{20,12},{24,16},{28,20},{1,25},{... | collective-permute-start | bytes 786440 | tf_op jit(solution)/shard_map/ppermute | solution.py:203
  90.1 1.0 %add_convert_fusion = bf16[512,512]{1,0:T(8,128)(2,1)} fusion(bf16[512,512]{1,0:T(8,128)(2,1)S(1)} %collective-permute-done.22, bf16[1536,512]{1,0:T(8,128)(2,1)S(1)} %fusion, bf16[512,512]{1,0:T(8,128)(2,1)S(1)} %collective-permute-done.24, pred[]{:T(512)S(6)} %or.3), kind=kLoop, calls=%fused_computation.26 | loop fusion | flops 1835008 | bytes 2097153 | tf_op jit(solution)/shard_map/convert_element_type | solution.py:378
  91.1 4.7 %collective-permute-done.20 = bf16[512,256]{1,0:T(8,128)(2,1)S(1)} collective-permute-done((bf16[512,256]{1,0:T(8,128)(2,1)S(1)}, bf16[512,256]{1,0:T(8,128)(2,1)S(1)}, u32[]{:S(2)}, u32[]{:S(2)}) %collective-permute-start.20) | collective-permute-done | bytes 262176 | tf_op jit(solution)/shard_map/ppermute | solution.py:203
  95.8 0.1 add_convert_fusion.6
  95.9 0.7 fusion.26
  96.7 2.6 %collective-permute-done.16 = bf16[512,512]{1,0:T(8,128)(2,1)S(1)} collective-permute-done((bf16[512,512]{1,0:T(8,128)(2,1)S(1)}, bf16[512,512]{1,0:T(8,128)(2,1)S(1)}, u32[]{:S(2)}, u32[]{:S(2)}) %collective-permute-start.16) | collective-permute-done | bytes 524320 | tf_op jit(solution)/shard_map/ppermute | solution.py:198
  99.3 0.3 broadcast_select_fusion.3
  99.6 1.1 %pad_maximum_fusion.2 = bf16[512,1024]{1,0:T(8,128)(2,1)} fusion(bf16[512,512]{1,0:T(8,128)(2,1)S(1)} %get-tuple-element.74, bf16[512,512]{1,0:T(8,128)(2,1)S(1)} %get-tuple-element.73), kind=kLoop, calls=%fused_computation.18 | loop fusion | flops 2097152 | bytes 2097152 | tf_op jit(solution)/shard_map/concatenate | solution.py:382
  (42 shorter events, 0.9 us)
Async XLA Ops:
  0.6 6.0 %copy-start.3 = (bf16[512,512]{1,0:T(8,128)(2,1)S(1)}, bf16[512,512]{1,0:T(8,128)(2,1)}, u32[]{:S(2)}) copy-start(bf16[512,512]{1,0:T(8,128)(2,1)} %param.10) | copy-start | bytes 1572868
  2.4 12.5 %collective-permute-start = (bf16[528,256]{1,0:T(8,128)(2,1)S(1)}, bf16[528,256]{1,0:T(8,128)(2,1)S(1)}, u32[]{:S(2)}, u32[]{:S(2)}) collective-permute-start(bf16[528,256]{1,0:T(8,128)(2,1)S(1)} %fusion.20), channel_id=1, source_target_pairs={{0,8},{4,12},{8,16},{12,20},{16,24},{20,28},{24,0},{28,4},{1,9},{5... | collective-permute-start | bytes 811016 | tf_op jit(solution)/shard_map/ppermute | solution.py:203
  6.7 20.1 %collective-permute-start.4 = (bf16[512,512]{1,0:T(8,128)(2,1)S(1)}, bf16[512,512]{1,0:T(8,128)(2,1)S(1)}, u32[]{:S(2)}, u32[]{:S(2)}) collective-permute-start(bf16[512,512]{1,0:T(8,128)(2,1)S(1)} %copy-done.3), channel_id=1, source_target_pairs={{8,16},{9,17},{10,18},{11,19},{12,20},{13,21},{14,22},{15,23},{16,... | collective-permute-start | bytes 1572872 | tf_op jit(solution)/shard_map/ppermute | solution.py:229
  6.7 19.5 %collective-permute-start.2 = (bf16[512,512]{1,0:T(8,128)(2,1)S(1)}, bf16[512,512]{1,0:T(8,128)(2,1)S(1)}, u32[]{:S(2)}, u32[]{:S(2)}) collective-permute-start(bf16[512,512]{1,0:T(8,128)(2,1)S(1)} %copy-done.3), channel_id=1, source_target_pairs={{0,8},{4,12},{8,0},{12,4},{16,24},{20,28},{24,16},{28,20},{1,9},{5... | collective-permute-start | bytes 1572872 | tf_op jit(solution)/shard_map/ppermute | solution.py:216
  9.9 14.9 %collective-permute-start.3 = (bf16[128,2048]{1,0:T(8,128)(2,1)S(1)}, bf16[128,2048]{1,0:T(8,128)(2,1)S(1)}, u32[]{:S(2)}, u32[]{:S(2)}) collective-permute-start(bf16[128,2048]{1,0:T(8,128)(2,1)S(1)} %pad_maximum_fusion.3), channel_id=1, source_target_pairs={{0,4},{4,0},{8,12},{12,8},{16,20},{20,16},{24,28},{28,24},{1,5},{5... | collective-permute-start | bytes 1572872 | tf_op jit(solution)/shard_map/ppermute | solution.py:198
  11.4 3.4 %copy-start = (bf16[512,128]{1,0:T(8,128)(2,1)S(1)}, bf16[512,128]{1,0:T(8,128)(2,1)}, u32[]{:S(2)}) copy-start(bf16[512,128]{1,0:T(8,128)(2,1)} %value_ref.5) | copy-start | bytes 393220
  11.4 3.4 %copy-start.1 = (bf16[512,128]{1,0:T(8,128)(2,1)S(1)}, bf16[512,128]{1,0:T(8,128)(2,1)}, u32[]{:S(2)}) copy-start(bf16[512,128]{1,0:T(8,128)(2,1)} %key_ref.5) | copy-start | bytes 393220
  14.9 13.6 %collective-permute-start.1 = (bf16[528,256]{1,0:T(8,128)(2,1)S(1)}, bf16[528,256]{1,0:T(8,128)(2,1)S(1)}, u32[]{:S(2)}, u32[]{:S(2)}) collective-permute-start(bf16[528,256]{1,0:T(8,128)(2,1)S(1)} %broadcast_select_fusion.4), channel_id=1, source_target_pairs={{0,4},{4,0},{8,12},{12,8},{16,20},{20,16},{24,28},{28,24},{1,5},{5... | collective-permute-start | bytes 811016 | tf_op jit(solution)/shard_map/ppermute | solution.py:198
  24.7 12.5 %collective-permute-start.8 = (bf16[128,2048]{1,0:T(8,128)(2,1)S(1)}, bf16[128,2048]{1,0:T(8,128)(2,1)S(1)}, u32[]{:S(2)}, u32[]{:S(2)}) collective-permute-start(bf16[128,2048]{1,0:T(8,128)(2,1)S(1)} %collective-permute-done.3), channel_id=1, source_target_pairs={{0,2},{1,3},{2,0},{3,1},{4,6},{5,7},{6,4},{7,5},{8,10},{9,11},{10,... | collective-permute-start | bytes 1572872 | tf_op jit(solution)/shard_map/ppermute | solution.py:208
  26.2 11.1 %collective-permute-start.7 = (bf16[128,2048]{1,0:T(8,128)(2,1)S(1)}, bf16[128,2048]{1,0:T(8,128)(2,1)S(1)}, u32[]{:S(2)}, u32[]{:S(2)}) collective-permute-start(bf16[128,2048]{1,0:T(8,128)(2,1)S(1)} %collective-permute-done.3), channel_id=1, source_target_pairs={{0,1},{1,0},{2,3},{3,2},{4,5},{5,4},{6,7},{7,6},{8,9},{9,8},{10,11... | collective-permute-start | bytes 1572872 | tf_op jit(solution)/shard_map/ppermute | solution.py:208
  26.2 9.7 %collective-permute-start.5 = (bf16[512,512]{1,0:T(8,128)(2,1)S(1)}, bf16[512,512]{1,0:T(8,128)(2,1)S(1)}, u32[]{:S(2)}, u32[]{:S(2)}) collective-permute-start(bf16[512,512]{1,0:T(8,128)(2,1)S(1)} %collective-permute-done.2), channel_id=1, source_target_pairs={{8,16},{9,17},{10,18},{11,19},{12,20},{13,21},{14,22},{15,23},{16,... | collective-permute-start | bytes 1572872 | tf_op jit(solution)/shard_map/ppermute | solution.py:229
  26.8 13.9 %collective-permute-start.11 = (bf16[512,512]{1,0:T(8,128)(2,1)S(1)}, bf16[512,512]{1,0:T(8,128)(2,1)S(1)}, u32[]{:S(2)}, u32[]{:S(2)}) collective-permute-start(bf16[512,512]{1,0:T(8,128)(2,1)S(1)} %collective-permute-done.4), channel_id=1, source_target_pairs={{0,8},{4,12},{8,0},{12,4},{16,24},{20,28},{24,16},{28,20},{1,9},{5... | collective-permute-start | bytes 1572872 | tf_op jit(solution)/shard_map/ppermute | solution.py:216
  27.2 1.3 %copy-start.4 = (s32[512]{0:T(512)S(1)}, s32[512]{0:T(512)}, u32[]{:S(2)}) copy-start(s32[512]{0:T(512)} %param.6) | copy-start | bytes 6148
  27.3 1.6 %copy-start.2 = (bf16[512,512]{1,0:T(8,128)(2,1)S(1)}, bf16[512,512]{1,0:T(8,128)(2,1)}, u32[]{:S(2)}) copy-start(bf16[512,512]{1,0:T(8,128)(2,1)} %query.5) | copy-start | bytes 1572868
  33.1 13.4 %collective-permute-start.10 = (bf16[512,512]{1,0:T(8,128)(2,1)S(1)}, bf16[512,512]{1,0:T(8,128)(2,1)S(1)}, u32[]{:S(2)}, u32[]{:S(2)}) collective-permute-start(bf16[512,512]{1,0:T(8,128)(2,1)S(1)} %get-tuple-element.43.tokens.attended), channel_id=1, source_target_pairs={{0,4},{4,0},{8,12},{12,8},{16,20},{20,16},{24,28},{28,24},{1,5},{5... | collective-permute-start | bytes 1572872 | tf_op jit(solution)/shard_map/ppermute | solution.py:198
  36.0 17.7 %collective-permute-start.6 = (bf16[512,512]{1,0:T(8,128)(2,1)S(1)}, bf16[512,512]{1,0:T(8,128)(2,1)S(1)}, u32[]{:S(2)}, u32[]{:S(2)}) collective-permute-start(bf16[512,512]{1,0:T(8,128)(2,1)S(1)} %collective-permute-done.5), channel_id=1, source_target_pairs={{8,0},{12,4},{16,24},{20,28},{9,1},{13,5},{17,25},{21,29},{10,2},{... | collective-permute-start | bytes 1572872 | tf_op jit(solution)/shard_map/ppermute | solution.py:216
  37.3 9.2 %collective-permute-start.9 = (bf16[128,2048]{1,0:T(8,128)(2,1)S(1)}, bf16[128,2048]{1,0:T(8,128)(2,1)S(1)}, u32[]{:S(2)}, u32[]{:S(2)}) collective-permute-start(bf16[128,2048]{1,0:T(8,128)(2,1)S(1)} %collective-permute-done.8), channel_id=1, source_target_pairs={{0,1},{1,0},{2,3},{3,2},{4,5},{5,4},{6,7},{7,6},{8,9},{9,8},{10,11... | collective-permute-start | bytes 1572872 | tf_op jit(solution)/shard_map/ppermute | solution.py:208
  47.1 15.5 %collective-permute-start.18 = (bf16[512,512]{1,0:T(8,128)(2,1)S(1)}, bf16[512,512]{1,0:T(8,128)(2,1)S(1)}, u32[]{:S(2)}, u32[]{:S(2)}) collective-permute-start(bf16[512,512]{1,0:T(8,128)(2,1)S(1)} %fusion.3), channel_id=1, source_target_pairs={{0,8},{4,12},{24,16},{28,20},{1,9},{5,13},{25,17},{29,21},{2,10},{... | collective-permute-start | bytes 1572872 | tf_op jit(solution)/shard_map/ppermute | solution.py:216
  54.5 13.0 %collective-permute-start.17 = (bf16[512,512]{1,0:T(8,128)(2,1)S(1)}, bf16[512,512]{1,0:T(8,128)(2,1)S(1)}, u32[]{:S(2)}, u32[]{:S(2)}) collective-permute-start(bf16[512,512]{1,0:T(8,128)(2,1)S(1)} %fusion.2), channel_id=1, source_target_pairs={{0,4},{4,0},{8,12},{12,8},{16,20},{20,16},{24,28},{28,24},{1,5},{5... | collective-permute-start | bytes 1572872 | tf_op jit(solution)/shard_map/ppermute | solution.py:198
  57.9 4.9 %collective-permute-start.13 = (bf16[2,512,512]{2,1,0:T(8,128)(2,1)S(1)}, bf16[2,512,512]{2,1,0:T(8,128)(2,1)S(1)}, u32[]{:S(2)}, u32[]{:S(2)}) collective-permute-start(bf16[2,512,512]{2,1,0:T(8,128)(2,1)S(1)} %get-tuple-element.52), channel_id=1, source_target_pairs={{0,1},{1,0},{2,3},{3,2},{4,5},{5,4},{6,7},{7,6},{8,9},{9,8},{10,11... | collective-permute-start | bytes 3145736 | tf_op jit(solution)/shard_map/ppermute | solution.py:208
  60.9 18.0 %collective-permute-start.12 = (bf16[2,512,512]{2,1,0:T(8,128)(2,1)S(1)}, bf16[2,512,512]{2,1,0:T(8,128)(2,1)S(1)}, u32[]{:S(2)}, u32[]{:S(2)}) collective-permute-start(bf16[2,512,512]{2,1,0:T(8,128)(2,1)S(1)} %get-tuple-element.49), channel_id=1, source_target_pairs={{0,1},{1,0},{2,3},{3,2},{4,5},{5,4},{6,7},{7,6},{8,9},{9,8},{10,11... | collective-permute-start | bytes 3145736 | tf_op jit(solution)/shard_map/ppermute | solution.py:208
  61.8 16.8 %collective-permute-start.23 = (bf16[512,512]{1,0:T(8,128)(2,1)S(1)}, bf16[512,512]{1,0:T(8,128)(2,1)S(1)}, u32[]{:S(2)}, u32[]{:S(2)}) collective-permute-start(bf16[512,512]{1,0:T(8,128)(2,1)S(1)} %get-tuple-element.75), channel_id=1, source_target_pairs={{0,8},{4,12},{8,0},{12,4},{16,24},{20,28},{24,16},{28,20},{1,9},{5... | collective-permute-start | bytes 1572872 | tf_op jit(solution)/shard_map/ppermute | solution.py:216
  62.7 13.0 %collective-permute-start.21 = (bf16[512,512]{1,0:T(8,128)(2,1)S(1)}, bf16[512,512]{1,0:T(8,128)(2,1)S(1)}, u32[]{:S(2)}, u32[]{:S(2)}) collective-permute-start(bf16[512,512]{1,0:T(8,128)(2,1)S(1)} %add_convert_fusion.3), channel_id=1, source_target_pairs={{8,16},{9,17},{10,18},{11,19},{12,20},{13,21},{14,22},{15,23},{16,... | collective-permute-start | bytes 1572872 | tf_op jit(solution)/shard_map/ppermute | solution.py:229
  63.0 17.2 %collective-permute-start.15 = (bf16[512,512]{1,0:T(8,128)(2,1)S(1)}, bf16[512,512]{1,0:T(8,128)(2,1)S(1)}, u32[]{:S(2)}, u32[]{:S(2)}) collective-permute-start(bf16[512,512]{1,0:T(8,128)(2,1)S(1)} %fusion.18), channel_id=1, source_target_pairs={{0,2},{1,3},{2,0},{3,1},{4,6},{5,7},{6,4},{7,5},{8,10},{9,11},{10,... | collective-permute-start | bytes 1572872 | tf_op jit(solution)/shard_map/ppermute | solution.py:208
  76.0 14.2 %collective-permute-start.22 = (bf16[512,512]{1,0:T(8,128)(2,1)S(1)}, bf16[512,512]{1,0:T(8,128)(2,1)S(1)}, u32[]{:S(2)}, u32[]{:S(2)}) collective-permute-start(bf16[512,512]{1,0:T(8,128)(2,1)S(1)} %add_convert_fusion.2), channel_id=1, source_target_pairs={{0,8},{4,12},{8,0},{12,4},{16,24},{20,28},{24,16},{28,20},{1,9},{5... | collective-permute-start | bytes 1572872 | tf_op jit(solution)/shard_map/ppermute | solution.py:216
  78.8 11.3 %collective-permute-start.24 = (bf16[512,512]{1,0:T(8,128)(2,1)S(1)}, bf16[512,512]{1,0:T(8,128)(2,1)S(1)}, u32[]{:S(2)}, u32[]{:S(2)}) collective-permute-start(bf16[512,512]{1,0:T(8,128)(2,1)S(1)} %add_convert_fusion.1), channel_id=1, source_target_pairs={{8,16},{9,17},{10,18},{11,19},{12,20},{13,21},{14,22},{15,23},{16,... | collective-permute-start | bytes 1572872 | tf_op jit(solution)/shard_map/ppermute | solution.py:229
  79.0 17.6 %collective-permute-start.14 = (bf16[512,512]{1,0:T(8,128)(2,1)S(1)}, bf16[512,512]{1,0:T(8,128)(2,1)S(1)}, u32[]{:S(2)}, u32[]{:S(2)}) collective-permute-start(bf16[512,512]{1,0:T(8,128)(2,1)S(1)} %fusion.17), channel_id=1, source_target_pairs={{0,2},{1,3},{2,0},{3,1},{4,6},{5,7},{6,4},{7,5},{8,10},{9,11},{10,... | collective-permute-start | bytes 1572872 | tf_op jit(solution)/shard_map/ppermute | solution.py:208
  79.6 9.1 %collective-permute-start.19 = (bf16[512,256]{1,0:T(8,128)(2,1)S(1)}, bf16[512,256]{1,0:T(8,128)(2,1)S(1)}, u32[]{:S(2)}, u32[]{:S(2)}) collective-permute-start(bf16[512,256]{1,0:T(8,128)(2,1)S(1)} %get-tuple-element.60), channel_id=1, source_target_pairs={{0,4},{4,0},{8,12},{12,8},{16,20},{20,16},{24,28},{28,24},{1,5},{5... | collective-permute-start | bytes 786440 | tf_op jit(solution)/shard_map/ppermute | solution.py:198
  80.4 18.9 %collective-permute-start.16 = (bf16[512,512]{1,0:T(8,128)(2,1)S(1)}, bf16[512,512]{1,0:T(8,128)(2,1)S(1)}, u32[]{:S(2)}, u32[]{:S(2)}) collective-permute-start(bf16[512,512]{1,0:T(8,128)(2,1)S(1)} %fusion.14), channel_id=1, source_target_pairs={{0,4},{4,0},{8,12},{12,8},{16,20},{20,16},{24,28},{28,24},{1,5},{5... | collective-permute-start | bytes 1572872 | tf_op jit(solution)/shard_map/ppermute | solution.py:198
  88.9 6.9 %collective-permute-start.20 = (bf16[512,256]{1,0:T(8,128)(2,1)S(1)}, bf16[512,256]{1,0:T(8,128)(2,1)S(1)}, u32[]{:S(2)}, u32[]{:S(2)}) collective-permute-start(bf16[512,256]{1,0:T(8,128)(2,1)S(1)} %add_convert_fusion.7), channel_id=1, source_target_pairs={{0,24},{4,28},{8,0},{12,4},{16,8},{20,12},{24,16},{28,20},{1,25},{... | collective-permute-start | bytes 786440 | tf_op jit(solution)/shard_map/ppermute | solution.py:203
